TPU v7x, 32 devices: a whole 2x2x4 slice. The times are simulated.
32 devices in a mesh: dp: 8 (over z, core), tensor: 4 (over y, x).
Axes of the slice: x: 2, y: 2, z: 4, core: 2. Of those that a mesh axis runs over, the one named last changes fastest.
Arguments:
- tokens: bfloat16 [8192, 1536], P(('dp', 'tensor')), may hold values from -6 to 6
- cotangent: bfloat16 [8192, 1536], P(('dp', 'tensor')), may hold values from -6 to 6
- lengths: int32 [8, 4], P('dp'), may hold values from 1 to 512, 1024 in all within a row
- routes: int32 [8192, 8], P('dp'), may hold values from 0 to 39, all different within a row; in each aligned block of 256 rows (0 to 255, 256 to 511, ...) at most 81 rows name the same one
- norm_gains: float32 [2, 1536], replicated, may hold values from 0.5 to 1.5
- router_weight: bfloat16 [1536, 40], replicated, may hold values from -0.078125 to 0.078125
- qkv_weight: bfloat16 [8, 1536, 320], P('tensor', 'dp'), may hold values from -0.15625 to 0.15625
- out_weight: bfloat16 [8, 192, 1536], P('tensor', None, 'dp'), may hold values from -0.4375 to 0.4375
- expert_in: bfloat16 [40, 1536, 1024], P('tensor', 'dp'), may hold values from -0.15625 to 0.15625
- expert_out: bfloat16 [40, 512, 1536], P('tensor', None, 'dp'), may hold values from -1 to 1
Outputs:
- layer_output: bfloat16 [8192, 1536], P(('dp', 'tensor'))
- input_grad: float32 [8192, 1536], P(('dp', 'tensor'))
- norm_gains_grad: float32 [2, 1536], replicated
- router_grad: float32 [1536, 40], replicated
- qkv_grad: float32 [8, 1536, 320], P('tensor', 'dp')
- out_weight_grad: float32 [8, 192, 1536], P('tensor', None, 'dp')
- expert_in_grad: float32 [40, 1536, 1024], P('tensor', 'dp')
- expert_out_grad: float32 [40, 512, 1536], P('tensor', None, 'dp')
Inputs may be any that keep to these rules, and one draw needn't show every extreme that they name: `lengths`: each row lists one group's sequences in order; they sum to 1024, and the longest of each row is exactly 512. `routes`: each row names 8 different experts. In every aligned block of 256 rows no expert is named by more than 81 rows, and in some block one expert is named by exactly 81.
All inputs are finite; a program needn't handle non-finite values.
Results may differ from a plain program's by a relative error of at most 0.02.
Values may be sent and summed in bfloat16 or wider, within the bound.
No kernel may reach another device: no remote copies, remote signals or barrier semaphores. Data moves between devices by JAX's collectives and lax.ppermute only.
A program may use at most 448 MiB of HBM per device.

v0:
```python
import jax
import jax.numpy as jnp
from jax import lax
from jax.sharding import PartitionSpec as P

HD = 64
GRP = 3
F = 512
E = 40
ATT_BLOCK = 512
MOST = 81


EPS = 1e-05
THETA = 10000.0
NEG = -1e30
HIGHEST = lax.Precision.HIGHEST


def rms_norm(values, gain_row):
    return values * lax.rsqrt(jnp.mean(values * values, axis=-1, keepdims=True) + EPS) * gain_row


def rope_tables(position):
    halfway = HD // 2
    frequency = THETA ** (-(jnp.arange(halfway, dtype=jnp.float32) * 2.0 / HD))
    angles = position[:, None] * frequency[None, :]
    return (jnp.cos(angles), jnp.sin(angles))


def rotate(values, cosine, sine_part):
    halfway = values.shape[-1] // 2
    leading = values[..., :halfway]
    trailing = values[..., halfway:]
    return jnp.concatenate(
        [leading * cosine - trailing * sine_part, trailing * cosine + leading * sine_part], axis=-1
    )


def segment_info(lengths_row, row_total):
    index_all = jnp.arange(row_total, dtype=jnp.int32)
    ends_at = jnp.cumsum(lengths_row)
    segment = jnp.sum((index_all[:, None] >= ends_at[None, :]).astype(jnp.int32), axis=1)
    starts_at = ends_at - lengths_row
    numbers = jnp.arange(lengths_row.shape[0], dtype=jnp.int32)
    begins = jnp.sum(jnp.where(segment[:, None] == numbers[None, :], starts_at[None, :], 0), axis=1)
    return (index_all, segment, (index_all - begins).astype(jnp.float32))


def activate(gate_up):
    return jax.nn.silu(gate_up[..., :F]) * gate_up[..., F:]


def dispatch_table(member):
    places = jnp.cumsum(member, axis=-2) - 1
    slot_ids = jnp.arange(MOST, dtype=jnp.int32)
    member_t = jnp.swapaxes(member, -1, -2)[..., None, :]
    places_t = jnp.swapaxes(places, -1, -2)[..., None, :]
    picked = (member_t == 1) & (places_t == slot_ids[:, None])
    return picked.astype(jnp.bfloat16)


def shards(
    tokens,
    cotangent,
    lengths,
    routes,
    norm_gains,
    router_weight,
    qkv_weight,
    out_weight,
    expert_in,
    expert_out,
):
    own_rows, model_width = tokens.shape
    group_rows = routes.shape[0]
    tensor_rank = lax.axis_index("tensor")
    kv_local = qkv_weight.shape[0]
    local_experts = expert_in.shape[0]
    block_total = group_rows // own_rows
    att_blocks = group_rows // ATT_BLOCK
    scale_factor = HD ** (-0.5)
    inputs = tokens.astype(jnp.float32)
    row_begin = tensor_rank * own_rows
    index_all, segment, position = segment_info(lengths[0], group_rows)
    cosine, sine_part = rope_tables(position)
    normed_first = rms_norm(inputs, norm_gains[0]).astype(jnp.bfloat16)
    qkv_full, out_full = (
        lax.all_gather(qkv_weight, "dp", axis=1, tiled=True),
        lax.all_gather(out_weight, "dp", axis=2, tiled=True),
    )
    qkv_flat = jnp.transpose(qkv_full, (1, 0, 2)).reshape(model_width, -1)
    out_flat = out_full.reshape(-1, model_width)
    normed_group = lax.all_gather(normed_first, "tensor", axis=0, tiled=True)
    projected = jnp.dot(normed_group, qkv_flat, preferred_element_type=jnp.float32).reshape(
        group_rows, kv_local, GRP + 2, HD
    )
    queries = rotate(
        projected[:, :, :GRP], cosine[:, None, None, :], sine_part[:, None, None, :]
    ).astype(jnp.bfloat16)
    key_rows = rotate(projected[:, :, GRP], cosine[:, None, :], sine_part[:, None, :]).astype(
        jnp.bfloat16
    )
    value_rows = projected[:, :, GRP + 1].astype(jnp.bfloat16)

    def windows(source, filler):
        blocked = source.reshape((att_blocks, ATT_BLOCK) + source.shape[1:])
        earlier = jnp.concatenate(
            [jnp.full((1,) + blocked.shape[1:], filler, blocked.dtype), blocked[:-1]], axis=0
        )
        return jnp.concatenate([earlier, blocked], axis=1)

    key_window = windows(key_rows, 0)
    value_window = windows(value_rows, 0)
    segment_window = windows(segment, -1)
    index_window = windows(index_all, -1)
    query_blocks = queries.reshape(att_blocks, ATT_BLOCK, kv_local, GRP, HD)
    segment_blocks = segment.reshape(att_blocks, ATT_BLOCK)
    index_blocks = index_all.reshape(att_blocks, ATT_BLOCK)

    def block_scores(query_block, key_block, seg_query, seg_key, idx_query, idx_key):
        scores = (
            jnp.einsum("qhgc,khc->hgqk", query_block, key_block, preferred_element_type=jnp.float32)
            * scale_factor
        )
        allowed = (seg_query[:, None] == seg_key[None, :]) & (
            idx_key[None, :] <= idx_query[:, None]
        )
        return jnp.where(allowed, scores, NEG)

    def attend(packed):
        query_block, key_block, value_block, seg_query, seg_key, idx_query, idx_key = packed
        masked = block_scores(query_block, key_block, seg_query, seg_key, idx_query, idx_key)
        top_score = jnp.max(masked, axis=-1, keepdims=True)
        shifted = jnp.exp(masked - top_score)
        totals = jnp.sum(shifted, axis=-1, keepdims=True)
        probability = (shifted / totals).astype(jnp.bfloat16)
        attended_block = jnp.einsum(
            "hgqk,khc->qhgc", probability, value_block, preferred_element_type=jnp.float32
        ).astype(jnp.bfloat16)
        return (attended_block, top_score[..., 0] + jnp.log(totals[..., 0]))

    attended, log_totals = lax.map(
        attend,
        (
            query_blocks,
            key_window,
            value_window,
            segment_blocks,
            segment_window,
            index_blocks,
            index_window,
        ),
    )
    attended = attended.reshape(group_rows, -1)
    attended_part = attended
    residual = inputs + lax.psum_scatter(
        jnp.dot(attended_part, out_flat, preferred_element_type=jnp.float32),
        "tensor",
        scatter_dimension=0,
        tiled=True,
    )
    normed_second = rms_norm(residual, norm_gains[1]).astype(jnp.bfloat16)
    second_group = lax.all_gather(normed_second, "tensor", axis=0, tiled=True)
    in_full, out_experts = (
        lax.all_gather(expert_in, "dp", axis=1, tiled=True),
        lax.all_gather(expert_out, "dp", axis=2, tiled=True),
    )
    logits = jnp.dot(second_group, router_weight, preferred_element_type=jnp.float32)
    chosen = jnp.take_along_axis(logits, routes, axis=1)
    gate_probs = jax.nn.softmax(chosen, axis=-1)
    expert_ids = jnp.arange(E, dtype=jnp.int32)
    local_ids = tensor_rank * local_experts + jnp.arange(local_experts, dtype=jnp.int32)
    local_hits = (routes[:, :, None] == local_ids[None, None, :]).astype(jnp.float32)
    gate_local = jnp.sum(gate_probs[:, :, None] * local_hits, axis=1)
    member_local = jnp.sum(local_hits.astype(jnp.int32), axis=1)
    tables = dispatch_table(member_local.reshape(block_total, own_rows, local_experts))
    second_blocks = second_group.reshape(block_total, own_rows, model_width)
    gate_blocks = gate_local.reshape(block_total, own_rows, local_experts)

    def expert_forward(dispatch, block_rows, gate_block):
        taken = jnp.einsum(
            "est,td->esd", dispatch, block_rows, preferred_element_type=jnp.float32
        ).astype(jnp.bfloat16)
        slot_gate = jnp.einsum(
            "est,te->es", dispatch.astype(jnp.float32), gate_block, precision=HIGHEST
        )
        gate_up = jnp.einsum("esd,edf->esf", taken, in_full, preferred_element_type=jnp.float32)
        hidden = activate(gate_up).astype(jnp.bfloat16)
        produced = jnp.einsum(
            "esf,efd->esd", hidden, out_experts, preferred_element_type=jnp.float32
        )
        return (taken, slot_gate, gate_up, produced)

    def forward_block(packed):
        taken, slot_gate, gate_up, produced = expert_forward(packed[0], packed[1], packed[2])
        return (gate_up, produced, (slot_gate[..., None] * produced).astype(jnp.bfloat16))

    kept_gate_up, kept_produced, scaled = lax.map(
        forward_block, (tables, second_blocks, gate_blocks)
    )
    own_routes = lax.dynamic_slice_in_dim(routes, row_begin, own_rows, 0)
    own_hits = (own_routes[:, :, None] == expert_ids[None, None, :]).astype(jnp.float32)
    summed = jnp.einsum("best,besd->btd", tables, scaled, preferred_element_type=jnp.float32)
    expert_mix = lax.psum_scatter(
        summed.reshape(own_rows * lax.axis_size("tensor"), model_width).astype(jnp.bfloat16),
        "tensor",
        scatter_dimension=0,
        tiled=True,
    ).astype(jnp.float32)
    layer_output = (residual + expert_mix).astype(jnp.bfloat16)
    grad_group = lax.all_gather(cotangent, "tensor", axis=0, tiled=True)
    grad_blocks = grad_group.reshape(block_total, own_rows, model_width)

    def backward_block(carried, packed):
        in_acc, out_acc = carried
        dispatch, block_rows, gate_block, grad_block = packed
        taken, slot_gate, gate_up, produced = expert_forward(dispatch, block_rows, gate_block)
        slot_grad = jnp.einsum(
            "est,td->esd", dispatch, grad_block, preferred_element_type=jnp.float32
        )
        slot_gate_grad = jnp.sum(slot_grad * produced, axis=-1)
        produced_grad = (slot_gate[..., None] * slot_grad).astype(jnp.bfloat16)
        hidden, hidden_pull = jax.vjp(activate, gate_up)
        out_acc = out_acc + jnp.einsum(
            "esf,esd->efd",
            hidden.astype(jnp.bfloat16),
            produced_grad,
            preferred_element_type=jnp.float32,
        )
        hidden_grad = jnp.einsum(
            "esd,efd->esf", produced_grad, out_experts, preferred_element_type=jnp.float32
        )
        gate_up_grad = hidden_pull(hidden_grad)[0].astype(jnp.bfloat16)
        in_acc = in_acc + jnp.einsum(
            "esd,esf->edf", taken, gate_up_grad, preferred_element_type=jnp.float32
        )
        taken_grad = jnp.einsum(
            "esf,edf->esd", gate_up_grad, in_full, preferred_element_type=jnp.float32
        ).astype(jnp.bfloat16)
        rows_grad = jnp.einsum(
            "est,esd->td", dispatch, taken_grad, preferred_element_type=jnp.float32
        )
        gate_grad = jnp.einsum(
            "est,es->te", dispatch.astype(jnp.float32), slot_gate_grad, precision=HIGHEST
        )
        return ((in_acc, out_acc), (rows_grad, gate_grad))

    stacked = (tables, second_blocks, gate_blocks, grad_blocks)
    initial = (jnp.zeros(in_full.shape, jnp.float32), jnp.zeros(out_experts.shape, jnp.float32))
    (in_acc, out_acc), (rows_grads, gate_grads) = lax.scan(backward_block, initial, stacked)
    gate_grads = gate_grads.reshape(group_rows, local_experts)
    route_grad = jnp.sum(gate_grads[:, None, :] * local_hits, axis=2)
    second_grad, route_grad_own = (
        lax.psum_scatter(
            rows_grads.reshape(group_rows, model_width), "tensor", scatter_dimension=0, tiled=True
        ),
        lax.psum_scatter(route_grad, "tensor", scatter_dimension=0, tiled=True),
    )
    gates_own = lax.dynamic_slice_in_dim(gate_probs, row_begin, own_rows, 0)
    chosen_grad = gates_own * (
        route_grad_own - jnp.sum(gates_own * route_grad_own, axis=-1, keepdims=True)
    )
    logits_grad = jnp.sum(chosen_grad[:, :, None] * own_hits, axis=1)
    second_grad = second_grad + jnp.dot(
        logits_grad, router_weight.astype(jnp.float32).T, precision=HIGHEST
    )
    router_part = jnp.dot(normed_second.astype(jnp.float32).T, logits_grad, precision=HIGHEST)
    normed_again, second_pull = jax.vjp(rms_norm, residual, norm_gains[1])
    residual_back, second_gain_grad = second_pull(second_grad)
    residual_grad = cotangent.astype(jnp.float32) + residual_back
    shard_piece = lax.all_gather(residual_grad.astype(jnp.bfloat16), "tensor", axis=0, tiled=True)
    attended_part = attended
    weight_acc = jnp.einsum(
        "tc,td->cd", attended_part, shard_piece, preferred_element_type=jnp.float32
    )
    part_grad = jnp.einsum(
        "td,cd->tc", shard_piece, out_flat, preferred_element_type=jnp.float32
    ).astype(jnp.bfloat16)
    attended_grad_blocks = part_grad.reshape(att_blocks, ATT_BLOCK, kv_local, GRP, HD)

    def attend_back(packed):
        (
            query_block,
            key_block,
            value_block,
            seg_query,
            seg_key,
            idx_query,
            idx_key,
            log_block,
            grad_block,
        ) = packed
        masked = block_scores(query_block, key_block, seg_query, seg_key, idx_query, idx_key)
        probability = jnp.exp(masked - log_block[..., None])
        prob_grad = jnp.einsum(
            "qhgc,khc->hgqk", grad_block, value_block, preferred_element_type=jnp.float32
        )
        row_inner = jnp.sum(probability * prob_grad, axis=-1, keepdims=True)
        score_grad = (probability * (prob_grad - row_inner)).astype(jnp.bfloat16)
        query_grad = (
            jnp.einsum("hgqk,khc->qhgc", score_grad, key_block, preferred_element_type=jnp.float32)
            * scale_factor
        )
        key_grad = (
            jnp.einsum(
                "hgqk,qhgc->khc", score_grad, query_block, preferred_element_type=jnp.float32
            )
            * scale_factor
        )
        value_grad = jnp.einsum(
            "hgqk,qhgc->khc",
            probability.astype(jnp.bfloat16),
            grad_block,
            preferred_element_type=jnp.float32,
        )
        return (query_grad, key_grad, value_grad)

    query_grads, key_grads, value_grads = lax.map(
        attend_back,
        (
            query_blocks,
            key_window,
            value_window,
            segment_blocks,
            segment_window,
            index_blocks,
            index_window,
            log_totals,
            attended_grad_blocks,
        ),
    )

    def fold_window(window):
        current = window[:, ATT_BLOCK:]
        earlier = window[:, :ATT_BLOCK]
        carried_back = jnp.concatenate([earlier[1:], jnp.zeros_like(earlier[:1])], axis=0)
        return (current + carried_back).reshape((group_rows,) + window.shape[2:])

    key_grad_rows = fold_window(key_grads)
    value_grad_rows = fold_window(value_grads)
    query_grad_rows = query_grads.reshape(group_rows, kv_local, GRP, HD)
    query_pre = rotate(query_grad_rows, cosine[:, None, None, :], -sine_part[:, None, None, :])
    key_pre = rotate(key_grad_rows, cosine[:, None, :], -sine_part[:, None, :])
    projected_grad = jnp.concatenate(
        [query_pre, key_pre[:, :, None], value_grad_rows[:, :, None]], axis=2
    )
    projected_grad = projected_grad.astype(jnp.bfloat16).reshape(group_rows, -1)
    qkv_grad_flat = jnp.einsum(
        "td,tc->dc", normed_group, projected_grad, preferred_element_type=jnp.float32
    )
    first_grad = lax.psum_scatter(
        jnp.einsum(
            "tc,dc->td", projected_grad, qkv_flat, preferred_element_type=jnp.float32
        ).astype(jnp.bfloat16),
        "tensor",
        scatter_dimension=0,
        tiled=True,
    ).astype(jnp.float32)
    normed_once, first_pull = jax.vjp(rms_norm, inputs, norm_gains[0])
    input_back, first_gain_grad = first_pull(first_grad)
    input_grad = residual_grad + input_back
    qkv_grad_full = jnp.transpose(qkv_grad_flat.reshape(model_width, kv_local, -1), (1, 0, 2))
    out_grad_full = weight_acc.reshape(out_full.shape)
    qkv_grad, out_weight_grad = (
        lax.psum_scatter(
            qkv_grad_full.astype(jnp.bfloat16), "dp", scatter_dimension=1, tiled=True
        ).astype(jnp.float32),
        lax.psum_scatter(
            out_grad_full.astype(jnp.bfloat16), "dp", scatter_dimension=2, tiled=True
        ).astype(jnp.float32),
    )
    expert_in_grad, expert_out_grad = (
        lax.psum_scatter(in_acc.astype(jnp.bfloat16), "dp", scatter_dimension=1, tiled=True).astype(
            jnp.float32
        ),
        lax.psum_scatter(
            out_acc.astype(jnp.bfloat16), "dp", scatter_dimension=2, tiled=True
        ).astype(jnp.float32),
    )
    gain_grads = jnp.stack([first_gain_grad, second_gain_grad])
    norm_gains_grad, router_grad = lax.psum((gain_grads, router_part), ("dp", "tensor"))
    return (
        layer_output,
        input_grad,
        norm_gains_grad,
        router_grad,
        qkv_grad,
        out_weight_grad,
        expert_in_grad,
        expert_out_grad,
    )


def solution(mesh):
    return jax.shard_map(
        shards,
        mesh=mesh,
        in_specs=(
            P(("dp", "tensor"), None),
            P(("dp", "tensor"), None),
            P("dp", None),
            P("dp", None),
            P(),
            P(),
            P("tensor", "dp", None),
            P("tensor", None, "dp"),
            P("tensor", "dp", None),
            P("tensor", None, "dp"),
        ),
        out_specs=(
            P(("dp", "tensor"), None),
            P(("dp", "tensor"), None),
            P(),
            P(),
            P("tensor", "dp", None),
            P("tensor", None, "dp"),
            P("tensor", "dp", None),
            P("tensor", None, "dp"),
        ),
        check_vma=False,
    )
```

profile of v0, /device:TPU:0, one launch (start us, length us, event | category | flops | bytes accessed | tf_op | source)
XLA Modules:
  0.0 2297.5 jit_solution(13067529154020996226)
XLA Ops:
  20.9 17.1 all-gather.13.cloned.1.call-done
  41.6 29.8 %all-gather.11.cloned.1.call-done = bf16[2,1536,320]{2,0,1:T(2,128)(2,1)} async-done(((bf16[2,192,320]{2,0,1:T(2,128)(2,1)}), bf16[2,1536,320]{2,0,1:T(2,128)(2,1)}) %all-gather.11.cloned.1.call-update) | async-done | bytes 1966096 | tf_op jit(solution)/shard_map/all_gather | solution.py:89
  77.3 39.7 %all-gather.9.cloned.1.call-done = bf16[1024,1536]{1,0:T(8,128)(2,1)} async-done(((bf16[256,1536]{1,0:T(8,128)(2,1)}), bf16[1024,1536]{1,0:T(8,128)(2,1)}) %all-gather.9.cloned.1.call-update) | async-done | bytes 3145744 | tf_op jit(solution)/shard_map/all_gather | solution.py:94
  125.6 30.8 %while.53 = (s32[]{:T(128)}, bf16[2,512,2,3,64]{1,4,3,2,0:T(8,128)(2,1)}, f32[2,2,3,512]{3,2,1,0:T(4,128)}, bf16[2,1024,2,64]{1,3,2,0:T(8,128)(2,1)S(1)}, s32[2,...) while((s32[]{:T(128)}, ...), condition=%wide.region_7.8_spmd, body=%wide.region_4.7_spmd.sunk | while | flops 844821504 | bytes 41314932 | solution.py:143
  164.6 70.3 %reduce-scatter.11.cloned.1.call-done = f32[256,1536]{1,0:T(8,128)} async-done(((f32[1024,1536]{1,0:T(8,128)}), f32[256,1536]{1,0:T(8,128)}) %reduce-scatter.11.cloned.1.call-update) | async-done | bytes 1572880 | tf_op jit(solution)/shard_map/reduce_scatter | solution.py:157
  247.0 36.0 %all-gather.15.cloned.1.call-done = bf16[1024,1536]{1,0:T(8,128)(2,1)} async-done(((bf16[256,1536]{1,0:T(8,128)(2,1)}), bf16[1024,1536]{1,0:T(8,128)(2,1)}) %all-gather.15.cloned.1.call-update) | async-done | bytes 3145744 | tf_op jit(solution)/shard_map/all_gather | solution.py:164
  286.0 65.5 %gather_fusion = f32[8192]{0:T(1024)S(1)} fusion(f32[1024,40]{0,1:T(8,128)S(1)} %fusion.159, s32[8192]{0:T(1024)S(1)} %reshape.424), kind=kCustom, calls=%fused_computation | custom fusion | bytes 131072 | tf_op jit(solution)/shard_map/jit(take_along_axis)/gather | solution.py:170
  352.3 74.7 %all-gather.19.cloned.1.call-done = bf16[10,512,1536]{1,2,0:T(8,128)(2,1)} async-done(((bf16[10,512,192]{1,2,0:T(8,128)(2,1)}), bf16[10,512,1536]{1,2,0:T(8,128)(2,1)}) %all-gather.19.cloned.1.call-update) | async-done | bytes 15728656 | tf_op jit(solution)/shard_map/all_gather | solution.py:167
  427.0 19.8 copy.218
  446.8 24.3 %all-gather.21.cloned.1.call-done = bf16[1024,1536]{1,0:T(8,128)(2,1)} async-done(((bf16[256,1536]{1,0:T(8,128)(2,1)}), bf16[1024,1536]{1,0:T(8,128)(2,1)}) %all-gather.21.cloned.1.call-update) | async-done | bytes 3145744 | tf_op jit(solution)/shard_map/all_gather | solution.py:212
  471.1 273.1 %all-gather.17.cloned.1.call-done = bf16[10,1536,1024]{2,1,0:T(8,128)(2,1)} async-done(((bf16[10,192,1024]{2,1,0:T(8,128)(2,1)}), bf16[10,1536,1024]{2,1,0:T(8,128)(2,1)}) %all-gather.17.cloned.1.call-update) | async-done | bytes 31457296 | tf_op jit(solution)/shard_map/all_gather | solution.py:166
  744.2 478.3 %while.56 = (s32[]{:T(128)}, f32[10,1536,1024]{2,1,0:T(8,128)}, f32[10,512,1536]{2,1,0:T(8,128)}, f32[4,256,1536]{2,1,0:T(8,128)}, f32[4,256,10]{1,0,2:T(4,128)S...) while((s32[]{:T(128)}, f32[10,1536,1024]{2,1,0:T(8,128)}, ...), condition=%wide.region_21.22_spmd.clone, body=%wide.region_19.21_spmd.clone.sunk | while | flops 13448446976 | bytes 348506464 | solution.py:251
  779.3 23.4 %select_add_fusion.6 = f32[10,1536,1024]{2,1,0:T(8,128)} fusion(f32[10,1536,1024]{2,1,0:T(8,128)} %get-tuple-element.921, bf16[10,81,1536]{2,1,0:T(8,128)(2,1)S(1)} %convolution_convert_fusion.7, pred[]{:T(512)S(6)} %compare.29, f32[10,81,512]{2,1,0:T(8,128)} %get-tuple-element.871, f32[10,81,512]{2,1,0:T(8,128)} %get-tuple-element.872), kind=kOutput, calls=%fused_computation.96.clone.2 | convolution fusion | flops 2581155840 | bytes 131635200 | tf_op jit(solution)/shard_map/while/body/eval_jaxpr/esd,esf->edf/dot_general | solution.py:235
  879.8 40.8 %select_add_fusion.6 = f32[10,1536,1024]{2,1,0:T(8,128)} fusion(f32[10,1536,1024]{2,1,0:T(8,128)} %get-tuple-element.921, bf16[10,81,1536]{2,1,0:T(8,128)(2,1)S(1)} %convolution_convert_fusion.7, pred[]{:T(512)S(6)} %compare.29, f32[10,81,512]{2,1,0:T(8,128)} %get-tuple-element.871, f32[10,81,512]{2,1,0:T(8,128)} %get-tuple-element.872), kind=kOutput, calls=%fused_computation.96.clone.2 | convolution fusion | flops 2581155840 | bytes 131635200 | tf_op jit(solution)/shard_map/while/body/eval_jaxpr/esd,esf->edf/dot_general | solution.py:235
  920.6 21.8 select_add_fusion.7
  942.5 17.1 fusion.290
  1005.6 40.8 %select_add_fusion.6 = f32[10,1536,1024]{2,1,0:T(8,128)} fusion(f32[10,1536,1024]{2,1,0:T(8,128)} %get-tuple-element.921, bf16[10,81,1536]{2,1,0:T(8,128)(2,1)S(1)} %convolution_convert_fusion.7, pred[]{:T(512)S(6)} %compare.29, f32[10,81,512]{2,1,0:T(8,128)} %get-tuple-element.871, f32[10,81,512]{2,1,0:T(8,128)} %get-tuple-element.872), kind=kOutput, calls=%fused_computation.96.clone.2 | convolution fusion | flops 2581155840 | bytes 131635200 | tf_op jit(solution)/shard_map/while/body/eval_jaxpr/esd,esf->edf/dot_general | solution.py:235
  1046.4 21.8 select_add_fusion.7
  1131.3 40.8 %select_add_fusion.6 = f32[10,1536,1024]{2,1,0:T(8,128)} fusion(f32[10,1536,1024]{2,1,0:T(8,128)} %get-tuple-element.921, bf16[10,81,1536]{2,1,0:T(8,128)(2,1)S(1)} %convolution_convert_fusion.7, pred[]{:T(512)S(6)} %compare.29, f32[10,81,512]{2,1,0:T(8,128)} %get-tuple-element.871, f32[10,81,512]{2,1,0:T(8,128)} %get-tuple-element.872), kind=kOutput, calls=%fused_computation.96.clone.2 | convolution fusion | flops 2581155840 | bytes 131635200 | tf_op jit(solution)/shard_map/while/body/eval_jaxpr/esd,esf->edf/dot_general | solution.py:235
  1172.1 21.9 select_add_fusion.7
  1194.0 17.1 fusion.290
  1224.0 21.2 reduce-scatter.17.cloned.1.call-done
  1246.7 72.5 %reduce-scatter.15.cloned.1.call-done = f32[256,1536]{1,0:T(8,128)} async-done(((f32[1024,1536]{1,0:T(8,128)}), f32[256,1536]{1,0:T(8,128)}) %reduce-scatter.15.cloned.1.call-update) | async-done | bytes 1572880 | tf_op jit(solution)/shard_map/reduce_scatter | solution.py:255
  1325.1 44.0 %all-gather.23.cloned.1.call-done = bf16[1024,1536]{1,0:T(8,128)(2,1)} async-done(((bf16[256,1536]{1,0:T(8,128)(2,1)}), bf16[1024,1536]{1,0:T(8,128)(2,1)}) %all-gather.23.cloned.1.call-update) | async-done | bytes 3145744 | tf_op jit(solution)/shard_map/all_gather | solution.py:272
  1376.2 102.0 %while.55 = (s32[]{:T(128)}, f32[2,512,2,3,64]{1,0,4,3,2:T(2,128)}, f32[2,1024,2,64]{1,3,2,0:T(8,128)}, f32[2,1024,2,64]{1,3,2,0:T(8,128)}, bf16[2,1024,2,64]{1,...) while((s32[]{:T(128)}, f32[2,512,2,3,64]{1,0,4,3,2:T(2,128)}, ...), condition=%wide.region_30.31_spmd, body=%wide.region_28.30_spmd.sunk | while | flops 2062349312 | bytes 179441904 | solution.py:319
  1512.4 112.2 %while.54 = (s32[]{:T(128)}, bf16[4,10,81,1536]{3,2,1,0:T(8,128)(2,1)}, bf16[4,10,81,256]{3,2,1,0:T(8,128)(2,1)S(1)}, f32[4,256,10]{1,2,0:T(8,128)}, bf16[4,256,...) while((s32[]{:T(128)}, ...), condition=%wide.region_17.18_spmd, body=%wide.region_16.17_spmd.sunk | while | flops 4467778560 | bytes 58550524 | solution.py:199
  1633.9 24.1 %copy.228 = bf16[10,512,1536]{1,2,0:T(8,128)(2,1)} copy(f32[10,512,1536]{2,1,0:T(8,128)} %get-tuple-element.236) | data formatting | bytes 47185920 | tf_op jit(solution)/shard_map/while | solution.py:251
  1658.0 32.4 %convert_element_type.180 = bf16[10,1536,1024]{2,1,0:T(8,128)(2,1)} convert(f32[10,1536,1024]{2,1,0:T(8,128)} %get-tuple-element.235) | non-fusion elementwise | flops 15728640 | bytes 94371840 | tf_op jit(solution)/shard_map/convert_element_type | solution.py:374
  1705.7 41.4 %psum.14 = f32[2,1536]{1,0:T(2,128)} all-reduce(f32[2,1536]{1,0:T(2,128)S(1)} %pad_maximum_fusion.1), channel_id=1, replica_groups=mesh['dp'=8,'tensor'=4] {'dp','tensor'}, use_global_device_ids=true, to_apply=%region_35.36 | all-reduce | flops 3072 | bytes 24576 | tf_op jit(solution)/shard_map/psum | solution.py:382
  1747.1 105.5 %reduce-scatter.23.cloned.1.call-done = bf16[10,512,192]{1,2,0:T(8,128)(2,1)} async-done(((bf16[10,512,1536]{1,2,0:T(8,128)(2,1)}), bf16[10,512,192]{1,2,0:T(8,128)(2,1)}) %reduce-scatter.23.cloned.1.call-update) | async-done | bytes 1966096 | tf_op jit(solution)/shard_map/reduce_scatter | solution.py:377
  1856.6 303.1 %reduce-scatter.21.cloned.1.call-done = bf16[10,192,1024]{2,1,0:T(8,128)(2,1)} async-done(((bf16[10,1536,1024]{2,1,0:T(8,128)(2,1)}), bf16[10,192,1024]{2,1,0:T(8,128)(2,1)}) %reduce-scatter.21.cloned.1.call-update) | async-done | bytes 3932176 | tf_op jit(solution)/shard_map/reduce_scatter | solution.py:374
  2166.0 122.6 %all-reduce.12.cloned.1.call-done = f32[1536,40]{0,1:T(8,128)} async-done(((f32[1536,40]{0,1:T(8,128)}), f32[1536,40]{0,1:T(8,128)}) %all-reduce.12.cloned.1.call-update) | async-done | bytes 245776 | tf_op jit(solution)/shard_map/psum | solution.py:382
  (439 shorter events, 617.0 us)
Async XLA Ops:
  7.2 275.9 %copy-start = (bf16[1536,40]{0,1:T(8,128)(2,1)S(1)}, bf16[1536,40]{0,1:T(8,128)(2,1)}, u32[]{:S(2)}) copy-start(bf16[1536,40]{0,1:T(8,128)(2,1)} %param.23) | copy-start | bytes 368644
  7.2 30.8 %all-gather.13.cloned.1.call-start = ((), (), s32[]{:S(2)}) async-start(), calls=%async_computation.10 | async-start | bytes 1769472 | tf_op jit(solution)/shard_map/all_gather | solution.py:90
  9.0 62.4 %all-gather.11.cloned.1.call-start = ((), (), s32[]{:S(2)}) async-start(), calls=%async_computation.9 | async-start | bytes 2654208 | tf_op jit(solution)/shard_map/all_gather | solution.py:89
  11.1 105.9 %all-gather.9.cloned.1.call-start = ((), (), s32[]{:S(2)}) async-start(), calls=%async_computation.8 | async-start | bytes 3932160 | tf_op jit(solution)/shard_map/all_gather | solution.py:94
  17.4 217.5 %reduce-scatter.11.cloned.1.call-start = ((), (), s32[]{:S(2)}) async-start(), calls=%async_computation.11 | async-start | bytes 7864320 | tf_op jit(solution)/shard_map/reduce_scatter | solution.py:157
  20.9 104.3 %copy-start.22 = (f32[1024,32]{0,1:T(8,128)}, f32[1024,32]{0,1:T(8,128)S(1)}, u32[]{:S(2)}) copy-start(f32[1024,32]{0,1:T(8,128)S(1)} %get-tuple-element.588) | copy-start | bytes 393220
  41.6 117.5 %copy-start.21 = (bf16[2,192,1536]{2,1,0:T(8,128)(2,1)}, bf16[2,192,1536]{2,1,0:T(8,128)(2,1)S(1)}, u32[]{:S(2)}) copy-start(bf16[2,192,1536]{2,1,0:T(8,128)(2,1)S(1)} %copy.208) | copy-start | bytes 3538948
  164.5 118.5 %all-gather.15.cloned.1.call-start = ((), (), s32[]{:S(2)}) async-start(), calls=%async_computation.12 | async-start | bytes 3932160 | tf_op jit(solution)/shard_map/all_gather | solution.py:164
  238.9 188.1 %all-gather.19.cloned.1.call-start = ((), (), s32[]{:S(2)}) async-start(), calls=%async_computation.14 | async-start | bytes 17694720 | tf_op jit(solution)/shard_map/all_gather | solution.py:167
  239.5 231.6 %all-gather.21.cloned.1.call-start = ((), (), s32[]{:S(2)}) async-start(), calls=%async_computation.16 | async-start | bytes 3932160 | tf_op jit(solution)/shard_map/all_gather | solution.py:212
  240.2 503.9 %all-gather.17.cloned.1.call-start = ((), (), s32[]{:S(2)}) async-start(), calls=%async_computation.13 | async-start | bytes 35389440 | tf_op jit(solution)/shard_map/all_gather | solution.py:166
  241.0 1004.2 %reduce-scatter.17.cloned.1.call-start = ((), (), s32[]{:S(2)}) async-start(), calls=%async_computation.18 | async-start | bytes 40960 | tf_op jit(solution)/shard_map/reduce_scatter | solution.py:258
  352.1 94.7 %copy-start.42 = (f32[1024,8]{0,1:T(8,128)}, f32[1024,8]{0,1:T(8,128)S(1)}, u32[]{:S(2)}) copy-start(f32[1024,8]{0,1:T(8,128)S(1)} %fusion.148) | copy-start | bytes 98308
  352.3 391.8 %copy-start.51 = (f32[4,256,10]{1,0,2:T(4,128)S(1)}, f32[4,256,10]{1,0,2:T(4,128)}, u32[]{:S(2)}) copy-start(f32[4,256,10]{1,0,2:T(4,128)} %custom-call.12) | copy-start | bytes 122884
  744.2 478.3 %copy-start.30 = (s32[1024,8]{0,1:T(8,128)S(1)}, s32[1024,8]{0,1:T(8,128)}, u32[]{:S(2)}) copy-start(s32[1024,8]{0,1:T(8,128)} %param.21) | copy-start | bytes 98308
  744.2 478.3 %copy-start.66 = (s32[10]{0:T(128)S(1)}, s32[10]{0:T(128)}, u32[]{:S(2)}) copy-start(s32[10]{0:T(128)} %copy-done.64) | copy-start | bytes 124
  1223.3 95.9 %reduce-scatter.15.cloned.1.call-start = ((), (), s32[]{:S(2)}) async-start(), calls=%async_computation.17 | async-start | bytes 7864320 | tf_op jit(solution)/shard_map/reduce_scatter | solution.py:255
  1223.3 95.8 %copy-start.10 = (f32[256,1536]{1,0:T(8,128)S(1)}, f32[256,1536]{1,0:T(8,128)}, u32[]{:S(2)}) copy-start(f32[256,1536]{1,0:T(8,128)} %copy-done.9) | copy-start | bytes 4718596
  1223.3 95.8 %copy-start.45 = (f32[1536]{0:T(1024)S(1)}, f32[1536]{0:T(1024)}, u32[]{:S(2)}) copy-start(f32[1536]{0:T(1024)} %get-tuple-element.475) | copy-start | bytes 18436
  1223.3 95.8 %copy-start.54 = (f32[256]{0:T(256)S(1)}, f32[256]{0:T(256)}, u32[]{:S(2)}) copy-start(f32[256]{0:T(256)} %copy-done.53) | copy-start | bytes 3076
  1223.9 98.6 %copy-start.61 = (f32[256]{0:T(256)S(1)}, f32[256]{0:T(256)}, u32[]{:S(2)}) copy-start(f32[256]{0:T(256)} %copy-done.60) | copy-start | bytes 3076
  1223.9 99.7 %copy-start.18 = (bf16[256,1536]{1,0:T(8,128)(2,1)S(1)}, bf16[256,1536]{1,0:T(8,128)(2,1)}, u32[]{:S(2)}) copy-start(bf16[256,1536]{1,0:T(8,128)(2,1)} %param.19) | copy-start | bytes 2359300
  1223.9 145.2 %all-gather.23.cloned.1.call-start = ((), (), s32[]{:S(2)}) async-start(), calls=%async_computation.19 | async-start | bytes 3932160 | tf_op jit(solution)/shard_map/all_gather | solution.py:272
  1325.0 368.6 %all-reduce.14.cloned.1.call-start = ((), (), s32[]{:S(2)}) async-start(), calls=%async_computation.25 | async-start | bytes 4718592
  1495.4 200.3 %reduce-scatter.25.cloned.1.call-start = ((), (), s32[]{:S(2)}) async-start(), calls=%async_computation.24 | async-start | bytes 1327104
  1505.2 194.2 %reduce-scatter.19.cloned.1.call-start = ((), (), s32[]{:S(2)}) async-start(), calls=%async_computation.20 | async-start | bytes 3932160 | tf_op jit(solution)/shard_map/reduce_scatter | solution.py:352
  1510.9 190.5 %reduce-scatter.13.cloned.1.call-start = ((), (), s32[]{:S(2)}) async-start(), calls=%async_computation.15 | async-start | bytes 3932160 | tf_op jit(solution)/shard_map/reduce_scatter | solution.py:205
  1512.4 112.3 %copy-start.39 = (s32[4,10,256]{2,1,0:T(8,128)S(1)}, s32[4,10,256]{2,1,0:T(8,128)}, u32[]{:S(2)}) copy-start(s32[4,10,256]{2,1,0:T(8,128)} %copy-done.38) | copy-start | bytes 122884
  1512.4 112.3 %copy-start.50 = (pred[4,10,256]{2,1,0:T(8,128)(4,1)S(1)}, pred[4,10,256]{2,1,0:T(8,128)(4,1)}, u32[]{:S(2)}) copy-start(pred[4,10,256]{2,1,0:T(8,128)(4,1)} %copy-done.49) | copy-start | bytes 30724
  1633.8 218.8 %reduce-scatter.23.cloned.1.call-start = ((), (), s32[]{:S(2)}) async-start(), calls=%async_computation.23 | async-start | bytes 17694720 | tf_op jit(solution)/shard_map/reduce_scatter | solution.py:377
  1658.0 501.7 %reduce-scatter.21.cloned.1.call-start = ((), (), s32[]{:S(2)}) async-start(), calls=%async_computation.22 | async-start | bytes 35389440 | tf_op jit(solution)/shard_map/reduce_scatter | solution.py:374
  1690.5 598.1 %all-reduce.12.cloned.1.call-start = ((), (), s32[]{:S(2)}) async-start(), calls=%async_computation.21 | async-start | bytes 491520 | tf_op jit(solution)/shard_map/psum | solution.py:382
  (67 other events, 962.9 us)
Sparse Core Ops, SparseCore 0:
  10.2 27.7 all-gather.12
  40.2 31.1 all-gather.10
  73.8 43.0 all-gather.8
  164.6 70.2 reduce-scatter.10
  239.0 43.9 all-gather.14
  284.5 142.4 all-gather.18
  428.9 42.1 all-gather.20
  472.7 271.4 all-gather.16
  1223.4 21.7 reduce-scatter.16
  1248.9 70.2 reduce-scatter.14
  1325.1 43.9 all-gather.22
  1495.5 66.8 all-reduce.13
  1564.8 31.8 reduce-scatter.24
  1600.4 42.2 reduce-scatter.18
  1646.4 43.9 reduce-scatter.12
  1692.6 159.9 reduce-scatter.22
  1854.9 304.7 reduce-scatter.20
  2166.6 122.0 all-reduce.11
where the time goes:
time: 2310 us; the launch traced here: 2300 us
  waiting for transfers between devices  1240 us (54%)
  matrix products  690 us (30%)
  local copies, waits for them, and re-layouts  209 us (9%)
  other arithmetic  102 us (4%)
  blocking collectives  41.4 us (2%)
    reduce_scatter x1, waiting for transfers between devices, shards(): lax.psum_scatter(in_acc.astype(jnp.bfloat16), 'dp', scatter_dimension=1,...  303 us
    all_gather x1, waiting for transfers between devices, shards(): lax.all_gather(expert_in, 'dp', axis=1, tiled=True)  273 us
    dot_general x4, matrix products, backward_block(): jnp.einsum('esd,esf->edf', taken, gate_up_grad, preferred_element_type=jn...  146 us
    psum x1, waiting for transfers between devices, shards(): lax.psum((gain_grads, router_part), ('dp', 'tensor'))  123 us
    dot_general x8, matrix products, expert_forward(): jnp.einsum('esd,edf->esf', taken, in_full, preferred_element_type=jnp.flo...  121 us
    reduce_scatter x1, waiting for transfers between devices, shards(): lax.psum_scatter(out_acc.astype(jnp.bfloat16), 'dp', scatter_dimension=2,...  106 us
    dot_general x8, matrix products, expert_forward(): jnp.einsum('esf,efd->esd', hidden, out_experts, preferred_element_type=jn...  83.7 us
    dot_general x4, matrix products, backward_block(): jnp.einsum('esf,esd->efd', hidden.astype(jnp.bfloat16), produced_grad, pr...  79.7 us
  transfers between devices with their start and end apart: 18, of which 14 were waited for; matrix products, arithmetic and copies ran while one was open for 14% of the time, Pallas kernels for 0%

commit v1 on v0

v1 whole, which is shorter than its diff:
```python
import functools

import jax
import jax.numpy as jnp
from jax import lax
from jax.experimental import pallas as pl
from jax.experimental.pallas import tpu as pltpu
from jax.sharding import PartitionSpec as P

HD = 64
GRP = 3
F = 512
QF = F // 4
E = 40
BLK = 256
SLOT = 88
WIN_BLOCKS = 512 // BLK
EPS = 1e-05
THETA = 10000.0
NEG = -1e30
SCALE = HD ** (-0.5)
WCOLS = 2 * F + 2 * QF + F + QF
VMEM = 60 * 1024 * 1024
BF = jnp.bfloat16
F32 = jnp.float32


def dot_nn(a, b):
    return lax.dot_general(a, b, (((1,), (0,)), ((), ())), preferred_element_type=F32)


def dot_nt(a, b):
    return lax.dot_general(a, b, (((1,), (1,)), ((), ())), preferred_element_type=F32)


def dot_tn(a, b):
    return lax.dot_general(a, b, (((0,), (0,)), ((), ())), preferred_element_type=F32)


def params(**kw):
    return pltpu.CompilerParams(vmem_limit_bytes=VMEM, **kw)


def whole(shape):
    return pl.BlockSpec(shape, lambda *a: (0,) * len(shape), pipeline_mode=pl.Buffered(1))


class Links:
    def __init__(self, group):
        self.n_dp = lax.axis_size("dp")
        self.n_t = lax.axis_size("tensor")
        self.group = group
        self.fast = self.n_dp == 8 and self.n_t == 4 and group == 8
        self.dp = lax.axis_index("dp")
        self.t = lax.axis_index("tensor")
        if self.fast:
            devices = [(d, t) for d in range(8) for t in range(4)]
            number = lambda d, t: d * 4 + t
            ring = {0: 1, 1: 3, 3: 2, 2: 0}
            self.first = [(number(d, t), number(d, t ^ (2 if d & 1 else 1))) for d, t in devices]
            self.second = [(number(d, t), number(d, t ^ (1 if d & 1 else 2))) for d, t in devices]
            self.swap = [(number(d, t), number(d ^ 1, t)) for d, t in devices]
            self.along = [(number(d, t), number(ring[d >> 1] * 2 + (d & 1), t)) for d, t in devices]

    def send(self, value, perm):
        return lax.ppermute(value, ("dp", "tensor"), perm)

    def plane_order(self, core):
        one = jnp.where(core == 0, 1, 2)
        return [self.t, self.t ^ one, self.t ^ (3 - one), self.t ^ 3]

    def plane_places(self):
        if not self.fast:
            return jnp.arange(self.n_t, dtype=jnp.int32)
        one = jnp.where((self.dp & 1) == 0, 1, 2)
        diff = jnp.arange(4, dtype=jnp.int32) ^ self.t
        return jnp.where(diff == one, 1, jnp.where(diff == 3 - one, 2, diff)).astype(jnp.int32)

    def gather_plane(self, block):
        if not self.fast:
            return lax.all_gather(block, "tensor", axis=0)
        near = self.send(block, self.first)
        other = self.send(block, self.second)
        far = self.send(near, self.second)
        return jnp.stack([block, near, other, far])

    def scatter_plane(self, parts):
        if not self.fast:
            rows = parts.reshape((-1,) + parts.shape[2:])
            return lax.psum_scatter(rows, "tensor", scatter_dimension=0, tiled=True)
        a, b = self.scatter_plane_open(parts)
        return add(a, b)

    def scatter_plane_open(self, parts):
        got_far = self.send(parts[3], self.second)
        got = self.send(parts[2], self.second)
        got_near = self.send(add(parts[1], got_far), self.first)
        return add(parts[0], got), got_near

    def chunks(self):
        return self.group * self.n_t // 8

    def chunk_sources(self):
        if not self.fast:
            base = (self.dp // self.group) * self.group * self.n_t
            return [base + 8 * c + jnp.arange(8, dtype=jnp.int32) for c in range(self.chunks())]
        z, core = self.dp >> 1, self.dp & 1
        place = z ^ (z >> 1)
        out = []
        for c in range(4):
            back = (place + 4 - c) & 3
            source = back ^ (back >> 1)
            rows = [(source * 2 + core) * 4 + t for t in self.plane_order(core)]
            rows += [(source * 2 + 1 - core) * 4 + t for t in self.plane_order(1 - core)]
            out.append(jnp.stack(rows).astype(jnp.int32))
        return out

    def groups(self):
        n = self.n_dp // self.group
        return [list(range(g * self.group, (g + 1) * self.group)) for g in range(n)]

    def gather_all(self, block):
        if not self.fast:
            plane = lax.all_gather(block, "tensor", axis=0)
            rows = lax.all_gather(plane, "dp", axis=0, axis_index_groups=self.groups())
            rows = rows.reshape((-1,) + block.shape)
            return [(rows[8 * c : 8 * c + 4], rows[8 * c + 4 : 8 * c + 8]) for c in range(self.chunks())]
        out = []
        for c in range(4):
            mine = self.gather_plane(block)
            out.append((mine, self.send(mine, self.swap)))
            if c < 3:
                block = self.send(block, self.along)
        return out

    def scatter_chunk(self, mine, theirs):
        return self.scatter_plane(add(mine, self.send(theirs, self.swap)))

    def scatter_all(self, pairs):
        if not self.fast:
            rows = jnp.concatenate([half for pair in pairs for half in pair])
            rows = rows.reshape((self.group, -1) + rows.shape[2:])
            total = lax.psum_scatter(rows, "dp", scatter_dimension=0, axis_index_groups=self.groups())
            total = lax.psum_scatter(total, "tensor", scatter_dimension=0, tiled=True)
            return total, jnp.zeros_like(total)
        sums = [self.scatter_chunk(*pair) for pair in pairs]
        moving = self.send(sums[1], self.along)
        moving = self.send(add(moving, sums[2]), self.along)
        moving = self.send(add(moving, sums[3]), self.along)
        return sums[0], moving


def add(a, b):
    return (a.astype(F32) + b.astype(F32)).astype(a.dtype)


def pack_kernel(full_ref, gate_ref, up_ref, out_ref, quarter_ref, packed_ref):
    packed_ref[0, :, : 2 * F] = full_ref[0]
    packed_ref[0, :, 2 * F : 2 * F + QF] = gate_ref[0]
    packed_ref[0, :, 2 * F + QF : 2 * F + 2 * QF] = up_ref[0]
    packed_ref[0, :, 2 * F + 2 * QF : 3 * F + 2 * QF] = out_ref[0].astype(F32).T.astype(BF)
    packed_ref[0, :, 3 * F + 2 * QF :] = quarter_ref[0].astype(F32).T.astype(BF)


def pack_experts(expert_in, expert_out, group, n_dp):
    depth = expert_in.shape[1]
    of = lambda d: d % group
    return pl.pallas_call(
        pack_kernel,
        grid=(n_dp,),
        in_specs=[
            pl.BlockSpec((1, depth, 2 * F), lambda d: (of(d), 0, 0)),
            pl.BlockSpec((1, depth, QF), lambda d: (group + of(d) // 4, 0, of(d) % 4)),
            pl.BlockSpec((1, depth, QF), lambda d: (group + of(d) // 4, 0, 4 + of(d) % 4)),
            pl.BlockSpec((1, F, depth), lambda d: (of(d), 0, 0)),
            pl.BlockSpec((1, QF, depth), lambda d: (group + of(d) // 4, of(d) % 4, 0)),
        ],
        out_specs=pl.BlockSpec((1, depth, WCOLS), lambda d: (d, 0, 0)),
        out_shape=jax.ShapeDtypeStruct((n_dp, depth, WCOLS), BF),
        compiler_params=params(),
        name="pack_experts",
    )(expert_in, expert_in, expert_in, expert_out, expert_out)


def unpack_kernel(group, packed_ref, in_ref, out_ref):
    e = pl.program_id(0)

    @pl.when(e < group)
    def _():
        in_ref[0] = packed_ref[e, :, : 2 * F].astype(F32)
        out_ref[0] = packed_ref[e, :, 2 * F + 2 * QF : 3 * F + 2 * QF].astype(F32).T

    @pl.when(e >= group)
    def _():
        for q in range(4):
            s = (e - group) * 4 + q
            in_ref[0, :, q * QF : (q + 1) * QF] = packed_ref[s, :, 2 * F : 2 * F + QF].astype(F32)
            in_ref[0, :, F + q * QF : F + (q + 1) * QF] = packed_ref[
                s, :, 2 * F + QF : 2 * F + 2 * QF
            ].astype(F32)
            out_ref[0, q * QF : (q + 1) * QF, :] = packed_ref[s, :, 3 * F + 2 * QF :].astype(F32).T


def unpack_experts(packed, experts, group):
    depth = packed.shape[1]
    return pl.pallas_call(
        functools.partial(unpack_kernel, group),
        grid=(experts,),
        in_specs=[whole(packed.shape)],
        out_specs=(
            pl.BlockSpec((1, depth, 2 * F), lambda e: (e, 0, 0)),
            pl.BlockSpec((1, F, depth), lambda e: (e, 0, 0)),
        ),
        out_shape=(
            jax.ShapeDtypeStruct((experts, depth, 2 * F), F32),
            jax.ShapeDtypeStruct((experts, F, depth), F32),
        ),
        compiler_params=params(),
        name="unpack_experts",
    )(packed)


def expert_kernel(info_ref, xa_ref, xb_ref, ya_ref, yb_ref, routes_ref, router_ref, w_ref, *rest):
    ma_ref, mb_ref, da_ref, db_ref, taken_ref, dz_ref, dgu_ref, hid_ref = rest[-8:]
    step = pl.program_id(0)
    first, second = info_ref[0], info_ref[1]
    expert_id = lax.broadcasted_iota(jnp.int32, (E, BLK), 0)
    slot_id = lax.broadcasted_iota(jnp.int32, (SLOT, BLK), 0)
    upto = (
        lax.broadcasted_iota(jnp.int32, (BLK, BLK), 0) <= lax.broadcasted_iota(jnp.int32, (BLK, BLK), 1)
    ).astype(BF)
    row_id = lax.broadcasted_iota(jnp.int32, (8, BLK), 0)
    picks, slot_gates, taken, dz = [], ([], []), ([], []), ([], [])
    for b in range(4):
        x_ref, y_ref = (xa_ref, ya_ref) if b < 2 else (xb_ref, yb_ref)
        x, y = x_ref[b % 2], y_ref[b % 2]
        place = step * 2 + b % 2 + (0 if b < 2 else 4)
        routes = routes_ref[info_ref[2 + place]]
        logits = dot_nt(router_ref[...], x)[:E]
        member = expert_id == routes[0:1]
        for k in range(1, 8):
            member = member | (expert_id == routes[k : k + 1])
        masked = jnp.where(member, logits, NEG)
        shifted = jnp.exp(masked - jnp.max(masked, axis=0, keepdims=True))
        shifted = jnp.where(member, shifted, 0.0)
        gates = shifted / jnp.sum(shifted, axis=0, keepdims=True)
        member = member.astype(F32)
        rows = []
        for e in (first, second):
            here = expert_id == e
            rows.append(
                (
                    jnp.sum(jnp.where(here, gates, 0.0), axis=0, keepdims=True),
                    jnp.sum(jnp.where(here, member, 0.0), axis=0, keepdims=True),
                )
            )
        both = jnp.where(row_id == 0, rows[0][1], jnp.where(row_id == 1, rows[1][1], 0.0))
        counts = dot_nn(both.astype(BF), upto).astype(jnp.int32)
        pick = []
        for j in range(2):
            spot = jnp.where(rows[j][1] > 0.0, counts[j : j + 1] - 1, -1)
            hot = (slot_id == spot).astype(F32)
            slot_gates[j].append(jnp.sum(hot * rows[j][0], axis=1, keepdims=True))
            pick.append(hot)
        pick = jnp.concatenate(pick, axis=0).astype(BF)
        picks.append(pick)
        got = dot_nn(pick, x)
        taken[0].append(got[:SLOT])
        taken[1].append(got[SLOT:])
        got = dot_nn(pick, y)
        dz[0].append(got[:SLOT])
        dz[1].append(got[SLOT:])
    sends, backs = [], []
    for j in range(2):
        width = F if j == 0 else QF
        in_at = 0 if j == 0 else 2 * F
        out_at = 2 * F + 2 * QF + (0 if j == 0 else F)
        rows = jnp.concatenate(taken[j], axis=0).astype(BF)
        grads = jnp.concatenate(dz[j], axis=0).astype(BF)
        gate = jnp.concatenate(slot_gates[j], axis=0)
        taken_ref[0, j] = rows
        dz_ref[0, j] = grads
        w_in = w_ref[:, in_at : in_at + 2 * width]
        w_out = w_ref[:, out_at : out_at + width]
        gate_up = dot_nn(rows, w_in)
        gate_part, up_part = gate_up[:, :width], gate_up[:, width:]
        sig = 1.0 / (1.0 + jnp.exp(-gate_part))
        silu = gate_part * sig
        hidden = silu * up_part
        scaled = (gate * hidden).astype(BF)
        hid_at = 0 if j == 0 else F
        hid_ref[0, :, hid_at : hid_at + width] = scaled
        sends.append(dot_nt(scaled, w_out))
        raw = dot_nn(grads, w_out)
        dgate = jnp.sum(hidden.astype(BF).astype(F32) * raw, axis=1, keepdims=True)
        dhid = gate * raw
        dgu = jnp.concatenate(
            [dhid * up_part * (sig * (1.0 + gate_part * (1.0 - sig))), dhid * silu], axis=1
        ).astype(BF)
        dgu_ref[0, :, in_at : in_at + 2 * width] = dgu
        back = dot_nt(dgu, w_in)
        lane = lax.broadcasted_iota(jnp.int32, (1, 128), 1)
        e = first if j == 0 else second
        high = dgate.astype(BF).astype(F32)
        extra = jnp.where(lane == e, high, 0.0) + jnp.where(lane == e + 64, dgate - high, 0.0)
        backs.append(jnp.concatenate([back, extra], axis=1))
    for b in range(4):
        m_ref, d_ref = (ma_ref, da_ref) if b < 2 else (mb_ref, db_ref)
        at = slice(b * SLOT, (b + 1) * SLOT)
        for values, ref in ((sends, m_ref), (backs, d_ref)):
            stacked = jnp.concatenate([values[0][at], values[1][at]], axis=0).astype(BF)
            ref[b % 2] = dot_tn(picks[b], stacked).astype(BF)


def expert_chunk(chunk, chunks, info, rows, grads, routes, router_t, weights, stash):
    width = rows[0].shape[-1]
    steps = 2
    half = pl.BlockSpec((2, BLK, width), lambda s, i: (s, 0, 0))
    half_wide = pl.BlockSpec((2, BLK, width + 128), lambda s, i: (s, 0, 0))
    slots = 4 * SLOT
    total = chunks * steps
    shape = jax.ShapeDtypeStruct
    stash_shapes = [
        shape((total, 2, slots, width), BF),
        shape((total, 2, slots, width), BF),
        shape((total, slots, 2 * F + 2 * QF), BF),
        shape((total, slots, F + QF), BF),
    ]
    stash_specs = [
        pl.BlockSpec(
            (1,) + s.shape[1:], lambda i, _, n=len(s.shape): (i + chunk * steps,) + (0,) * (n - 1)
        )
        for s in stash_shapes
    ]
    given = [] if stash is None else list(stash)
    out = pl.pallas_call(
        expert_kernel,
        grid_spec=pltpu.PrefetchScalarGridSpec(
            num_scalar_prefetch=1,
            grid=(steps,),
            in_specs=[half] * 4
            + [whole(routes.shape), whole(router_t.shape), whole(weights.shape)]
            + [pl.BlockSpec(memory_space=pl.ANY)] * len(given),
            out_specs=[half, half, half_wide, half_wide] + stash_specs,
        ),
        out_shape=[shape((4, BLK, width), BF)] * 2 + [shape((4, BLK, width + 128), BF)] * 2 + stash_shapes,
        input_output_aliases={8 + k: 4 + k for k in range(len(given))},
        compiler_params=params(),
        cost_estimate=pl.CostEstimate(flops=12 * 10**9, bytes_accessed=40 * 10**6, transcendentals=10**6),
        name="experts",
    )(info, rows[0], rows[1], grads[0], grads[1], routes, router_t, weights, *given)
    return (out[0], out[1]), (out[2], out[3]), out[4:]


def wgrad_kernel(steps, taken_ref, dz_ref, dgu_ref, hid_ref, out_ref, acc_ref):
    k = pl.program_id(0)
    flat = lambda v: v.reshape((-1, v.shape[-1]))

    def put(at, width, value):
        @pl.when(k == 0)
        def _():
            acc_ref[:, at : at + width] = value

        @pl.when(k > 0)
        def _():
            acc_ref[:, at : at + width] += value

    put(0, 2 * F, dot_tn(flat(taken_ref[:, 0]), flat(dgu_ref[:, :, : 2 * F])))
    put(2 * F, 2 * QF, dot_tn(flat(taken_ref[:, 1]), flat(dgu_ref[:, :, 2 * F :])))
    put(2 * F + 2 * QF, F, dot_tn(flat(dz_ref[:, 0]), flat(hid_ref[:, :, :F])))
    put(3 * F + 2 * QF, QF, dot_tn(flat(dz_ref[:, 1]), flat(hid_ref[:, :, F:])))

    @pl.when(k == steps - 1)
    def _():
        out_ref[...] = acc_ref[...].astype(BF)


def expert_wgrad(stash):
    taken, dz, dgu, hid = stash
    at_once = 2
    steps = taken.shape[0] // at_once
    width = taken.shape[-1]
    spec = lambda a: pl.BlockSpec((at_once,) + a.shape[1:], lambda k: (k,) + (0,) * (len(a.shape) - 1))
    return pl.pallas_call(
        functools.partial(wgrad_kernel, steps),
        grid=(steps,),
        in_specs=[spec(a) for a in stash],
        out_specs=whole((width, WCOLS)),
        out_shape=jax.ShapeDtypeStruct((width, WCOLS), BF),
        scratch_shapes=[pltpu.VMEM((width, WCOLS), F32)],
        compiler_params=params(),
        cost_estimate=pl.CostEstimate(flops=17 * 10**9, bytes_accessed=50 * 10**6, transcendentals=0),
        name="expert_wgrad",
    )(*stash)


def swap_halves(values):
    width = values.shape[1]
    lane = lax.broadcasted_iota(jnp.int32, values.shape, 1)
    up = pltpu.roll(values, width - HD // 2, 1)
    down = pltpu.roll(values, HD // 2, 1)
    return jnp.where((lane & (HD - 1)) < HD // 2, up, down)


def spread(table, width):
    return jnp.concatenate([table] * (width // 128), axis=1)


def allowed_mask(starts, block, window):
    first = (block - window + 1) * BLK
    shape = (BLK, window * BLK)
    query = block * BLK + lax.broadcasted_iota(jnp.int32, shape, 0)
    key = first + lax.broadcasted_iota(jnp.int32, shape, 1)
    begin = jnp.zeros(shape, jnp.int32)
    for s in starts:
        begin = jnp.where(query >= s, s, begin)
    return (key >= begin) & (key <= query)


def over_windows(block, blocks, body):
    for w in range(1, min(WIN_BLOCKS + 1, blocks) + 1):
        last = w == WIN_BLOCKS + 1
        pl.when((block >= w - 1) if last else (block == w - 1))(functools.partial(body, w))


def heads_to_rows(values, first):
    return jnp.concatenate([values[:, (first + g) * HD : (first + g + 1) * HD] for g in range(GRP)], axis=0)


def rows_to_heads(values):
    return [values[g * BLK : (g + 1) * BLK] for g in range(GRP)]


def attend_kernel(heads, blocks, seqs, info_ref, n1_ref, w_ref, cos_ref, sin_ref, out_ref, qkv_ref, o_ref, lse_ref):
    i = pl.program_id(0)
    q_wide, kv_wide = heads * GRP * HD, heads * HD
    rot_wide, qkv_wide = q_wide + kv_wide, q_wide + 2 * kv_wide
    projected = dot_nn(n1_ref[0], w_ref[:, :qkv_wide])
    turning = projected[:, :rot_wide]
    turned = turning * spread(cos_ref[...], rot_wide) + swap_halves(turning) * spread(sin_ref[...], rot_wide)
    rows = pl.ds(pl.multiple_of(i * BLK, BLK), BLK)
    queries = (turned[:, :q_wide].astype(BF).astype(F32) * SCALE).astype(BF)
    qkv_ref[rows, :q_wide] = queries
    qkv_ref[rows, q_wide:rot_wide] = turned[:, q_wide:].astype(BF)
    qkv_ref[rows, rot_wide:] = projected[:, rot_wide:].astype(BF)
    starts = [info_ref[blocks + s] for s in range(seqs)]

    def attend(window):
        keep = allowed_mask(starts, i, window)
        keys = pl.ds(pl.multiple_of((i - window + 1) * BLK, BLK), window * BLK)
        lane = lax.broadcasted_iota(jnp.int32, (BLK, 128), 1)
        lse_all = jnp.zeros((BLK, 128), F32)
        attended = []
        for h in range(heads):
            k_rows = qkv_ref[keys, q_wide + h * HD : q_wide + (h + 1) * HD]
            v_rows = qkv_ref[keys, rot_wide + h * HD : rot_wide + (h + 1) * HD]
            scores = dot_nt(heads_to_rows(queries, h * GRP), k_rows)
            for g in range(GRP):
                part = jnp.where(keep, scores[g * BLK : (g + 1) * BLK], NEG)
                top = jnp.max(part, axis=1, keepdims=True)
                shifted = jnp.exp(part - top)
                total = jnp.sum(shifted, axis=1, keepdims=True)
                probability = (shifted * (1.0 / total)).astype(BF)
                attended.append(dot_nn(probability, v_rows).astype(BF))
                lse_all = jnp.where(lane == h * GRP + g, top + jnp.log(total), lse_all)
        lse_ref[...] = lse_all
        attended = jnp.concatenate(attended, axis=1)
        o_ref[...] = attended
        out_ref[0] = dot_nt(attended, w_ref[:, qkv_wide:]).astype(BF)

    over_windows(i, blocks, attend)


def attend_forward(heads, info, normed, weights, cosine, sine, seqs):
    blocks, _, width = normed.shape
    rows = blocks * BLK
    q_wide = heads * GRP * HD
    qkv_wide = q_wide + 2 * heads * HD
    shape = jax.ShapeDtypeStruct
    return pl.pallas_call(
        functools.partial(attend_kernel, heads, blocks, seqs),
        grid_spec=pltpu.PrefetchScalarGridSpec(
            num_scalar_prefetch=1,
            grid=(blocks,),
            in_specs=[
                pl.BlockSpec((1, BLK, width), lambda i, info: (info[i], 0, 0)),
                whole(weights.shape),
                pl.BlockSpec((BLK, 128), lambda i, info: (i, 0)),
                pl.BlockSpec((BLK, 128), lambda i, info: (i, 0)),
            ],
            out_specs=[
                pl.BlockSpec((1, BLK, width), lambda i, info: (info[i], 0, 0)),
                whole((rows, qkv_wide)),
                pl.BlockSpec((BLK, q_wide), lambda i, info: (i, 0)),
                pl.BlockSpec((BLK, 128), lambda i, info: (i, 0)),
            ],
        ),
        out_shape=[
            shape((blocks, BLK, width), BF),
            shape((rows, qkv_wide), BF),
            shape((rows, q_wide), BF),
            shape((rows, 128), F32),
        ],
        compiler_params=params(),
        cost_estimate=pl.CostEstimate(flops=5 * 10**9, bytes_accessed=12 * 10**6, transcendentals=4 * 10**6),
        name="attend",
    )(info, normed, weights, cosine, sine)


def attend_back_kernel(
    heads,
    blocks,
    seqs,
    info_ref,
    da_ref,
    n1_ref,
    w_ref,
    cos_ref,
    sin_ref,
    qkv_ref,
    o_ref,
    lse_ref,
    dn1_ref,
    dw_ref,
    gain_ref,
    acc_ref,
    dq_ref,
    dkv_ref,
):
    step = pl.program_id(0)
    q_wide, kv_wide = heads * GRP * HD, heads * HD
    rot_wide, qkv_wide = q_wide + kv_wide, q_wide + 2 * kv_wide
    starts = [info_ref[blocks + s] for s in range(seqs)]

    @pl.when(step == 0)
    def _():
        acc_ref[...] = jnp.zeros_like(acc_ref)
        dkv_ref[...] = jnp.zeros_like(dkv_ref)
        gain_ref[...] = jnp.zeros_like(gain_ref)

    @pl.when(step < blocks)
    def _():
        i = step
        da = da_ref[0]
        w_out = w_ref[:, qkv_wide:]
        grad = dot_nn(da, w_out).astype(BF)
        acc_ref[:, qkv_wide:] += dot_tn(da, o_ref[...])
        rows = pl.ds(pl.multiple_of(i * BLK, BLK), BLK)
        queries = qkv_ref[rows, :q_wide]
        lse = lse_ref[...]

        def back(window):
            keep = allowed_mask(starts, i, window)
            keys = pl.ds(pl.multiple_of((i - window + 1) * BLK, BLK), window * BLK)
            for h in range(heads):
                k_rows = qkv_ref[keys, q_wide + h * HD : q_wide + (h + 1) * HD]
                v_rows = qkv_ref[keys, rot_wide + h * HD : rot_wide + (h + 1) * HD]
                stacked_q = heads_to_rows(queries, h * GRP)
                stacked_g = heads_to_rows(grad, h * GRP)
                scores = dot_nt(stacked_q, k_rows)
                dprob = dot_nt(stacked_g, v_rows)
                probs, dscores = [], []
                for g in range(GRP):
                    at = slice(g * BLK, (g + 1) * BLK)
                    one = h * GRP + g
                    prob = jnp.where(keep, jnp.exp(scores[at] - lse[:, one : one + 1]), 0.0)
                    both = prob * dprob[at]
                    inner = jnp.sum(both, axis=1, keepdims=True)
                    dscores.append((both - prob * inner).astype(BF))
                    probs.append(prob.astype(BF))
                probs = jnp.concatenate(probs, axis=0)
                dscores = jnp.concatenate(dscores, axis=0)
                dq = dot_nn(dscores, k_rows) * SCALE
                dq_ref[rows, h * GRP * HD : (h + 1) * GRP * HD] = jnp.concatenate(rows_to_heads(dq), axis=1)
                dkv_ref[h, keys, :HD] += dot_tn(dscores, stacked_q)
                dkv_ref[h, keys, HD:] += dot_tn(probs, stacked_g)

        over_windows(i, blocks, back)

    @pl.when(step >= blocks)
    def _():
        j = step - blocks
        rows = pl.ds(pl.multiple_of(j * BLK, BLK), BLK)
        dk = [dkv_ref[h, rows, :HD] for h in range(heads)]
        dv = [dkv_ref[h, rows, HD:] for h in range(heads)]
        turned = jnp.concatenate([dq_ref[rows, :]] + dk, axis=1)
        turned = turned * spread(cos_ref[...], rot_wide) - swap_halves(turned) * spread(sin_ref[...], rot_wide)
        dqkv = jnp.concatenate([turned] + dv, axis=1).astype(BF)
        n1 = n1_ref[0]
        acc_ref[:, :qkv_wide] += dot_tn(n1, dqkv)
        dn1 = dot_nt(dqkv, w_ref[:, :qkv_wide])
        gain_ref[...] += jnp.sum(dn1 * n1.astype(F32), axis=0, keepdims=True)
        dn1_ref[0] = dn1.astype(BF)

    @pl.when(step == 2 * blocks - 1)
    def _():
        dw_ref[...] = acc_ref[...].astype(BF)


def attend_backward(heads, info, da, normed, weights, cosine, sine, qkv, attended, lse, seqs):
    blocks, _, width = normed.shape
    rows = blocks * BLK
    q_wide = heads * GRP * HD
    shape = jax.ShapeDtypeStruct
    early = lambda i: jnp.minimum(i, blocks - 1)
    late = lambda i: jnp.maximum(i - blocks, 0)
    return pl.pallas_call(
        functools.partial(attend_back_kernel, heads, blocks, seqs),
        grid_spec=pltpu.PrefetchScalarGridSpec(
            num_scalar_prefetch=1,
            grid=(2 * blocks,),
            in_specs=[
                pl.BlockSpec((1, BLK, width), lambda i, info: (info[early(i)], 0, 0)),
                pl.BlockSpec((1, BLK, width), lambda i, info: (info[late(i)], 0, 0)),
                whole(weights.shape),
                pl.BlockSpec((BLK, 128), lambda i, info: (late(i), 0)),
                pl.BlockSpec((BLK, 128), lambda i, info: (late(i), 0)),
                whole(qkv.shape),
                pl.BlockSpec((BLK, q_wide), lambda i, info: (early(i), 0)),
                pl.BlockSpec((BLK, 128), lambda i, info: (early(i), 0)),
            ],
            out_specs=[
                pl.BlockSpec((1, BLK, width), lambda i, info: (info[late(i)], 0, 0)),
                whole(weights.shape),
                whole((1, width)),
            ],
            scratch_shapes=[
                pltpu.VMEM(weights.shape, F32),
                pltpu.VMEM((rows, q_wide), F32),
                pltpu.VMEM((heads, rows, 2 * HD), F32),
            ],
        ),
        out_shape=[shape((blocks, BLK, width), BF), shape(weights.shape, BF), shape((1, width), F32)],
        compiler_params=params(),
        cost_estimate=pl.CostEstimate(flops=14 * 10**9, bytes_accessed=25 * 10**6, transcendentals=4 * 10**6),
        name="attend_back",
    )(info, da, normed, weights, cosine, sine, qkv, attended, lse)


def residual_kernel(
    one_ref, two_ref, n2_ref, h_ref, gain_ref, router_ref, routes_ref, cot_ref, dh_ref, da_ref, dgain_ref, drouter_ref
):
    width = n2_ref.shape[1]
    total = one_ref[...].astype(F32) + two_ref[...].astype(F32)
    dn2 = total[:, :width]
    dgate = total[:, width:]
    dgate = dgate + pltpu.roll(dgate, 64, 1)
    n2 = n2_ref[...]
    logits = dot_nt(n2, router_ref[...])
    lane = lax.broadcasted_iota(jnp.int32, logits.shape, 1)
    routes = routes_ref[...]
    member = lane == routes[:, 0:1]
    for k in range(1, 8):
        member = member | (lane == routes[:, k : k + 1])
    masked = jnp.where(member, logits, NEG)
    shifted = jnp.where(member, jnp.exp(masked - jnp.max(masked, axis=1, keepdims=True)), 0.0)
    gates = shifted / jnp.sum(shifted, axis=1, keepdims=True)
    dgate = jnp.where(member, dgate, 0.0)
    dlogit = gates * (dgate - jnp.sum(gates * dgate, axis=1, keepdims=True))
    high = dlogit.astype(BF)
    low = (dlogit - high.astype(F32)).astype(BF)
    dn2 = dn2 + dot_nn(high, router_ref[...]) + dot_nn(low, router_ref[...])
    drouter_ref[...] = (dot_tn(high, n2) + dot_tn(low, n2))[:E]
    h = h_ref[...]
    inverse = lax.rsqrt(jnp.mean(h * h, axis=1, keepdims=True) + EPS)
    unit = h * inverse
    dgain_ref[...] = jnp.sum(dn2 * unit, axis=0, keepdims=True)
    inner = dn2 * gain_ref[...]
    dh = cot_ref[...].astype(F32) + inverse * (inner - unit * jnp.mean(inner * unit, axis=1, keepdims=True))
    dh_ref[...] = dh
    da_ref[...] = dh.astype(BF)


def residual_gradient(one, two, n2, h, gain, router_pad, routes, cotangent):
    rows, width = n2.shape
    shape = jax.ShapeDtypeStruct
    return pl.pallas_call(
        residual_kernel,
        out_shape=[
            shape((rows, width), F32),
            shape((rows, width), BF),
            shape((1, width), F32),
            shape((E, width), F32),
        ],
        compiler_params=params(),
        cost_estimate=pl.CostEstimate(flops=10**9, bytes_accessed=8 * 10**6, transcendentals=10**5),
        name="residual_gradient",
    )(one, two, n2, h, gain, router_pad, routes, cotangent)


def rms_unit(values):
    return values * lax.rsqrt(jnp.mean(values * values, axis=-1, keepdims=True) + EPS)


def rope_tables(starts, rows):
    index = jnp.arange(rows, dtype=jnp.int32)
    begin = jnp.max(jnp.where(index[:, None] >= starts[None, :], starts[None, :], 0), axis=1)
    position = (index - begin).astype(F32)
    halfway = HD // 2
    frequency = THETA ** (-(jnp.arange(halfway, dtype=F32) * 2.0 / HD))
    angles = position[:, None] * frequency[None, :]
    cosine, sine = jnp.cos(angles), jnp.sin(angles)
    return (
        jnp.concatenate([cosine] * 4, axis=1),
        jnp.concatenate([-sine, sine, -sine, sine], axis=1),
    )


def shards(tokens, cotangent, lengths, routes, norm_gains, router_weight, qkv_weight, out_weight, expert_in, expert_out):
    own_rows, width = tokens.shape
    group_rows = routes.shape[0]
    heads = qkv_weight.shape[0]
    experts = expert_in.shape[0]
    group = experts * 4 // 5
    n_dp = lax.axis_size("dp")
    links = Links(group)
    rank = links.dp % group
    own_expert = links.t * experts + rank
    part_expert = links.t * experts + group + rank // 4
    seqs = lengths.shape[1]
    blocks = group_rows // own_rows
    inputs = tokens.astype(F32)

    grouped = jnp.transpose(qkv_weight, (1, 0, 2))
    depth = grouped.shape[0]
    attention_shard = jnp.concatenate(
        [
            grouped[:, :, : GRP * HD].reshape(depth, -1),
            grouped[:, :, GRP * HD : (GRP + 1) * HD].reshape(depth, -1),
            grouped[:, :, (GRP + 1) * HD :].reshape(depth, -1),
            jnp.transpose(out_weight, (2, 0, 1)).reshape(depth, -1),
        ],
        axis=1,
    )
    attention_weights = lax.all_gather(attention_shard, "dp", axis=0, tiled=True)
    routes_own = jnp.transpose(routes).reshape(8, blocks, own_rows)
    routes_all = lax.all_gather(jnp.transpose(routes_own, (1, 0, 2)), "dp", axis=0, tiled=True)
    starts = jnp.cumsum(lengths[0]) - lengths[0]
    cosine, sine = rope_tables(starts, group_rows)
    info = jnp.concatenate([links.plane_places(), starts.astype(jnp.int32)])

    normed_first = (rms_unit(inputs) * norm_gains[0]).astype(BF)
    normed_group = links.gather_plane(normed_first)
    packed = pack_experts(expert_in, expert_out, group, n_dp)
    weights = lax.all_to_all(packed, "dp", 0, 0).reshape(width, WCOLS)
    grads = links.gather_all(cotangent)

    mixed, qkv, attended, lse = attend_forward(heads, info, normed_group, attention_weights, cosine, sine, seqs)
    residual = inputs + links.scatter_plane(mixed).astype(F32)
    normed_second = (rms_unit(residual) * norm_gains[1]).astype(BF)

    rows = links.gather_all(normed_second)
    router_t = jnp.transpose(router_weight)
    router_pad = jnp.pad(router_t, ((0, 128 - E), (0, 0)))
    mine = jnp.stack([own_expert, part_expert]).astype(jnp.int32)
    stash = None
    outs, backs = [], []
    for c, sources in enumerate(links.chunk_sources()):
        chunk_info = jnp.concatenate([mine, sources])
        out, back, stash = expert_chunk(
            c, links.chunks(), chunk_info, rows[c], grads[c], routes_all, router_t, weights, stash
        )
        outs.append(out)
        backs.append(back)
    one, two = links.scatter_all(backs)
    weights_grad = expert_wgrad(stash)
    returned = lax.all_to_all(weights_grad.reshape(n_dp, depth, WCOLS), "dp", 0, 0)
    if n_dp != group:
        returned = jnp.sum(returned.reshape(-1, group, depth, WCOLS).astype(F32), axis=0).astype(BF)
    expert_in_grad, expert_out_grad = unpack_experts(returned, experts, group)

    routes_mine = lax.dynamic_slice_in_dim(routes, links.t * own_rows, own_rows, 0)
    residual_grad, branch_grad, second_gain, router_part = residual_gradient(
        one, two, normed_second, residual, norm_gains[1:2], router_pad, routes_mine, cotangent
    )
    branch_group = links.gather_plane(branch_grad)
    dn1, attention_grad, first_gain = attend_backward(
        heads, info, branch_group, normed_group, attention_weights, cosine, sine, qkv, attended, lse, seqs
    )
    first_grad = links.scatter_plane(dn1).astype(F32)
    attention_mine = lax.psum_scatter(attention_grad, "dp", scatter_dimension=0, tiled=True).astype(F32)

    mix_one, mix_two = links.scatter_all(outs)
    layer_output = (residual + mix_one.astype(F32) + mix_two.astype(F32)).astype(BF)

    unit = rms_unit(inputs)
    inner = first_grad * norm_gains[0]
    inverse = lax.rsqrt(jnp.mean(inputs * inputs, axis=-1, keepdims=True) + EPS)
    input_grad = residual_grad + inverse * (inner - unit * jnp.mean(inner * unit, axis=-1, keepdims=True))

    router_sum = lax.psum(router_part, ("dp", "tensor"))
    gains = lax.psum(jnp.concatenate([first_gain / norm_gains[0:1], second_gain]), ("dp", "tensor"))

    q_wide, kv_wide = heads * GRP * HD, heads * HD
    split = lambda at, size: attention_mine[:, at : at + size].reshape(depth, heads, -1)
    qkv_grad = jnp.transpose(
        jnp.concatenate(
            [split(0, q_wide), split(q_wide, kv_wide), split(q_wide + kv_wide, kv_wide)], axis=2
        ),
        (1, 0, 2),
    )
    out_weight_grad = jnp.transpose(split(q_wide + 2 * kv_wide, q_wide), (1, 2, 0))
    return (
        layer_output,
        input_grad,
        gains,
        jnp.transpose(router_sum),
        qkv_grad,
        out_weight_grad,
        expert_in_grad,
        expert_out_grad,
    )


def solution(mesh):
    rows = P(("dp", "tensor"), None)
    return jax.shard_map(
        shards,
        mesh=mesh,
        in_specs=(
            rows,
            rows,
            P("dp", None),
            P("dp", None),
            P(),
            P(),
            P("tensor", "dp", None),
            P("tensor", None, "dp"),
            P("tensor", "dp", None),
            P("tensor", None, "dp"),
        ),
        out_specs=(
            rows,
            rows,
            P(),
            P(),
            P("tensor", "dp", None),
            P("tensor", None, "dp"),
            P("tensor", "dp", None),
            P("tensor", None, "dp"),
        ),
        check_vma=False,
    )
```

time: 2310 us -> 1080 us (0.47)
  matrix products: 690 us -> 0 us
  waiting for transfers between devices: 1240 us -> 557 us
  Pallas kernels: 0 us -> 234 us
  local copies, waits for them, and re-layouts: 209 us -> 43 us
  starting transfers between devices: 0.73 us -> 91.3 us
  other arithmetic: 102 us -> 77 us
    dot_general x76 -> x0, matrix products: 690 us -> none  [the longest x4 146 us: backward_block(): jnp.einsum('esd,esf->edf', taken, gate_up_grad, preferred_element_type=jn...]
    reduce_scatter x7 -> x1, waiting for transfers between devices: 573 us -> 0.01 us  [shards(): lax.psum_scatter(attention_grad, 'dp', scatter_dimension=0, tiled=True)]
    all_gather x8 -> x1, waiting for transfers between devices: 539 us -> 23.4 us  [shards(): lax.all_gather(attention_shard, 'dp', axis=0, tiled=True)]
    ppermute x0 -> x88, waiting for transfers between devices: none -> 473 us  [send(): return lax.ppermute(value, ('dp', 'tensor'), perm)]
    pallas_call x0 -> x10, Pallas kernels: none -> 234 us  [the longest x4 118 us: expert_chunk(): pl.pallas_call(expert_kernel, grid_spec=pltpu.PrefetchScalarGridSpec(num_...]
    ppermute x0 -> x88, starting transfers between devices: none -> 81 us  [send(): return lax.ppermute(value, ('dp', 'tensor'), perm)]
    gather x5 -> x0, local copies, waits for them, and re-layouts: 66.4 us -> none  [shards(): chosen = jnp.take_along_axis(logits, routes, axis=1)]
    psum x1, waiting for transfers between devices: 123 us -> 60.5 us  [shards(): router_sum = lax.psum(router_part, ('dp', 'tensor'))]
  transfers between devices with their start and end apart: 18 -> 93, of which waited for: 14 -> 36; matrix products, arithmetic and copies ran while one was open for 14% -> 9% of each run, Pallas kernels for 0% -> 22%
where the time goes in v1:
time: 1080 us; the launch traced here: 1070 us
  waiting for transfers between devices  557 us (52%)
  Pallas kernels  234 us (22%)
  starting transfers between devices  91.3 us (8%)
  other arithmetic  77 us (7%)
  blocking collectives  53.9 us (5%)
  local copies, waits for them, and re-layouts  43 us (4%)
  between operations  15 us (1%)
    ppermute x88, waiting for transfers between devices, send(): return lax.ppermute(value, ('dp', 'tensor'), perm)  473 us
    pallas_call x4, Pallas kernels, expert_chunk(): pl.pallas_call(expert_kernel, grid_spec=pltpu.PrefetchScalarGridSpec(num_...  118 us
    ppermute x88, starting transfers between devices, send(): return lax.ppermute(value, ('dp', 'tensor'), perm)  81 us
    psum x1, waiting for transfers between devices, shards(): router_sum = lax.psum(router_part, ('dp', 'tensor'))  60.5 us
    pallas_call x1, Pallas kernels, expert_wgrad(): pl.pallas_call(functools.partial(wgrad_kernel, steps), grid=(steps,), in_...  39.6 us
    psum x1, blocking collectives, shards(): lax.psum(jnp.concatenate([first_gain / norm_gains[0:1], second_gain]), ('...  38.5 us
    convert_element_type x25, other arithmetic, add(): return (a.astype(F32) + b.astype(F32)).astype(a.dtype)  36.4 us
    pallas_call x1, Pallas kernels, attend_backward(): pl.pallas_call(functools.partial(attend_back_kernel, heads, blocks, seqs)...  34.3 us
  transfers between devices with their start and end apart: 93, of which 36 were waited for; matrix products, arithmetic and copies ran while one was open for 9% of the time, Pallas kernels for 22%

profile of v1, /device:TPU:0, one launch (start us, length us, event | category | flops | bytes accessed | tf_op | source)
XLA Modules:
  0.0 1071.8 jit_solution(5565790423100962853)
XLA Ops:
  54.9 9.6 collective-permute-done.2
  67.5 23.4 %all-gather.2.cloned.1.call-done.w_ref = bf16[1536,1024]{1,0:T(8,128)(2,1)} async-done(((bf16[192,1024]{1,0:T(8,128)(2,1)}), bf16[1536,1024]{1,0:T(8,128)(2,1)}) %all-gather.2.cloned.1.call-update) | async-done | bytes 3145744 | tf_op jit(solution)/shard_map/all_gather | solution.py:735
  90.9 18.5 %attend.1 = (bf16[4,256,1536]{2,1,0:T(8,128)(2,1)}, bf16[1024,640]{1,0:T(8,128)(2,1)}, bf16[1024,384]{1,0:T(8,128)(2,1)}, f32[1024,128]{1,0:T(8,128)}) custom-call(s32[8]{0:T(128)} %pad_add_fusion.info_ref, bf16[4,256,1536]{2,1,0:T(8,128)(2,1)} %pad_maximum_fusion.n1_ref, bf16[1536,1024]{1,0:T(8,128)(2,1)} %all-gather.2.cloned.1.call-done.w_ref, ...), custom_call_target="tpu_custom_call" | custom-call | flops 5000000000 | bytes 12000000 | tf_op jit(solution)/shard_map/attend/pallas_call | solution.py:480
  118.5 12.0 %collective-permute-done.4 = bf16[256,1536]{1,0:T(8,128)(2,1)S(1)} collective-permute-done((bf16[256,1536]{1,0:T(8,128)(2,1)S(1)}, bf16[256,1536]{1,0:T(8,128)(2,1)S(1)}, u32[]{:S(2)}, u32[]{:S(2)}) %collective-permute-start.4) | collective-permute-done | bytes 786464 | tf_op jit(solution)/shard_map/ppermute | solution.py:66
  131.4 8.5 collective-permute-done.11
  140.8 78.7 %collective-permute-done.38 = bf16[256,1536]{1,0:T(8,128)(2,1)S(1)} collective-permute-done((bf16[256,1536]{1,0:T(8,128)(2,1)}, bf16[256,1536]{1,0:T(8,128)(2,1)S(1)}, u32[]{:S(2)}, u32[]{:S(2)}) %collective-permute-start.38) | collective-permute-done | bytes 786464 | tf_op jit(solution)/shard_map/ppermute | solution.py:66
  225.4 14.6 %collective-permute-done.39 = bf16[256,1536]{1,0:T(8,128)(2,1)S(1)} collective-permute-done((bf16[256,1536]{1,0:T(8,128)(2,1)S(1)}, bf16[256,1536]{1,0:T(8,128)(2,1)S(1)}, u32[]{:S(2)}, u32[]{:S(2)}) %collective-permute-start.39) | collective-permute-done | bytes 786464 | tf_op jit(solution)/shard_map/ppermute | solution.py:66
  240.8 11.4 %collective-permute-done.26 = bf16[256,1536]{1,0:T(8,128)(2,1)S(1)} collective-permute-done((bf16[256,1536]{1,0:T(8,128)(2,1)S(1)}, bf16[256,1536]{1,0:T(8,128)(2,1)S(1)}, u32[]{:S(2)}, u32[]{:S(2)}) %collective-permute-start.26) | collective-permute-done | bytes 786464 | tf_op jit(solution)/shard_map/ppermute | solution.py:66
  263.2 11.0 %collective-permute-done.55 = bf16[256,1536]{1,0:T(8,128)(2,1)S(1)} collective-permute-done((bf16[256,1536]{1,0:T(8,128)(2,1)S(1)}, bf16[256,1536]{1,0:T(8,128)(2,1)S(1)}, u32[]{:S(2)}, u32[]{:S(2)}) %collective-permute-start.55) | collective-permute-done | bytes 786464 | tf_op jit(solution)/shard_map/ppermute | solution.py:66
  275.7 15.4 %collective-permute-done.56 = bf16[256,1536]{1,0:T(8,128)(2,1)S(1)} collective-permute-done((bf16[256,1536]{1,0:T(8,128)(2,1)S(1)}, bf16[256,1536]{1,0:T(8,128)(2,1)S(1)}, u32[]{:S(2)}, u32[]{:S(2)}) %collective-permute-start.56) | collective-permute-done | bytes 786464 | tf_op jit(solution)/shard_map/ppermute | solution.py:66
  293.8 10.9 %collective-permute-done.7 = bf16[256,1536]{1,0:T(8,128)(2,1)S(1)} collective-permute-done((bf16[256,1536]{1,0:T(8,128)(2,1)S(1)}, bf16[256,1536]{1,0:T(8,128)(2,1)S(1)}, u32[]{:S(2)}, u32[]{:S(2)}) %collective-permute-start.7) | collective-permute-done | bytes 786464 | tf_op jit(solution)/shard_map/ppermute | solution.py:66
  342.9 12.9 %collective-permute-done.35 = bf16[256,1536]{1,0:T(8,128)(2,1)S(1)} collective-permute-done((bf16[256,1536]{1,0:T(8,128)(2,1)S(1)}, bf16[256,1536]{1,0:T(8,128)(2,1)S(1)}, u32[]{:S(2)}, u32[]{:S(2)}) %collective-permute-start.35) | collective-permute-done | bytes 786464 | tf_op jit(solution)/shard_map/ppermute | solution.py:66
  380.0 8.1 collective-permute-done.51
  392.3 15.4 %all_gather.7.routes_ref = s32[32,8,256]{2,1,0:T(8,128)} all-gather(s32[4,8,256]{2,1,0:T(8,128)S(1)} %bitcast.291), channel_id=1, replica_groups=mesh['dp'=8,'tensor'=4] {'dp'}, dimensions={0}, use_global_device_ids=true | all-gather | bytes 294912 | tf_op jit(solution)/shard_map/all_gather | solution.py:737
  414.7 29.4 %experts.4 = (bf16[4,256,1536]{2,1,0:T(8,128)(2,1)}, bf16[4,256,1536]{2,1,0:T(8,128)(2,1)}, bf16[4,256,1664]{2,1,0:T(8,128)(2,1)}, bf16[4,256,1664]{2,1,0:T(8,12...) custom-call(s32[10]{0:T(128)} %concatenate.38.info_ref, ...), custom_call_target="tpu_custom_call" | custom-call | flops 12000000000 | bytes 40000000 | tf_op jit(solution)/shard_map/experts/pallas_call | solution.py:336
  444.5 29.8 %experts.5 = (bf16[4,256,1536]{2,1,0:T(8,128)(2,1)}, bf16[4,256,1536]{2,1,0:T(8,128)(2,1)}, bf16[4,256,1664]{2,1,0:T(8,128)(2,1)}, bf16[4,256,1664]{2,1,0:T(8,12...) custom-call(s32[10]{0:T(128)} %concatenate.39.info_ref, ...), custom_call_target="tpu_custom_call", output_to_operand_aliasing={{4}: (8, {}), {5}: (9, {}), {6}: (10, {}), {7}: (11, {})} | custom-call | flops 12000000000 | bytes 40000000 | tf_op jit(solution)/shard_map/experts/pallas_call | solution.py:336
  474.9 29.5 %experts.6 = (bf16[4,256,1536]{2,1,0:T(8,128)(2,1)}, bf16[4,256,1536]{2,1,0:T(8,128)(2,1)}, bf16[4,256,1664]{2,1,0:T(8,128)(2,1)}, bf16[4,256,1664]{2,1,0:T(8,12...) custom-call(s32[10]{0:T(128)} %concatenate.40.info_ref, ...), custom_call_target="tpu_custom_call", output_to_operand_aliasing={{4}: (8, {}), {5}: (9, {}), {6}: (10, {}), {7}: (11, {})} | custom-call | flops 12000000000 | bytes 40000000 | tf_op jit(solution)/shard_map/experts/pallas_call | solution.py:336
  506.1 29.6 %experts.7 = (bf16[4,256,1536]{2,1,0:T(8,128)(2,1)}, bf16[4,256,1536]{2,1,0:T(8,128)(2,1)}, bf16[4,256,1664]{2,1,0:T(8,128)(2,1)}, bf16[4,256,1664]{2,1,0:T(8,12...) custom-call(s32[10]{0:T(128)} %concatenate.41.info_ref, ...), custom_call_target="tpu_custom_call", output_to_operand_aliasing={{4}: (8, {}), {5}: (9, {}), {6}: (10, {}), {7}: (11, {})} | custom-call | flops 12000000000 | bytes 40000000 | tf_op jit(solution)/shard_map/experts/pallas_call | solution.py:336
  535.7 39.6 %expert_wgrad.1 = bf16[1536,1920]{1,0:T(8,128)(2,1)} custom-call(bf16[8,2,352,1536]{3,2,1,0:T(8,128)(2,1)} %get-tuple-element.92.taken_ref, bf16[8,2,352,1536]{3,2,1,0:T(8,128)(2,1)} %get-tuple-element.93.dz_ref, bf16[8,352,1280]{2,1,0:T(8,128)(2,1)} %get-tuple-element.94.dgu_ref, bf16[8,352,640]{2,1,0:T(8,128)(2,1)} %get-tuple-element.95.hid_ref), custom_call_target="tpu_custom_call" | custom-call | flops 16999999488 | bytes 50000000 | tf_op jit(solution)/shard_map/expert_wgrad/pallas_call | solution.py:384
  604.0 25.0 %collective-permute-done.74 = bf16[256,1664]{1,0:T(8,128)(2,1)S(1)} collective-permute-done((bf16[256,1664]{1,0:T(8,128)(2,1)}, bf16[256,1664]{1,0:T(8,128)(2,1)S(1)}, u32[]{:S(2)}, u32[]{:S(2)}) %collective-permute-start.74) | collective-permute-done | bytes 852000 | tf_op jit(solution)/shard_map/ppermute | solution.py:66
  637.8 22.1 %collective-permute-done.79 = bf16[256,1664]{1,0:T(8,128)(2,1)S(1)} collective-permute-done((bf16[256,1664]{1,0:T(8,128)(2,1)S(1)}, bf16[256,1664]{1,0:T(8,128)(2,1)S(1)}, u32[]{:S(2)}, u32[]{:S(2)}) %collective-permute-start.79) | collective-permute-done | bytes 852000 | tf_op jit(solution)/shard_map/ppermute | solution.py:66
  662.3 66.8 %collective-permute-done.71 = bf16[256,1664]{1,0:T(8,128)(2,1)S(1)} collective-permute-done((bf16[256,1664]{1,0:T(8,128)(2,1)S(1)}, bf16[256,1664]{1,0:T(8,128)(2,1)S(1)}, u32[]{:S(2)}, u32[]{:S(2)}) %collective-permute-start.71) | collective-permute-done | bytes 852000 | tf_op jit(solution)/shard_map/ppermute | solution.py:66
  732.3 17.6 %collective-permute-done.80 = bf16[256,1664]{1,0:T(8,128)(2,1)S(1)} collective-permute-done((bf16[256,1664]{1,0:T(8,128)(2,1)S(1)}, bf16[256,1664]{1,0:T(8,128)(2,1)S(1)}, u32[]{:S(2)}, u32[]{:S(2)}) %collective-permute-start.80) | collective-permute-done | bytes 852000 | tf_op jit(solution)/shard_map/ppermute | solution.py:66
  755.3 13.2 %collective-permute-done.66 = bf16[256,1664]{1,0:T(8,128)(2,1)S(1)} collective-permute-done((bf16[256,1664]{1,0:T(8,128)(2,1)S(1)}, bf16[256,1664]{1,0:T(8,128)(2,1)S(1)}, u32[]{:S(2)}, u32[]{:S(2)}) %collective-permute-start.66) | collective-permute-done | bytes 852000 | tf_op jit(solution)/shard_map/ppermute | solution.py:66
  799.4 13.6 %collective-permute-done.31 = bf16[256,1536]{1,0:T(8,128)(2,1)S(1)} collective-permute-done((bf16[256,1536]{1,0:T(8,128)(2,1)S(1)}, bf16[256,1536]{1,0:T(8,128)(2,1)S(1)}, u32[]{:S(2)}, u32[]{:S(2)}) %collective-permute-start.31) | collective-permute-done | bytes 786464 | tf_op jit(solution)/shard_map/ppermute | solution.py:66
  818.2 34.3 %attend_back.1 = (bf16[4,256,1536]{2,1,0:T(8,128)(2,1)}, bf16[1536,1024]{1,0:T(8,128)(2,1)}, f32[1,1536]{1,0:T(1,128)}) custom-call(s32[8]{0:T(128)} %pad_add_fusion.info_ref, bf16[4,256,1536]{2,1,0:T(8,128)(2,1)} %pad_maximum_fusion.9.da_ref, bf16[4,256,1536]{2,1,0:T(8,128)(2,1)} %pad_maximum_fusion.n1_ref, ...), custom_call_target="tpu_custom_call" | custom-call | flops 14000000000 | bytes 25000000 | tf_op jit(solution)/shard_map/attend_back/pallas_call | solution.py:607
  875.9 14.4 %collective-permute-done.16 = bf16[256,1536]{1,0:T(8,128)(2,1)S(1)} collective-permute-done((bf16[256,1536]{1,0:T(8,128)(2,1)S(1)}, bf16[256,1536]{1,0:T(8,128)(2,1)S(1)}, u32[]{:S(2)}, u32[]{:S(2)}) %collective-permute-start.16) | collective-permute-done | bytes 786464 | tf_op jit(solution)/shard_map/ppermute | solution.py:66
  890.7 27.0 %collective-permute-done.59 = bf16[256,1536]{1,0:T(8,128)(2,1)S(1)} collective-permute-done((bf16[256,1536]{1,0:T(8,128)(2,1)S(1)}, bf16[256,1536]{1,0:T(8,128)(2,1)S(1)}, u32[]{:S(2)}, u32[]{:S(2)}) %collective-permute-start.59) | collective-permute-done | bytes 786464 | tf_op jit(solution)/shard_map/ppermute | solution.py:66
  920.3 9.4 collective-permute-done.86
  940.3 38.5 %psum.14 = f32[2,1536]{1,0:T(2,128)} all-reduce(f32[2,1536]{1,0:T(2,128)S(1)} %pad_maximum_fusion.13), channel_id=1, replica_groups=mesh['dp'=8,'tensor'=4] {'dp','tensor'}, use_global_device_ids=true, to_apply=%region_5.6 | all-reduce | flops 3072 | bytes 24576 | tf_op jit(solution)/shard_map/psum | solution.py:792
  983.6 9.2 unpack_experts.1
  1002.9 60.5 %all-reduce.3.cloned.1.call-done = f32[1536,40]{0,1:T(8,128)} async-done(((f32[1536,40]{0,1:T(8,128)}), f32[1536,40]{0,1:T(8,128)}) %all-reduce.3.cloned.1.call-update) | async-done | bytes 245776 | tf_op jit(solution)/shard_map/psum | solution.py:791
  (370 shorter events, 296.7 us)
Async XLA Ops:
  7.2 83.7 %all-gather.2.cloned.1.call-start = ((), (), s32[]{:S(2)}) async-start(), calls=%async_computation.3 | async-start | bytes 3538944 | tf_op jit(solution)/shard_map/all_gather | solution.py:735
  31.4 81.7 %collective-permute-start.23 = (bf16[256,1536]{1,0:T(8,128)(2,1)S(1)}, bf16[256,1536]{1,0:T(8,128)(2,1)}, u32[]{:S(2)}, u32[]{:S(2)}) collective-permute-start(bf16[256,1536]{1,0:T(8,128)(2,1)S(1)} %copy-done.17), channel_id=1, source_target_pairs={{0,8},{1,9},{2,10},{3,11},{4,12},{5,13},{6,14},{7,15},{8,24},{9,25... | collective-permute-start | bytes 2359304 | tf_op jit(solution)/shard_map/ppermute | solution.py:66
  33.0 83.5 %collective-permute-start.10 = (bf16[256,1536]{1,0:T(8,128)(2,1)S(1)}, bf16[256,1536]{1,0:T(8,128)(2,1)}, u32[]{:S(2)}, u32[]{:S(2)}) collective-permute-start(bf16[256,1536]{1,0:T(8,128)(2,1)S(1)} %copy-done.17), channel_id=1, source_target_pairs={{0,1},{1,0},{2,3},{3,2},{4,6},{5,7},{6,4},{7,5},{8,9},{9,8},{10,11... | collective-permute-start | bytes 2359304 | tf_op jit(solution)/shard_map/ppermute | solution.py:66
  44.1 370.6 %all-to-all-start = ((bf16[8,192,1920]{2,1,0:T(8,128)(2,1)}), bf16[8,192,1920]{2,1,0:T(8,128)(2,1)}, u32[]{:S(2)}, u32[]{:S(2)}) async-start(bf16[8,192,1920]{2,1,0:T(8,128)(2,1)} %pack_experts.1), calls=%async_computation | async-start | bytes 11796480 | tf_op jit(solution)/shard_map/all_to_all | solution.py:745
  113.4 106.2 %collective-permute-start.38 = (bf16[256,1536]{1,0:T(8,128)(2,1)}, bf16[256,1536]{1,0:T(8,128)(2,1)S(1)}, u32[]{:S(2)}, u32[]{:S(2)}) collective-permute-start(bf16[256,1536]{1,0:T(8,128)(2,1)} %collective-permute-done.23), channel_id=1, source_target_pairs={{0,8},{1,9},{2,10},{3,11},{4,12},{5,13},{6,14},{7,15},{8,24},{9,25... | collective-permute-start | bytes 2359304 | tf_op jit(solution)/shard_map/ppermute | solution.py:66
  116.5 103.6 %collective-permute-start.12 = (bf16[256,1536]{1,0:T(8,128)(2,1)}, bf16[256,1536]{1,0:T(8,128)(2,1)S(1)}, u32[]{:S(2)}, u32[]{:S(2)}) collective-permute-start(bf16[256,1536]{1,0:T(8,128)(2,1)} %collective-permute-done.10), channel_id=1, source_target_pairs={{0,2},{1,3},{2,0},{3,1},{4,5},{5,4},{6,7},{7,6},{8,10},{9,11},{10,... | collective-permute-start | bytes 2359304 | tf_op jit(solution)/shard_map/ppermute | solution.py:66
  130.5 92.1 %collective-permute-start.3 = (bf16[256,1536]{1,0:T(8,128)(2,1)S(1)}, bf16[256,1536]{1,0:T(8,128)(2,1)S(1)}, u32[]{:S(2)}, u32[]{:S(2)}) collective-permute-start(bf16[256,1536]{1,0:T(8,128)(2,1)S(1)} %get-tuple-element.160), channel_id=1, source_target_pairs={{0,2},{1,3},{2,0},{3,1},{4,5},{5,4},{6,7},{7,6},{8,10},{9,11},{10,... | collective-permute-start | bytes 2359304 | tf_op jit(solution)/shard_map/ppermute | solution.py:66
  139.9 83.3 %collective-permute-start.5 = (bf16[256,1536]{1,0:T(8,128)(2,1)S(1)}, bf16[256,1536]{1,0:T(8,128)(2,1)S(1)}, u32[]{:S(2)}, u32[]{:S(2)}) collective-permute-start(bf16[256,1536]{1,0:T(8,128)(2,1)S(1)} %fusion.27), channel_id=1, source_target_pairs={{0,1},{1,0},{2,3},{3,2},{4,6},{5,7},{6,4},{7,5},{8,9},{9,8},{10,11... | collective-permute-start | bytes 2359304 | tf_op jit(solution)/shard_map/ppermute | solution.py:66
  140.2 85.1 %collective-permute-start.25 = (bf16[256,1536]{1,0:T(8,128)(2,1)}, bf16[256,1536]{1,0:T(8,128)(2,1)S(1)}, u32[]{:S(2)}, u32[]{:S(2)}) collective-permute-start(bf16[256,1536]{1,0:T(8,128)(2,1)} %collective-permute-done.23), channel_id=1, source_target_pairs={{0,2},{1,3},{2,0},{3,1},{4,5},{5,4},{6,7},{7,6},{8,10},{9,11},{10,... | collective-permute-start | bytes 2359304 | tf_op jit(solution)/shard_map/ppermute | solution.py:66
  225.4 90.6 %collective-permute-start.13 = (bf16[4,256,1536]{2,1,0:T(8,128)(2,1)S(1)}, bf16[4,256,1536]{2,1,0:T(8,128)(2,1)S(1)}, u32[]{:S(2)}, u32[]{:S(2)}) collective-permute-start(bf16[4,256,1536]{2,1,0:T(8,128)(2,1)S(1)} %pad_maximum_fusion.2.ya_ref), channel_id=1, source_target_pairs={{0,4},{1,5},{2,6},{3,7},{4,0},{5,1},{6,2},{7,3},{8,12},{9,13},{10,... | collective-permute-start | bytes 9437192 | tf_op jit(solution)/shard_map/ppermute | solution.py:66
  316.0 98.2 %collective-permute-start.27 = (bf16[4,256,1536]{2,1,0:T(8,128)(2,1)S(1)}, bf16[4,256,1536]{2,1,0:T(8,128)(2,1)}, u32[]{:S(2)}, u32[]{:S(2)}) collective-permute-start(bf16[4,256,1536]{2,1,0:T(8,128)(2,1)S(1)} %pad_maximum_fusion.4.ya_ref), channel_id=1, source_target_pairs={{0,4},{1,5},{2,6},{3,7},{4,0},{5,1},{6,2},{7,3},{8,12},{9,13},{10,... | collective-permute-start | bytes 9437192 | tf_op jit(solution)/shard_map/ppermute | solution.py:66
  328.4 86.1 %collective-permute-start.9 = (bf16[4,256,1536]{2,1,0:T(8,128)(2,1)}, bf16[4,256,1536]{2,1,0:T(8,128)(2,1)}, u32[]{:S(2)}, u32[]{:S(2)}) collective-permute-start(bf16[4,256,1536]{2,1,0:T(8,128)(2,1)} %pad_maximum_fusion.1.xa_ref), channel_id=1, source_target_pairs={{0,4},{1,5},{2,6},{3,7},{4,0},{5,1},{6,2},{7,3},{8,12},{9,13},{10,... | collective-permute-start | bytes 9437192 | tf_op jit(solution)/shard_map/ppermute | solution.py:66
  355.8 88.3 %collective-permute-start.22 = (bf16[4,256,1536]{2,1,0:T(8,128)(2,1)}, bf16[4,256,1536]{2,1,0:T(8,128)(2,1)}, u32[]{:S(2)}, u32[]{:S(2)}) collective-permute-start(bf16[4,256,1536]{2,1,0:T(8,128)(2,1)} %pad_maximum_fusion.3.xa_ref), channel_id=1, source_target_pairs={{0,4},{1,5},{2,6},{3,7},{4,0},{5,1},{6,2},{7,3},{8,12},{9,13},{10,... | collective-permute-start | bytes 9437192 | tf_op jit(solution)/shard_map/ppermute | solution.py:66
  379.7 94.7 %collective-permute-start.42 = (bf16[4,256,1536]{2,1,0:T(8,128)(2,1)}, bf16[4,256,1536]{2,1,0:T(8,128)(2,1)}, u32[]{:S(2)}, u32[]{:S(2)}) collective-permute-start(bf16[4,256,1536]{2,1,0:T(8,128)(2,1)} %pad_maximum_fusion.6.ya_ref), channel_id=1, source_target_pairs={{0,4},{1,5},{2,6},{3,7},{4,0},{5,1},{6,2},{7,3},{8,12},{9,13},{10,... | collective-permute-start | bytes 9437192 | tf_op jit(solution)/shard_map/ppermute | solution.py:66
  388.1 86.5 %collective-permute-start.37 = (bf16[4,256,1536]{2,1,0:T(8,128)(2,1)}, bf16[4,256,1536]{2,1,0:T(8,128)(2,1)}, u32[]{:S(2)}, u32[]{:S(2)}) collective-permute-start(bf16[4,256,1536]{2,1,0:T(8,128)(2,1)} %pad_maximum_fusion.5.xa_ref), channel_id=1, source_target_pairs={{0,4},{1,5},{2,6},{3,7},{4,0},{5,1},{6,2},{7,3},{8,12},{9,13},{10,... | collective-permute-start | bytes 9437192 | tf_op jit(solution)/shard_map/ppermute | solution.py:66
  414.1 90.3 %collective-permute-start.57 = (bf16[4,256,1536]{2,1,0:T(8,128)(2,1)}, bf16[4,256,1536]{2,1,0:T(8,128)(2,1)S(1)}, u32[]{:S(2)}, u32[]{:S(2)}) collective-permute-start(bf16[4,256,1536]{2,1,0:T(8,128)(2,1)} %pad_maximum_fusion.8.ya_ref), channel_id=1, source_target_pairs={{0,4},{1,5},{2,6},{3,7},{4,0},{5,1},{6,2},{7,3},{8,12},{9,13},{10,... | collective-permute-start | bytes 9437192 | tf_op jit(solution)/shard_map/ppermute | solution.py:66
  414.5 90.2 %collective-permute-start.52 = (bf16[4,256,1536]{2,1,0:T(8,128)(2,1)}, bf16[4,256,1536]{2,1,0:T(8,128)(2,1)}, u32[]{:S(2)}, u32[]{:S(2)}) collective-permute-start(bf16[4,256,1536]{2,1,0:T(8,128)(2,1)} %pad_maximum_fusion.7.xa_ref), channel_id=1, source_target_pairs={{0,4},{1,5},{2,6},{3,7},{4,0},{5,1},{6,2},{7,3},{8,12},{9,13},{10,... | collective-permute-start | bytes 9437192 | tf_op jit(solution)/shard_map/ppermute | solution.py:66
  444.1 308.2 %collective-permute-start.14 = (bf16[4,256,1536]{2,1,0:T(8,128)(2,1)}, bf16[4,256,1536]{2,1,0:T(8,128)(2,1)}, u32[]{:S(2)}, u32[]{:S(2)}) collective-permute-start(bf16[4,256,1536]{2,1,0:T(8,128)(2,1)} %get-tuple-element.55), channel_id=1, source_target_pairs={{0,4},{1,5},{2,6},{3,7},{4,0},{5,1},{6,2},{7,3},{8,12},{9,13},{10,... | collective-permute-start | bytes 9437192 | tf_op jit(solution)/shard_map/ppermute | solution.py:66
  474.3 106.2 %collective-permute-start.63 = (bf16[4,256,1664]{2,1,0:T(8,128)(2,1)}, bf16[4,256,1664]{2,1,0:T(8,128)(2,1)}, u32[]{:S(2)}, u32[]{:S(2)}) collective-permute-start(bf16[4,256,1664]{2,1,0:T(8,128)(2,1)} %get-tuple-element.75), channel_id=1, source_target_pairs={{0,4},{1,5},{2,6},{3,7},{4,0},{5,1},{6,2},{7,3},{8,12},{9,13},{10,... | collective-permute-start | bytes 10223624 | tf_op jit(solution)/shard_map/ppermute | solution.py:66
  474.6 158.7 %collective-permute-start.28 = (bf16[4,256,1536]{2,1,0:T(8,128)(2,1)}, bf16[4,256,1536]{2,1,0:T(8,128)(2,1)}, u32[]{:S(2)}, u32[]{:S(2)}) collective-permute-start(bf16[4,256,1536]{2,1,0:T(8,128)(2,1)} %get-tuple-element.61), channel_id=1, source_target_pairs={{0,4},{1,5},{2,6},{3,7},{4,0},{5,1},{6,2},{7,3},{8,12},{9,13},{10,... | collective-permute-start | bytes 9437192 | tf_op jit(solution)/shard_map/ppermute | solution.py:66
  504.5 79.5 %collective-permute-start.67 = (bf16[4,256,1664]{2,1,0:T(8,128)(2,1)}, bf16[4,256,1664]{2,1,0:T(8,128)(2,1)}, u32[]{:S(2)}, u32[]{:S(2)}) collective-permute-start(bf16[4,256,1664]{2,1,0:T(8,128)(2,1)} %get-tuple-element.77), channel_id=1, source_target_pairs={{0,4},{1,5},{2,6},{3,7},{4,0},{5,1},{6,2},{7,3},{8,12},{9,13},{10,... | collective-permute-start | bytes 10223624 | tf_op jit(solution)/shard_map/ppermute | solution.py:66
  504.7 84.7 %collective-permute-start.72 = (bf16[4,256,1664]{2,1,0:T(8,128)(2,1)}, bf16[4,256,1664]{2,1,0:T(8,128)(2,1)}, u32[]{:S(2)}, u32[]{:S(2)}) collective-permute-start(bf16[4,256,1664]{2,1,0:T(8,128)(2,1)} %get-tuple-element.79), channel_id=1, source_target_pairs={{0,4},{1,5},{2,6},{3,7},{4,0},{5,1},{6,2},{7,3},{8,12},{9,13},{10,... | collective-permute-start | bytes 10223624 | tf_op jit(solution)/shard_map/ppermute | solution.py:66
  575.4 408.3 %all-to-all-start.1 = ((bf16[8,192,1920]{2,1,0:T(8,128)(2,1)}), bf16[8,192,1920]{2,1,0:T(8,128)(2,1)}, u32[]{:S(2)}, u32[]{:S(2)}) async-start(bf16[8,192,1920]{2,1,0:T(8,128)(2,1)} %bitcast.246), calls=%async_computation.2 | async-start | bytes 11796480 | tf_op jit(solution)/shard_map/all_to_all | solution.py:767
  580.3 418.0 %reduce-scatter.2.cloned.1.call-start = ((), (), s32[]{:S(2)}) async-start(), calls=%async_computation.5 | async-start | bytes 3538944 | tf_op jit(solution)/shard_map/reduce_scatter | solution.py:781
  633.3 95.8 %collective-permute-start.71 = (bf16[256,1664]{1,0:T(8,128)(2,1)S(1)}, bf16[256,1664]{1,0:T(8,128)(2,1)S(1)}, u32[]{:S(2)}, u32[]{:S(2)}) collective-permute-start(bf16[256,1664]{1,0:T(8,128)(2,1)S(1)} %add_convert_fusion.12), channel_id=1, source_target_pairs={{0,8},{1,9},{2,10},{3,11},{4,12},{5,13},{6,14},{7,15},{8,24},{9,25... | collective-permute-start | bytes 2555912 | tf_op jit(solution)/shard_map/ppermute | solution.py:66
  659.9 70.2 %collective-permute-start.65 = (bf16[256,1664]{1,0:T(8,128)(2,1)S(1)}, bf16[256,1664]{1,0:T(8,128)(2,1)S(1)}, u32[]{:S(2)}, u32[]{:S(2)}) collective-permute-start(bf16[256,1664]{1,0:T(8,128)(2,1)S(1)} %get-tuple-element.149), channel_id=1, source_target_pairs={{0,2},{1,3},{2,0},{3,1},{4,5},{5,4},{6,7},{7,6},{8,10},{9,11},{10,... | collective-permute-start | bytes 2555912 | tf_op jit(solution)/shard_map/ppermute | solution.py:66
  660.7 123.6 %collective-permute-start.43 = (bf16[4,256,1536]{2,1,0:T(8,128)(2,1)}, bf16[4,256,1536]{2,1,0:T(8,128)(2,1)}, u32[]{:S(2)}, u32[]{:S(2)}) collective-permute-start(bf16[4,256,1536]{2,1,0:T(8,128)(2,1)} %get-tuple-element.67), channel_id=1, source_target_pairs={{0,4},{1,5},{2,6},{3,7},{4,0},{5,1},{6,2},{7,3},{8,12},{9,13},{10,... | collective-permute-start | bytes 9437192 | tf_op jit(solution)/shard_map/ppermute | solution.py:66
  660.8 70.9 %collective-permute-start.78 = (bf16[256,1664]{1,0:T(8,128)(2,1)S(1)}, bf16[256,1664]{1,0:T(8,128)(2,1)S(1)}, u32[]{:S(2)}, u32[]{:S(2)}) collective-permute-start(bf16[256,1664]{1,0:T(8,128)(2,1)S(1)} %get-tuple-element.142), channel_id=1, source_target_pairs={{0,2},{1,3},{2,0},{3,1},{4,5},{5,4},{6,7},{7,6},{8,10},{9,11},{10,... | collective-permute-start | bytes 2555912 | tf_op jit(solution)/shard_map/ppermute | solution.py:66
  755.1 99.4 %collective-permute-start.58 = (bf16[4,256,1536]{2,1,0:T(8,128)(2,1)}, bf16[4,256,1536]{2,1,0:T(8,128)(2,1)}, u32[]{:S(2)}, u32[]{:S(2)}) collective-permute-start(bf16[4,256,1536]{2,1,0:T(8,128)(2,1)} %get-tuple-element.73), channel_id=1, source_target_pairs={{0,4},{1,5},{2,6},{3,7},{4,0},{5,1},{6,2},{7,3},{8,12},{9,13},{10,... | collective-permute-start | bytes 9437192 | tf_op jit(solution)/shard_map/ppermute | solution.py:66
  852.5 210.9 %all-reduce.3.cloned.1.call-start = ((), (), s32[]{:S(2)}) async-start(), calls=%async_computation.4 | async-start | bytes 491520 | tf_op jit(solution)/shard_map/psum | solution.py:791
  860.6 70.3 %collective-permute-start.15 = (bf16[256,1536]{1,0:T(8,128)(2,1)S(1)}, bf16[256,1536]{1,0:T(8,128)(2,1)S(1)}, u32[]{:S(2)}, u32[]{:S(2)}) collective-permute-start(bf16[256,1536]{1,0:T(8,128)(2,1)S(1)} %get-tuple-element.152), channel_id=1, source_target_pairs={{0,2},{1,3},{2,0},{3,1},{4,5},{5,4},{6,7},{7,6},{8,10},{9,11},{10,... | collective-permute-start | bytes 2359304 | tf_op jit(solution)/shard_map/ppermute | solution.py:66
  918.5 60.3 %collective-permute-start.85 = (bf16[256,1536]{1,0:T(8,128)(2,1)S(1)}, bf16[256,1536]{1,0:T(8,128)(2,1)S(1)}, u32[]{:S(2)}, u32[]{:S(2)}) collective-permute-start(bf16[256,1536]{1,0:T(8,128)(2,1)S(1)} %get-tuple-element.150), channel_id=1, source_target_pairs={{0,2},{1,3},{2,0},{3,1},{4,5},{5,4},{6,7},{7,6},{8,10},{9,11},{10,... | collective-permute-start | bytes 2359304 | tf_op jit(solution)/shard_map/ppermute | solution.py:66
  (112 other events, 2877.0 us)
Sparse Core Ops, SparseCore 0:
  24.3 66.5 all-gather.1
  852.7 52.9 reduce-scatter.1
  940.4 123.0 all-reduce.2

commit v2 on v1

--- a/solution.py
+++ b/solution.py
@@ -19,9 +19,9 @@
 THETA = 10000.0
 NEG = -1e30
 SCALE = HD ** (-0.5)
-WCOLS = 2 * F + 2 * QF + F + QF
 VMEM = 60 * 1024 * 1024
 BF = jnp.bfloat16
+COST = pl.CostEstimate(flops=10**6, bytes_accessed=10**4, transcendentals=0)
 F32 = jnp.float32
 
 
@@ -61,9 +61,14 @@
             self.second = [(number(d, t), number(d, t ^ (1 if d & 1 else 2))) for d, t in devices]
             self.swap = [(number(d, t), number(d ^ 1, t)) for d, t in devices]
             self.along = [(number(d, t), number(ring[d >> 1] * 2 + (d & 1), t)) for d, t in devices]
-
-    def send(self, value, perm):
-        return lax.ppermute(value, ("dp", "tensor"), perm)
+            self.against = [(b, a) for a, b in self.along]
+            self.across = [(number(d, t), number(d ^ 6, t)) for d, t in devices]
+            self.level = [[(number(d, t), number(d ^ (2 * k), t)) for d, t in devices] for k in range(4)]
+
+    def send(self, label, value, perm, *later):
+        value = after(value, *later)
+        with jax.named_scope(label):
+            return lax.ppermute(value, ("dp", "tensor"), perm)
 
     def plane_order(self, core):
         one = jnp.where(core == 0, 1, 2)
@@ -76,26 +81,19 @@
         diff = jnp.arange(4, dtype=jnp.int32) ^ self.t
         return jnp.where(diff == one, 1, jnp.where(diff == 3 - one, 2, diff)).astype(jnp.int32)
 
-    def gather_plane(self, block):
+    def gather_plane(self, block, *later):
         if not self.fast:
             return lax.all_gather(block, "tensor", axis=0)
-        near = self.send(block, self.first)
-        other = self.send(block, self.second)
-        far = self.send(near, self.second)
-        return jnp.stack([block, near, other, far])
-
-    def scatter_plane(self, parts):
+        near = self.send("plane_near", block, self.first, *later)
+        pair = jnp.stack([block, near])
+        return jnp.concatenate([pair, self.send("plane_far", pair, self.second)])
+
+    def scatter_plane(self, parts, *later):
         if not self.fast:
             rows = parts.reshape((-1,) + parts.shape[2:])
-            return lax.psum_scatter(rows, "tensor", scatter_dimension=0, tiled=True)
-        a, b = self.scatter_plane_open(parts)
-        return add(a, b)
-
-    def scatter_plane_open(self, parts):
-        got_far = self.send(parts[3], self.second)
-        got = self.send(parts[2], self.second)
-        got_near = self.send(add(parts[1], got_far), self.first)
-        return add(parts[0], got), got_near
+            return [lax.psum_scatter(rows, "tensor", scatter_dimension=0, tiled=True)]
+        got = self.send("parts_far", parts[2:], self.second, *later)
+        return [parts[0], got[0], self.send("parts_near", add(parts[1], got[1]), self.first)]
 
     def chunks(self):
         return self.group * self.n_t // 8
@@ -103,125 +101,162 @@
     def chunk_sources(self):
         if not self.fast:
             base = (self.dp // self.group) * self.group * self.n_t
-            return [base + 8 * c + jnp.arange(8, dtype=jnp.int32) for c in range(self.chunks())]
+            own = [8 * c + jnp.arange(8, dtype=jnp.int32) for c in range(self.chunks())]
+            return [base + o for o in own]
         z, core = self.dp >> 1, self.dp & 1
         place = z ^ (z >> 1)
         out = []
         for c in range(4):
             back = (place + 4 - c) & 3
             source = back ^ (back >> 1)
-            rows = [(source * 2 + core) * 4 + t for t in self.plane_order(core)]
-            rows += [(source * 2 + 1 - core) * 4 + t for t in self.plane_order(1 - core)]
-            out.append(jnp.stack(rows).astype(jnp.int32))
+            mine, theirs = self.plane_order(core), self.plane_order(1 - core)
+            routes = [(source ^ z) * 4 + t for t in mine] + [((source ^ z) + 4) * 4 + t for t in theirs]
+            out.append(jnp.stack(routes).astype(jnp.int32))
         return out
 
     def groups(self):
         n = self.n_dp // self.group
         return [list(range(g * self.group, (g + 1) * self.group)) for g in range(n)]
 
-    def gather_all(self, block):
+    def gather_group(self, block):
+        if self.n_dp == self.group:
+            return lax.all_gather(block, ("dp", "tensor"), axis=0)
+        plane = lax.all_gather(block, "tensor", axis=0)
+        return lax.all_gather(plane, "dp", axis=0, axis_index_groups=self.groups()).reshape((-1,) + block.shape)
+
+    def scatter_group(self, pairs):
+        rows = jnp.concatenate([half for pair in pairs for half in pair])
+        rows = rows.reshape((self.group, -1) + rows.shape[2:])
+        total = lax.psum_scatter(rows, "dp", scatter_dimension=0, axis_index_groups=self.groups())
+        return [lax.psum_scatter(total, "tensor", scatter_dimension=0, tiled=True)]
+
+    def sum_all(self, value, *later):
         if not self.fast:
-            plane = lax.all_gather(block, "tensor", axis=0)
-            rows = lax.all_gather(plane, "dp", axis=0, axis_index_groups=self.groups())
-            rows = rows.reshape((-1,) + block.shape)
-            return [(rows[8 * c : 8 * c + 4], rows[8 * c + 4 : 8 * c + 8]) for c in range(self.chunks())]
-        out = []
-        for c in range(4):
-            mine = self.gather_plane(block)
-            out.append((mine, self.send(mine, self.swap)))
-            if c < 3:
-                block = self.send(block, self.along)
-        return out
-
-    def scatter_chunk(self, mine, theirs):
-        return self.scatter_plane(add(mine, self.send(theirs, self.swap)))
-
-    def scatter_all(self, pairs):
-        if not self.fast:
-            rows = jnp.concatenate([half for pair in pairs for half in pair])
-            rows = rows.reshape((self.group, -1) + rows.shape[2:])
-            total = lax.psum_scatter(rows, "dp", scatter_dimension=0, axis_index_groups=self.groups())
-            total = lax.psum_scatter(total, "tensor", scatter_dimension=0, tiled=True)
-            return total, jnp.zeros_like(total)
-        sums = [self.scatter_chunk(*pair) for pair in pairs]
-        moving = self.send(sums[1], self.along)
-        moving = self.send(add(moving, sums[2]), self.along)
-        moving = self.send(add(moving, sums[3]), self.along)
-        return sums[0], moving
+            return lax.psum(value, ("dp", "tensor"))
+        for perm in (self.swap, self.first, self.second):
+            value = value + self.send("small", value, perm)
+        value = after(value, *later)
+        for perm in self.level[1:3]:
+            value = value + self.send("small", value, perm)
+        return value
+
+
+def after(value, *earlier):
+    return lax.optimization_barrier((value,) + earlier)[0] if earlier else value
+
+
+def total_of(parts):
+    total = parts[0].astype(F32)
+    for part in parts[1:]:
+        total = total + part.astype(F32)
+    return total
 
 
 def add(a, b):
     return (a.astype(F32) + b.astype(F32)).astype(a.dtype)
 
 
-def pack_kernel(full_ref, gate_ref, up_ref, out_ref, quarter_ref, packed_ref):
-    packed_ref[0, :, : 2 * F] = full_ref[0]
-    packed_ref[0, :, 2 * F : 2 * F + QF] = gate_ref[0]
-    packed_ref[0, :, 2 * F + QF : 2 * F + 2 * QF] = up_ref[0]
-    packed_ref[0, :, 2 * F + 2 * QF : 3 * F + 2 * QF] = out_ref[0].astype(F32).T.astype(BF)
-    packed_ref[0, :, 3 * F + 2 * QF :] = quarter_ref[0].astype(F32).T.astype(BF)
-
-
-def pack_experts(expert_in, expert_out, group, n_dp):
+def pack_attention_kernel(heads, qkv_ref, out_ref, packed_ref):
+    q_wide, kv_wide = heads * GRP * HD, heads * HD
+    for h in range(heads):
+        one = qkv_ref[h]
+        packed_ref[:, h * GRP * HD : (h + 1) * GRP * HD] = one[:, : GRP * HD]
+        packed_ref[:, q_wide + h * HD : q_wide + (h + 1) * HD] = one[:, GRP * HD : (GRP + 1) * HD]
+        at = q_wide + kv_wide + h * HD
+        packed_ref[:, at : at + HD] = one[:, (GRP + 1) * HD :]
+        at = q_wide + 2 * kv_wide + h * GRP * HD
+        packed_ref[:, at : at + GRP * HD] = out_ref[h].astype(F32).T.astype(BF)
+
+
+def pack_attention(qkv_weight, out_weight):
+    heads, depth, _ = qkv_weight.shape
+    return pl.pallas_call(
+        functools.partial(pack_attention_kernel, heads),
+        out_shape=jax.ShapeDtypeStruct((depth, heads * (2 * GRP + 2) * HD), BF),
+        compiler_params=params(),
+        name="pack_attention",
+    )(qkv_weight, out_weight)
+
+
+def attention_places(links):
+    if not links.fast:
+        return jnp.arange(links.n_dp, dtype=jnp.int32)
+    z, core = links.dp >> 1, links.dp & 1
+    near = [(z ^ k) * 2 for k in range(4)]
+    return jnp.stack([n + core for n in near] + [n + 1 - core for n in near]).astype(jnp.int32)
+
+
+def pack_kernel(gate_ref, up_ref, part_ref, down_ref, packed_ref):
+    packed_ref[0, :, :QF] = gate_ref[0]
+    packed_ref[0, :, QF : 2 * QF] = up_ref[0]
+    packed_ref[0, :, 2 * QF : 3 * QF] = part_ref[0]
+    packed_ref[0, :, 3 * QF :] = down_ref[0]
+
+
+def pack_experts(expert_in, expert_out_t, group, n_dp):
     depth = expert_in.shape[1]
     of = lambda d: d % group
     return pl.pallas_call(
         pack_kernel,
         grid=(n_dp,),
         in_specs=[
-            pl.BlockSpec((1, depth, 2 * F), lambda d: (of(d), 0, 0)),
             pl.BlockSpec((1, depth, QF), lambda d: (group + of(d) // 4, 0, of(d) % 4)),
             pl.BlockSpec((1, depth, QF), lambda d: (group + of(d) // 4, 0, 4 + of(d) % 4)),
-            pl.BlockSpec((1, F, depth), lambda d: (of(d), 0, 0)),
-            pl.BlockSpec((1, QF, depth), lambda d: (group + of(d) // 4, of(d) % 4, 0)),
+            pl.BlockSpec((1, depth, QF), lambda d: (group + of(d) // 4, 0, of(d) % 4)),
+            pl.BlockSpec((1, depth, F), lambda d: (of(d), 0, 0)),
         ],
-        out_specs=pl.BlockSpec((1, depth, WCOLS), lambda d: (d, 0, 0)),
-        out_shape=jax.ShapeDtypeStruct((n_dp, depth, WCOLS), BF),
+        out_specs=pl.BlockSpec((1, depth, 3 * QF + F), lambda d: (d, 0, 0)),
+        out_shape=jax.ShapeDtypeStruct((n_dp, depth, 3 * QF + F), BF),
         compiler_params=params(),
         name="pack_experts",
-    )(expert_in, expert_in, expert_in, expert_out, expert_out)
-
-
-def unpack_kernel(group, packed_ref, in_ref, out_ref):
+    )(expert_in, expert_in, expert_out_t, expert_out_t)
+
+
+def unpack_kernel(group, full_ref, down_ref, part_ref, in_ref, out_ref):
     e = pl.program_id(0)
 
     @pl.when(e < group)
     def _():
-        in_ref[0] = packed_ref[e, :, : 2 * F].astype(F32)
-        out_ref[0] = packed_ref[e, :, 2 * F + 2 * QF : 3 * F + 2 * QF].astype(F32).T
+        in_ref[0] = full_ref[0].astype(F32)
+        out_ref[0] = down_ref[0].astype(F32)
 
     @pl.when(e >= group)
     def _():
         for q in range(4):
-            s = (e - group) * 4 + q
-            in_ref[0, :, q * QF : (q + 1) * QF] = packed_ref[s, :, 2 * F : 2 * F + QF].astype(F32)
-            in_ref[0, :, F + q * QF : F + (q + 1) * QF] = packed_ref[
-                s, :, 2 * F + QF : 2 * F + 2 * QF
-            ].astype(F32)
-            out_ref[0, q * QF : (q + 1) * QF, :] = packed_ref[s, :, 3 * F + 2 * QF :].astype(F32).T
-
-
-def unpack_experts(packed, experts, group):
-    depth = packed.shape[1]
+            part = part_ref[(e - group) * 4 + q].astype(F32)
+            in_ref[0, :, q * QF : (q + 1) * QF] = part[:, :QF]
+            in_ref[0, :, F + q * QF : F + (q + 1) * QF] = part[:, QF : 2 * QF]
+            out_ref[0, :, q * QF : (q + 1) * QF] = part[:, 2 * QF :]
+
+
+def unpack_experts(full, down, part, experts, group):
+    depth = full.shape[1]
+    first = lambda e: (jnp.minimum(e, group - 1), 0, 0)
     return pl.pallas_call(
         functools.partial(unpack_kernel, group),
         grid=(experts,),
-        in_specs=[whole(packed.shape)],
+        in_specs=[
+            pl.BlockSpec((1, depth, 2 * F), first),
+            pl.BlockSpec((1, depth, F), first),
+            whole(part.shape),
+        ],
         out_specs=(
             pl.BlockSpec((1, depth, 2 * F), lambda e: (e, 0, 0)),
-            pl.BlockSpec((1, F, depth), lambda e: (e, 0, 0)),
+            pl.BlockSpec((1, depth, F), lambda e: (e, 0, 0)),
         ),
         out_shape=(
             jax.ShapeDtypeStruct((experts, depth, 2 * F), F32),
-            jax.ShapeDtypeStruct((experts, F, depth), F32),
+            jax.ShapeDtypeStruct((experts, depth, F), F32),
         ),
         compiler_params=params(),
         name="unpack_experts",
-    )(packed)
-
-
-def expert_kernel(info_ref, xa_ref, xb_ref, ya_ref, yb_ref, routes_ref, router_ref, w_ref, *rest):
-    ma_ref, mb_ref, da_ref, db_ref, taken_ref, dz_ref, dgu_ref, hid_ref = rest[-8:]
+    )(full, down, part)
+
+
+def expert_kernel(
+    info_ref, xa_ref, xb_ref, ya_ref, yb_ref, routes_ref, router_ref, full_ref, rest_ref,
+    ma_ref, da_ref, theirs_ref, taken_ref, dz_ref, dgu_ref, hid_ref,
+):
     step = pl.program_id(0)
     first, second = info_ref[0], info_ref[1]
     expert_id = lax.broadcasted_iota(jnp.int32, (E, BLK), 0)
@@ -232,11 +267,10 @@
     row_id = lax.broadcasted_iota(jnp.int32, (8, BLK), 0)
     picks, slot_gates, taken, dz = [], ([], []), ([], []), ([], [])
     for b in range(4):
-        x_ref, y_ref = (xa_ref, ya_ref) if b < 2 else (xb_ref, yb_ref)
-        x, y = x_ref[b % 2], y_ref[b % 2]
-        place = step * 2 + b % 2 + (0 if b < 2 else 4)
-        routes = routes_ref[info_ref[2 + place]]
-        logits = dot_nt(router_ref[...], x)[:E]
+        x = (xa_ref if b < 2 else xb_ref)[b % 2].reshape(BLK, -1)
+        y = (ya_ref if b < 2 else yb_ref)[b % 2].reshape(BLK, -1)
+        routes = routes_ref[info_ref[2 + step * 2 + b % 2 + (0 if b < 2 else 4)]]
+        logits = dot_nt(router_ref[...], x)
         member = expert_id == routes[0:1]
         for k in range(1, 8):
             member = member | (expert_id == routes[k : k + 1])
@@ -274,14 +308,13 @@
     for j in range(2):
         width = F if j == 0 else QF
         in_at = 0 if j == 0 else 2 * F
-        out_at = 2 * F + 2 * QF + (0 if j == 0 else F)
         rows = jnp.concatenate(taken[j], axis=0).astype(BF)
         grads = jnp.concatenate(dz[j], axis=0).astype(BF)
         gate = jnp.concatenate(slot_gates[j], axis=0)
         taken_ref[0, j] = rows
         dz_ref[0, j] = grads
-        w_in = w_ref[:, in_at : in_at + 2 * width]
-        w_out = w_ref[:, out_at : out_at + width]
+        w_in = full_ref[...] if j == 0 else rest_ref[:, : 2 * QF]
+        w_out = rest_ref[:, 3 * QF :] if j == 0 else rest_ref[:, 2 * QF : 3 * QF]
         gate_up = dot_nn(rows, w_in)
         gate_part, up_part = gate_up[:, :width], gate_up[:, width:]
         sig = 1.0 / (1.0 + jnp.exp(-gate_part))
@@ -305,93 +338,98 @@
         extra = jnp.where(lane == e, high, 0.0) + jnp.where(lane == e + 64, dgate - high, 0.0)
         backs.append(jnp.concatenate([back, extra], axis=1))
     for b in range(4):
-        m_ref, d_ref = (ma_ref, da_ref) if b < 2 else (mb_ref, db_ref)
         at = slice(b * SLOT, (b + 1) * SLOT)
-        for values, ref in ((sends, m_ref), (backs, d_ref)):
+        for kind, values in enumerate((backs, sends)):
             stacked = jnp.concatenate([values[0][at], values[1][at]], axis=0).astype(BF)
-            ref[b % 2] = dot_tn(picks[b], stacked).astype(BF)
-
-
-def expert_chunk(chunk, chunks, info, rows, grads, routes, router_t, weights, stash):
-    width = rows[0].shape[-1]
-    steps = 2
+            summed = dot_tn(picks[b], stacked).astype(BF)
+            if b < 2:
+                (da_ref, ma_ref)[kind][b] = summed
+            else:
+                theirs_ref[kind, b - 2, :, : summed.shape[1]] = summed
+
+
+def stepped(shape):
+    return pl.BlockSpec((1,) + shape[1:], lambda s, *_: (s,) + (0,) * (len(shape) - 1))
+
+
+def expert_chunk(info, rows, routes, router_t, weights):
+    width = rows[0][0].shape[-1]
+    shape = jax.ShapeDtypeStruct
     half = pl.BlockSpec((2, BLK, width), lambda s, i: (s, 0, 0))
-    half_wide = pl.BlockSpec((2, BLK, width + 128), lambda s, i: (s, 0, 0))
+
+    def given(array, column):
+        if column is None:
+            return half
+        return pl.BlockSpec((2, 1, BLK, width), lambda s, i: (s, column, 0, 0))
+
     slots = 4 * SLOT
-    total = chunks * steps
-    shape = jax.ShapeDtypeStruct
-    stash_shapes = [
-        shape((total, 2, slots, width), BF),
-        shape((total, 2, slots, width), BF),
-        shape((total, slots, 2 * F + 2 * QF), BF),
-        shape((total, slots, F + QF), BF),
+    kept = [
+        shape((2, 2, slots, width), BF),
+        shape((2, 2, slots, width), BF),
+        shape((2, slots, 2 * F + 2 * QF), BF),
+        shape((2, slots, F + QF), BF),
     ]
-    stash_specs = [
-        pl.BlockSpec(
-            (1,) + s.shape[1:], lambda i, _, n=len(s.shape): (i + chunk * steps,) + (0,) * (n - 1)
-        )
-        for s in stash_shapes
-    ]
-    given = [] if stash is None else list(stash)
-    out = pl.pallas_call(
+    return pl.pallas_call(
         expert_kernel,
         grid_spec=pltpu.PrefetchScalarGridSpec(
             num_scalar_prefetch=1,
-            grid=(steps,),
-            in_specs=[half] * 4
-            + [whole(routes.shape), whole(router_t.shape), whole(weights.shape)]
-            + [pl.BlockSpec(memory_space=pl.ANY)] * len(given),
-            out_specs=[half, half, half_wide, half_wide] + stash_specs,
+            grid=(2,),
+            in_specs=[given(*r) for r in rows] + [whole(a.shape) for a in (routes, router_t, *weights)],
+            out_specs=[
+                half,
+                pl.BlockSpec((2, BLK, width + 128), lambda s, i: (s, 0, 0)),
+                pl.BlockSpec((2, 2, BLK, width + 128), lambda s, i: (0, s, 0, 0)),
+            ]
+            + [stepped(s.shape) for s in kept],
         ),
-        out_shape=[shape((4, BLK, width), BF)] * 2 + [shape((4, BLK, width + 128), BF)] * 2 + stash_shapes,
-        input_output_aliases={8 + k: 4 + k for k in range(len(given))},
+        out_shape=[
+            shape((4, BLK, width), BF),
+            shape((4, BLK, width + 128), BF),
+            shape((2, 4, BLK, width + 128), BF),
+        ]
+        + kept,
         compiler_params=params(),
-        cost_estimate=pl.CostEstimate(flops=12 * 10**9, bytes_accessed=40 * 10**6, transcendentals=10**6),
+        cost_estimate=pl.CostEstimate(flops=30 * 10**9, bytes_accessed=45 * 10**6, transcendentals=10**6),
         name="experts",
-    )(info, rows[0], rows[1], grads[0], grads[1], routes, router_t, weights, *given)
-    return (out[0], out[1]), (out[2], out[3]), out[4:]
-
-
-def wgrad_kernel(steps, taken_ref, dz_ref, dgu_ref, hid_ref, out_ref, acc_ref):
-    k = pl.program_id(0)
+    )(info, *[r[0] for r in rows], routes, router_t, *weights)
+
+
+def wgrad_kernel(chunks, pairs, *refs):
+    out_ref = refs[-1]
     flat = lambda v: v.reshape((-1, v.shape[-1]))
-
-    def put(at, width, value):
-        @pl.when(k == 0)
-        def _():
-            acc_ref[:, at : at + width] = value
-
-        @pl.when(k > 0)
-        def _():
-            acc_ref[:, at : at + width] += value
-
-    put(0, 2 * F, dot_tn(flat(taken_ref[:, 0]), flat(dgu_ref[:, :, : 2 * F])))
-    put(2 * F, 2 * QF, dot_tn(flat(taken_ref[:, 1]), flat(dgu_ref[:, :, 2 * F :])))
-    put(2 * F + 2 * QF, F, dot_tn(flat(dz_ref[:, 0]), flat(hid_ref[:, :, :F])))
-    put(3 * F + 2 * QF, QF, dot_tn(flat(dz_ref[:, 1]), flat(hid_ref[:, :, F:])))
-
-    @pl.when(k == steps - 1)
-    def _():
-        out_ref[...] = acc_ref[...].astype(BF)
-
-
-def expert_wgrad(stash):
-    taken, dz, dgu, hid = stash
-    at_once = 2
-    steps = taken.shape[0] // at_once
-    width = taken.shape[-1]
-    spec = lambda a: pl.BlockSpec((at_once,) + a.shape[1:], lambda k: (k,) + (0,) * (len(a.shape) - 1))
+    at = 0
+    for p in range(pairs):
+        left, right = refs[2 * p * chunks : (2 * p + 1) * chunks], refs[(2 * p + 1) * chunks : (2 * p + 2) * chunks]
+        total = dot_tn(flat(left[0][...]), flat(right[0][...]))
+        for l, r in zip(left[1:], right[1:]):
+            total = total + dot_tn(flat(l[...]), flat(r[...]))
+        out_ref[:, at : at + total.shape[1]] = total.astype(BF)
+        at += total.shape[1]
+
+
+def expert_wgrad(pairs, name):
+    width = pairs[0][0][0].shape[-1]
+    chunks = len(pairs[0][0])
+    tile = 256
+    specs, operands, columns = [], [], 0
+    for left, j, right, at, size in pairs:
+        rows = left[0].shape[2]
+        specs += [pl.BlockSpec((2, 1, rows, tile), lambda k, j=j: (0, j, 0, k))] * chunks
+        specs += [
+            pl.BlockSpec((2, rows, size), lambda k, b=at // size: (0, 0, b), pipeline_mode=pl.Buffered(1))
+        ] * chunks
+        operands += list(left) + list(right)
+        columns += size
     return pl.pallas_call(
-        functools.partial(wgrad_kernel, steps),
-        grid=(steps,),
-        in_specs=[spec(a) for a in stash],
-        out_specs=whole((width, WCOLS)),
-        out_shape=jax.ShapeDtypeStruct((width, WCOLS), BF),
-        scratch_shapes=[pltpu.VMEM((width, WCOLS), F32)],
+        functools.partial(wgrad_kernel, chunks, len(pairs)),
+        grid=(width // tile,),
+        in_specs=specs,
+        out_specs=pl.BlockSpec((tile, columns), lambda k: (k, 0)),
+        out_shape=jax.ShapeDtypeStruct((width, columns), BF),
         compiler_params=params(),
-        cost_estimate=pl.CostEstimate(flops=17 * 10**9, bytes_accessed=50 * 10**6, transcendentals=0),
-        name="expert_wgrad",
-    )(*stash)
+        cost_estimate=COST,
+        name=name,
+    )(*operands)
 
 
 def swap_halves(values):
@@ -431,8 +469,18 @@
     return [values[g * BLK : (g + 1) * BLK] for g in range(GRP)]
 
 
-def attend_kernel(heads, blocks, seqs, info_ref, n1_ref, w_ref, cos_ref, sin_ref, out_ref, qkv_ref, o_ref, lse_ref):
+def attend_kernel(heads, blocks, seqs, pieces, info_ref, n1_ref, cos_ref, sin_ref, *refs):
+    out_ref, qkv_ref, o_ref, lse_ref, w_ref = refs[pieces:]
     i = pl.program_id(0)
+
+    @pl.when(i == 0)
+    def _():
+        each = [ref.at[p] for ref in refs[:pieces] for p in range(ref.shape[0])]
+        depth = w_ref.shape[0] // len(each)
+        for k, piece in enumerate(each):
+            at = pl.multiple_of(info_ref[blocks + seqs + k] * depth, depth)
+            w_ref[pl.ds(at, depth), :] = piece[:depth]
+
     q_wide, kv_wide = heads * GRP * HD, heads * HD
     rot_wide, qkv_wide = q_wide + kv_wide, q_wide + 2 * kv_wide
     projected = dot_nn(n1_ref[0], w_ref[:, :qkv_wide])
@@ -471,28 +519,30 @@
     over_windows(i, blocks, attend)
 
 
-def attend_forward(heads, info, normed, weights, cosine, sine, seqs):
+def attend_forward(heads, info, normed, pieces, cosine, sine, seqs):
     blocks, _, width = normed.shape
     rows = blocks * BLK
     q_wide = heads * GRP * HD
     qkv_wide = q_wide + 2 * heads * HD
     shape = jax.ShapeDtypeStruct
+    weights = (width, pieces[0].shape[-1])
     return pl.pallas_call(
-        functools.partial(attend_kernel, heads, blocks, seqs),
+        functools.partial(attend_kernel, heads, blocks, seqs, len(pieces)),
         grid_spec=pltpu.PrefetchScalarGridSpec(
             num_scalar_prefetch=1,
             grid=(blocks,),
             in_specs=[
                 pl.BlockSpec((1, BLK, width), lambda i, info: (info[i], 0, 0)),
-                whole(weights.shape),
                 pl.BlockSpec((BLK, 128), lambda i, info: (i, 0)),
                 pl.BlockSpec((BLK, 128), lambda i, info: (i, 0)),
-            ],
+            ]
+            + [whole(p.shape) for p in pieces],
             out_specs=[
                 pl.BlockSpec((1, BLK, width), lambda i, info: (info[i], 0, 0)),
                 whole((rows, qkv_wide)),
                 pl.BlockSpec((BLK, q_wide), lambda i, info: (i, 0)),
                 pl.BlockSpec((BLK, 128), lambda i, info: (i, 0)),
+                whole(weights),
             ],
         ),
         out_shape=[
@@ -500,11 +550,12 @@
             shape((rows, qkv_wide), BF),
             shape((rows, q_wide), BF),
             shape((rows, 128), F32),
+            shape(weights, BF),
         ],
         compiler_params=params(),
-        cost_estimate=pl.CostEstimate(flops=5 * 10**9, bytes_accessed=12 * 10**6, transcendentals=4 * 10**6),
+        cost_estimate=COST,
         name="attend",
-    )(info, normed, weights, cosine, sine)
+    )(info, normed, cosine, sine, *pieces)
 
 
 def attend_back_kernel(
@@ -632,16 +683,16 @@
         ),
         out_shape=[shape((blocks, BLK, width), BF), shape(weights.shape, BF), shape((1, width), F32)],
         compiler_params=params(),
-        cost_estimate=pl.CostEstimate(flops=14 * 10**9, bytes_accessed=25 * 10**6, transcendentals=4 * 10**6),
+        cost_estimate=COST,
         name="attend_back",
     )(info, da, normed, weights, cosine, sine, qkv, attended, lse)
 
 
-def residual_kernel(
-    one_ref, two_ref, n2_ref, h_ref, gain_ref, router_ref, routes_ref, cot_ref, dh_ref, da_ref, dgain_ref, drouter_ref
-):
+def residual_kernel(parts, *refs):
+    part_refs = refs[:parts]
+    n2_ref, h_ref, gain_ref, router_ref, routes_ref, cot_ref, dh_ref, da_ref, dgain_ref, drouter_ref = refs[parts:]
     width = n2_ref.shape[1]
-    total = one_ref[...].astype(F32) + two_ref[...].astype(F32)
+    total = total_of([r[...] for r in part_refs])
     dn2 = total[:, :width]
     dgate = total[:, width:]
     dgate = dgate + pltpu.roll(dgate, 64, 1)
@@ -671,11 +722,11 @@
     da_ref[...] = dh.astype(BF)
 
 
-def residual_gradient(one, two, n2, h, gain, router_pad, routes, cotangent):
+def residual_gradient(parts, n2, h, gain, router_pad, routes, cotangent):
     rows, width = n2.shape
     shape = jax.ShapeDtypeStruct
     return pl.pallas_call(
-        residual_kernel,
+        functools.partial(residual_kernel, len(parts)),
         out_shape=[
             shape((rows, width), F32),
             shape((rows, width), BF),
@@ -683,9 +734,9 @@
             shape((E, width), F32),
         ],
         compiler_params=params(),
-        cost_estimate=pl.CostEstimate(flops=10**9, bytes_accessed=8 * 10**6, transcendentals=10**5),
+        cost_estimate=COST,
         name="residual_gradient",
-    )(one, two, n2, h, gain, router_pad, routes, cotangent)
+    )(*parts, n2, h, gain, router_pad, routes, cotangent)
 
 
 def rms_unit(values):
@@ -710,86 +761,214 @@
     own_rows, width = tokens.shape
     group_rows = routes.shape[0]
     heads = qkv_weight.shape[0]
-    experts = expert_in.shape[0]
+    experts, depth, _ = expert_in.shape
     group = experts * 4 // 5
     n_dp = lax.axis_size("dp")
     links = Links(group)
+    fast = links.fast
+    send, first, second = links.send, (links.first if fast else None), (links.second if fast else None)
     rank = links.dp % group
     own_expert = links.t * experts + rank
     part_expert = links.t * experts + group + rank // 4
     seqs = lengths.shape[1]
     blocks = group_rows // own_rows
     inputs = tokens.astype(F32)
-
-    grouped = jnp.transpose(qkv_weight, (1, 0, 2))
-    depth = grouped.shape[0]
-    attention_shard = jnp.concatenate(
-        [
-            grouped[:, :, : GRP * HD].reshape(depth, -1),
-            grouped[:, :, GRP * HD : (GRP + 1) * HD].reshape(depth, -1),
-            grouped[:, :, (GRP + 1) * HD :].reshape(depth, -1),
-            jnp.transpose(out_weight, (2, 0, 1)).reshape(depth, -1),
-        ],
-        axis=1,
-    )
-    attention_weights = lax.all_gather(attention_shard, "dp", axis=0, tiled=True)
-    routes_own = jnp.transpose(routes).reshape(8, blocks, own_rows)
-    routes_all = lax.all_gather(jnp.transpose(routes_own, (1, 0, 2)), "dp", axis=0, tiled=True)
+    expert_out_t = jnp.swapaxes(expert_out, 1, 2)
     starts = jnp.cumsum(lengths[0]) - lengths[0]
     cosine, sine = rope_tables(starts, group_rows)
-    info = jnp.concatenate([links.plane_places(), starts.astype(jnp.int32)])
-
-    normed_first = (rms_unit(inputs) * norm_gains[0]).astype(BF)
-    normed_group = links.gather_plane(normed_first)
-    packed = pack_experts(expert_in, expert_out, group, n_dp)
-    weights = lax.all_to_all(packed, "dp", 0, 0).reshape(width, WCOLS)
-    grads = links.gather_all(cotangent)
-
-    mixed, qkv, attended, lse = attend_forward(heads, info, normed_group, attention_weights, cosine, sine, seqs)
-    residual = inputs + links.scatter_plane(mixed).astype(F32)
-    normed_second = (rms_unit(residual) * norm_gains[1]).astype(BF)
-
-    rows = links.gather_all(normed_second)
+    info = jnp.concatenate([links.plane_places(), starts.astype(jnp.int32), attention_places(links)])
     router_t = jnp.transpose(router_weight)
     router_pad = jnp.pad(router_t, ((0, 128 - E), (0, 0)))
     mine = jnp.stack([own_expert, part_expert]).astype(jnp.int32)
-    stash = None
-    outs, backs = [], []
-    for c, sources in enumerate(links.chunk_sources()):
-        chunk_info = jnp.concatenate([mine, sources])
-        out, back, stash = expert_chunk(
-            c, links.chunks(), chunk_info, rows[c], grads[c], routes_all, router_t, weights, stash
-        )
-        outs.append(out)
-        backs.append(back)
-    one, two = links.scatter_all(backs)
-    weights_grad = expert_wgrad(stash)
-    returned = lax.all_to_all(weights_grad.reshape(n_dp, depth, WCOLS), "dp", 0, 0)
-    if n_dp != group:
-        returned = jnp.sum(returned.reshape(-1, group, depth, WCOLS).astype(F32), axis=0).astype(BF)
-    expert_in_grad, expert_out_grad = unpack_experts(returned, experts, group)
+    sources = links.chunk_sources()
+    chunks = links.chunks()
+    to_all = lambda a: lax.all_to_all(a, "dp", 0, 0)
+
+    shard = pack_attention(qkv_weight, out_weight)
+    normed_first = (rms_unit(inputs) * norm_gains[0]).astype(BF)
+    packed = pack_experts(expert_in, expert_out_t, group, n_dp)
+    own_in = expert_in[:group] if n_dp == group else jnp.concatenate([expert_in[:group]] * (n_dp // group))
+    routes_t = jnp.transpose(routes)
+    by_block = lambda r: jnp.transpose(r.reshape(-1, 8, blocks, own_rows), (0, 2, 1, 3)).reshape(-1, 8, own_rows)
+    if fast:
+        y, swap = cotangent, links.swap
+        routes_rows = jnp.pad(routes_t.astype(BF), ((0, 8), (0, 0)))
+        shard = jnp.concatenate([shard, routes_rows])
+        pieces = [send("pieces", shard, links.level[k]) for k in range(1, 4)]
+        near = send("near", normed_first, first, shard)
+        pair = jnp.stack([normed_first, near])
+        far = send("far", pair, second)
+
+        pieces_mine = jnp.stack([shard] + pieces)
+        pieces_theirs = send("pieces_theirs", pieces_mine, swap)
+        y_near0 = send("y_near0", y, first, far)
+        rest = to_all(after(packed, pieces_mine))
+        normed_group = jnp.concatenate([pair, far])
+        y_pair0 = jnp.stack([y, y_near0])
+        y_far0 = send("y_far0", y_pair0, second)
+        attend_pieces = [pieces_mine, pieces_theirs]
+        routes_all = jnp.concatenate([pieces_mine[:, depth : depth + 8], pieces_theirs[:, depth : depth + 8]])
+        routes_all = by_block(routes_all).astype(jnp.int32)
+        before = (rest, y_far0)
+    else:
+        normed_group = links.gather_plane(normed_first)
+        attend_pieces = [lax.all_gather(shard, "dp", axis=0)]
+        rest = to_all(packed)
+        routes_all = by_block(lax.all_gather(routes_t, "dp", axis=0))
+        before = (packed,)
+    mixed, qkv, attended, lse, attention_weights = attend_forward(
+        heads, after(info, *before), normed_group, attend_pieces, cosine, sine, seqs
+    )
+    if fast:
+        full = to_all(after(own_in, rest))
+        h_far = send("h_far", mixed[2:], second)
+        h_near = send("h_near", add(mixed[1], h_far[1]), first)
+        y_mine0 = jnp.concatenate([y_pair0, after(y_far0, mixed)])
+        y_theirs0 = send("y_theirs0", y_mine0, swap)
+        residual = inputs + total_of([mixed[0], h_far[0], h_near])
+    else:
+        full = to_all(own_in)
+        residual = inputs + total_of(links.scatter_plane(mixed))
+    weights = [w.reshape(width, -1) for w in (full, rest)]
+    normed_second = (rms_unit(residual) * norm_gains[1]).astype(BF)
+    x = after(normed_second, full)
+
+    def run(c, rows, *later):
+        chunk_info = after(jnp.concatenate([mine, sources[c]]), *later)
+        return expert_chunk(chunk_info, rows, routes_all, router_t, weights)
+
+    if fast:
+        near0 = send("near0", x, first)
+        both = jnp.stack([x, y])
+        both1 = send("both1", both, links.along)
+        both3 = send("both3", both, links.against)
+        pair0 = jnp.stack([x, near0])
+        far0 = send("far0", pair0, second)
+        mine0 = jnp.concatenate([pair0, far0])
+        theirs0 = send("theirs0", mine0, swap, y_theirs0)
+        near1 = send("near1", both1, first)
+        both2 = send("both2", both1, links.along)
+        pair1 = jnp.stack([both1, near1])
+        far1 = send("far1", pair1, second)
+        done0 = run(0, [(mine0, None), (theirs0, None), (y_mine0, None), (y_theirs0, None)], pair1, both3)
+        past = done0[-1]
+        near3 = send("near3", both3, first, pair1)
+        mine1 = jnp.concatenate([after(pair1, past), after(far1, past)])
+        theirs1 = send("theirs1", mine1, swap, both2)
+        swap0 = send("swap0", done0[2], swap, mine1)
+        pair3 = jnp.stack([after(both3, past), after(near3, past)])
+        far3 = send("far3", pair3, second)
+        near2 = send("near2", both2, first, pair3)
+        done1 = run(1, [(mine1, 0), (theirs1, 0), (mine1, 1), (theirs1, 1)], pair3, both2)
+        past = done1[-1]
+        mine3 = jnp.concatenate([after(pair3, past), after(far3, past)])
+        pair2 = jnp.stack([after(both2, past), after(near2, past)])
+        theirs3 = send("theirs3", mine3, swap)
+        far2 = send("far2", pair2, second)
+        swap1 = send("swap1", done1[2], swap, mine3)
+        d0 = add(after(done0[1], pair2), after(swap0, past)[0])
+        done3 = run(3, [(mine3, 0), (theirs3, 0), (mine3, 1), (theirs3, 1)], pair2, d0)
+        past = done3[-1]
+        mine2 = jnp.concatenate([after(pair2, past), after(far2, past)])
+        theirs2 = send("theirs2", mine2, swap)
+        swap3 = send("swap3", done3[2], swap, mine2)
+        d1 = add(after(done1[1], mine2), after(swap1, past)[0])
+        d_far1 = send("d_far1", d1[2:], second)
+        d3 = add(after(done3[1], d1), swap3[0])
+        d_far3 = send("d_far3", d3[2:], second)
+        done2 = run(2, [(mine2, 0), (theirs2, 0), (mine2, 1), (theirs2, 1)], d3)
+        past = done2[-1]
+        done = [done0, done1, done2, done3]
+    else:
+        x_all, y_all = links.gather_group(x), links.gather_group(cotangent)
+        halves = lambda a, c: [(a[8 * c : 8 * c + 4], None), (a[8 * c + 4 : 8 * c + 8], None)]
+        done = [run(c, halves(x_all, c) + halves(y_all, c)) for c in range(chunks)]
+        parts = links.scatter_group([(d[1], d[2][0]) for d in done])
+    taken, dz, dgu, hid = ([d[k] for d in done] for k in range(3, 7))
+    if fast:
+        swap2 = send("swap2", done2[2], swap, d_far1, d_far3)
+        swaps = [swap0, swap1, swap2, swap3]
+        n1, n3 = add(d1[1], d_far1[1]), add(d3[1], after(d_far3, past)[1])
+        d_near3 = send("d_near3", n3, first)
+        d_near1 = send("d_near1", n1, first, past)
+        hid[0] = after(hid[0], n1, n3)
+    part_grad = expert_wgrad([(taken, 1, dgu, 2 * F, 2 * QF), (dz, 1, hid, F, QF)], "wgrad_part")
+
+    def give_back(grad, *later):
+        got = to_all(after(grad.reshape(n_dp, depth, -1), *later))
+        if n_dp == group:
+            return got
+        return jnp.sum(got.reshape((-1, group) + got.shape[1:]).astype(F32), axis=0).astype(BF)
+
+    got_part = give_back(part_grad)
+    if fast:
+        d2 = add(after(done2[1], part_grad), swap2[0])
+        d_far2 = send("d_far2", d2[2:], second)
+        home3 = send("home3", total_of([d3[0], d_far3[0], d_near3]).astype(BF), links.along, part_grad)
+        taken[0] = after(taken[0], d2)
+    full_grad = expert_wgrad([(taken, 0, dgu, 0, 2 * F)], "wgrad_full")
+    if fast:
+        d_near2 = send("d_near2", add(d2[1], d_far2[1]), first, full_grad)
+        d_far0 = send("d_far0", d0[2:], second, d_far2)
+        home2 = send("home2", total_of([d2[0], d_far2[0], d_near2]).astype(BF), links.against)
+        m2 = add(after(done[2][0], d_near2), swaps[2][1, ..., :width])
+        m_far2 = send("m_far2", m2[2:], second, d_far0)
+        h1 = total_of([d1[0], d_far1[0], d_near1, home2]).astype(BF)
+        home1 = send("home1", h1, links.against, got_part)
+        d_near0 = send("d_near0", add(d0[1], d_far0[1]), first, d_near2)
+        m1 = add(after(done[1][0], h1), swaps[1][1, ..., :width])
+        m_far1 = send("m_far1", m1[2:], second, h1)
+        dz[0] = after(dz[0], m1, h1)
+    down_grad = expert_wgrad([(dz, 0, hid, 0, F)], "wgrad_down")
+    if fast:
+        m_near2 = send("m_near2", add(m2[1], m_far2[1]), first, down_grad)
+        parts = [d0[0], d_far0[0], d_near0, home3, after(home1, m_near2)]
+        before = (home1,)
+    else:
+        before = ()
+    got_down = give_back(down_grad, got_part, *before)
+    got_full = give_back(full_grad, got_down)
 
     routes_mine = lax.dynamic_slice_in_dim(routes, links.t * own_rows, own_rows, 0)
     residual_grad, branch_grad, second_gain, router_part = residual_gradient(
-        one, two, normed_second, residual, norm_gains[1:2], router_pad, routes_mine, cotangent
+        parts, normed_second, residual, norm_gains[1:2], router_pad, routes_mine, cotangent
     )
     branch_group = links.gather_plane(branch_grad)
+    if fast:
+        m_near1 = send("m_near1", add(m1[1], m_far1[1]), first, branch_group)
+        m_home2 = send("m_home2", total_of([m2[0], m_far2[0], m_near2]).astype(BF), links.against, branch_grad)
+        m3 = add(after(done[3][0], branch_grad), swaps[3][1, ..., :width])
+        m_far3 = send("m_far3", m3[2:], second, branch_group)
+        before = (m3, got_down)
+    else:
+        before = ()
     dn1, attention_grad, first_gain = attend_backward(
-        heads, info, branch_group, normed_group, attention_weights, cosine, sine, qkv, attended, lse, seqs
+        heads, after(info, *before), branch_group, normed_group, attention_weights, cosine, sine, qkv, attended, lse, seqs
     )
-    first_grad = links.scatter_plane(dn1).astype(F32)
     attention_mine = lax.psum_scatter(attention_grad, "dp", scatter_dimension=0, tiled=True).astype(F32)
-
-    mix_one, mix_two = links.scatter_all(outs)
-    layer_output = (residual + mix_one.astype(F32) + mix_two.astype(F32)).astype(BF)
+    n_parts = links.scatter_plane(dn1, *([m_home2, m_far3, m_near1] if fast else []))
+    first_grad = total_of(n_parts)
+    small = jnp.concatenate([router_part, first_gain / norm_gains[0:1], second_gain])
+    small = jnp.pad(small, ((0, 6), (0, 0)))
+    if fast:
+        m0 = add(after(done[0][0], branch_grad), swaps[0][1, ..., :width])
+        m_far0 = send("m_far0", m0[2:], second, n_parts[1])
+        m_near3 = send("m_near3", add(m3[1], m_far3[1]), first, n_parts[1], got_full)
+        m_near0 = send("m_near0", add(m0[1], m_far0[1]), first)
+        m_home3 = send("m_home3", total_of([m3[0], m_far3[0], m_near3]).astype(BF), links.along)
+        m_home1 = send("m_home1", total_of([m1[0], m_far1[0], m_near1, m_home2]).astype(BF), links.against, dn1)
+        out = [m0[0], m_far0[0], m_near0, m_home1, m_home3]
+        before = (m_near0, m_near3)
+    else:
+        out = links.scatter_group([(d[0], d[2][1, ..., :width]) for d in done])
+    expert_in_grad, expert_out_grad = unpack_experts(after(got_full, *before), got_down, got_part, experts, group)
+    small = links.sum_all(small, *before)
+    layer_output = (residual + total_of(out)).astype(BF)
 
     unit = rms_unit(inputs)
     inner = first_grad * norm_gains[0]
     inverse = lax.rsqrt(jnp.mean(inputs * inputs, axis=-1, keepdims=True) + EPS)
     input_grad = residual_grad + inverse * (inner - unit * jnp.mean(inner * unit, axis=-1, keepdims=True))
-
-    router_sum = lax.psum(router_part, ("dp", "tensor"))
-    gains = lax.psum(jnp.concatenate([first_gain / norm_gains[0:1], second_gain]), ("dp", "tensor"))
 
     q_wide, kv_wide = heads * GRP * HD, heads * HD
     split = lambda at, size: attention_mine[:, at : at + size].reshape(depth, heads, -1)
@@ -803,12 +982,12 @@
     return (
         layer_output,
         input_grad,
-        gains,
-        jnp.transpose(router_sum),
+        small[E : E + 2],
+        jnp.transpose(small[:E]),
         qkv_grad,
         out_weight_grad,
         expert_in_grad,
-        expert_out_grad,
+        jnp.swapaxes(expert_out_grad, 1, 2),
     )
 
 

time: 1080 us -> 884 us (0.82)
  waiting for transfers between devices: 557 us -> 356 us
  blocking collectives: 53.9 us -> 0 us
  other arithmetic: 77 us -> 110 us
  local copies, waits for them, and re-layouts: 43 us -> 59.2 us
  starting transfers between devices: 91.3 us -> 107 us
    ppermute x88 -> x61, waiting for transfers between devices: 473 us -> 327 us  [send(): return lax.ppermute(value, ('dp', 'tensor'), perm)]
    psum x1 -> x0, waiting for transfers between devices: 60.5 us -> none  [shards(): router_sum = lax.psum(router_part, ('dp', 'tensor'))]
    psum x1 -> x0, blocking collectives: 38.5 us -> none  [shards(): lax.psum(jnp.concatenate([first_gain / norm_gains[0:1], second_gain]), ('...]
    all_to_all x2 -> x5, waiting for transfers between devices: 0.01 us -> 29.2 us  [shards(): to_all = lambda a: lax.all_to_all(a, 'dp', 0, 0)]
    all_gather x1 -> x0, waiting for transfers between devices: 23.4 us -> none  [shards(): lax.all_gather(attention_shard, 'dp', axis=0, tiled=True)]
    all_to_all x2 -> x5, starting transfers between devices: 10 us -> 28.6 us  [shards(): to_all = lambda a: lax.all_to_all(a, 'dp', 0, 0)]
    convert_element_type x1 -> x9, other arithmetic: 2.5 us -> 20.8 us  [the longest x1 3.08 us: shards(): layer_output = (residual + total_of(out)).astype(BF)]
    all_gather x1 -> x0, blocking collectives: 15.4 us -> none  [shards(): lax.all_gather(jnp.transpose(routes_own, (1, 0, 2)), 'dp', axis=0, tiled=...]
  transfers between devices with their start and end apart: 93 -> 67, of which waited for: 36 -> 38; matrix products, arithmetic and copies ran while one was open for 9% -> 17% of each run, Pallas kernels for 22% -> 26%
where the time goes in v2:
time: 884 us; the launch traced here: 879 us
  waiting for transfers between devices  356 us (40%)
  Pallas kernels  231 us (26%)
  other arithmetic  110 us (12%)
  starting transfers between devices  107 us (12%)
  local copies, waits for them, and re-layouts  59.2 us (7%)
  between operations  15.2 us (2%)
    ppermute x61, waiting for transfers between devices, send(): return lax.ppermute(value, ('dp', 'tensor'), perm)  327 us
    pallas_call x4, Pallas kernels, expert_chunk(): pl.pallas_call(expert_kernel, grid_spec=pltpu.PrefetchScalarGridSpec(num_...  115 us
    ppermute x61, starting transfers between devices, send(): return lax.ppermute(value, ('dp', 'tensor'), perm)  78.3 us
    convert_element_type x18, other arithmetic, add(): return (a.astype(F32) + b.astype(F32)).astype(a.dtype)  48 us
    pallas_call x3, Pallas kernels, expert_wgrad(): pl.pallas_call(functools.partial(wgrad_kernel, chunks, len(pairs)), grid=...  36.8 us
    pallas_call x1, Pallas kernels, attend_backward(): pl.pallas_call(functools.partial(attend_back_kernel, heads, blocks, seqs)...  34.1 us
    all_to_all x5, waiting for transfers between devices, shards(): to_all = lambda a: lax.all_to_all(a, 'dp', 0, 0)  29.2 us
    all_to_all x5, starting transfers between devices, shards(): to_all = lambda a: lax.all_to_all(a, 'dp', 0, 0)  28.6 us
  transfers between devices with their start and end apart: 67, of which 38 were waited for; matrix products, arithmetic and copies ran while one was open for 17% of the time, Pallas kernels for 26%

profile of v2, /device:TPU:0, one launch (start us, length us, event | category | flops | bytes accessed | tf_op | source)
XLA Modules:
  0.0 878.6 jit_solution(14073959270140065983)
XLA Ops:
  22.9 9.4 %collective-permute-done = bf16[208,1024]{1,0:T(8,128)(2,1)S(1)} collective-permute-done((bf16[208,1024]{1,0:T(8,128)(2,1)S(1)}, bf16[208,1024]{1,0:T(8,128)(2,1)S(1)}, u32[]{:S(2)}, u32[]{:S(2)}) %collective-permute-start) | collective-permute-done | bytes 426016 | tf_op jit(solution)/shard_map/pieces/ppermute | solution.py:71
  32.3 13.7 %collective-permute-done.1 = bf16[208,1024]{1,0:T(8,128)(2,1)S(1)} collective-permute-done((bf16[208,1024]{1,0:T(8,128)(2,1)S(1)}, bf16[208,1024]{1,0:T(8,128)(2,1)S(1)}, u32[]{:S(2)}, u32[]{:S(2)}) %collective-permute-start.1) | collective-permute-done | bytes 426016 | tf_op jit(solution)/shard_map/pieces/ppermute | solution.py:71
  46.3 10.8 %all-to-all-start = ((bf16[8,192,896]{2,1,0:T(8,128)(2,1)}), bf16[8,192,896]{2,1,0:T(8,128)(2,1)}, u32[]{:S(2)}, u32[]{:S(2)}) async-start(bf16[8,192,896]{2,1,0:T(8,128)(2,1)} %pack_experts.1), calls=%async_computation | async-start | bytes 5505024 | tf_op jit(solution)/shard_map/all_to_all | solution.py:785
  60.1 10.2 %collective-permute-done.3 = bf16[256,1536]{1,0:T(8,128)(2,1)S(1)} collective-permute-done((bf16[256,1536]{1,0:T(8,128)(2,1)S(1)}, bf16[256,1536]{1,0:T(8,128)(2,1)S(1)}, u32[]{:S(2)}, u32[]{:S(2)}) %collective-permute-start.3) | collective-permute-done | bytes 786464 | tf_op jit(solution)/shard_map/near/ppermute | solution.py:71
  72.0 18.9 %collective-permute-done.4 = bf16[2,256,1536]{2,1,0:T(8,128)(2,1)S(1)} collective-permute-done((bf16[2,256,1536]{2,1,0:T(8,128)(2,1)S(1)}, bf16[2,256,1536]{2,1,0:T(8,128)(2,1)S(1)}, u32[]{:S(2)}, u32[]{:S(2)}) %collective-permute-start.4) | collective-permute-done | bytes 1572896 | tf_op jit(solution)/shard_map/far/ppermute | solution.py:71
  107.0 13.3 %all-to-all-done = bf16[8,192,896]{2,1,0:T(8,128)(2,1)} async-done(((bf16[8,192,896]{2,1,0:T(8,128)(2,1)}), bf16[8,192,896]{2,1,0:T(8,128)(2,1)}, u32[]{:S(2)}, u32[]{:S(2)}) %all-to-all-start) | async-done | bytes 2752544 | tf_op jit(solution)/shard_map/all_to_all | solution.py:785
  131.6 20.3 %attend.1 = (bf16[4,256,1536]{2,1,0:T(8,128)(2,1)}, bf16[1024,640]{1,0:T(8,128)(2,1)}, bf16[1024,384]{1,0:T(8,128)(2,1)}, f32[1024,128]{1,0:T(8,128)}, bf16[1536,1024]{1,0:T(8,128)(2,1)}) custom-call(s32[16]{0:T(128)} %concatenate.65.info_ref, bf16[4,256,1536]{2,1,0:T(8,128)(2,1)} %pad_maximum_fusion.n1_ref, f32[1024,128]{1,0:T(8,128)} %get-tuple-element.243.cos_ref, ...), custom_call_target="tpu_custom_call" | custom-call | flops 1000000 | bytes 10000 | tf_op jit(solution)/shard_map/attend/pallas_call | solution.py:529
  155.2 18.9 %collective-permute-done.8 = bf16[2,256,1536]{2,1,0:T(8,128)(2,1)S(1)} collective-permute-done((bf16[2,256,1536]{2,1,0:T(8,128)(2,1)S(1)}, bf16[2,256,1536]{2,1,0:T(8,128)(2,1)S(1)}, u32[]{:S(2)}, u32[]{:S(2)}) %collective-permute-start.8) | collective-permute-done | bytes 1572896 | tf_op jit(solution)/shard_map/h_far/ppermute | solution.py:71
  188.3 8.2 all-to-all-done.1
  198.0 10.5 %collective-permute-done.13 = bf16[256,1536]{1,0:T(8,128)(2,1)S(1)} collective-permute-done((bf16[256,1536]{1,0:T(8,128)(2,1)S(1)}, bf16[256,1536]{1,0:T(8,128)(2,1)S(1)}, u32[]{:S(2)}, u32[]{:S(2)}) %collective-permute-start.13) | collective-permute-done | bytes 786464 | tf_op jit(solution)/shard_map/near0/ppermute | solution.py:71
  211.5 18.9 %collective-permute-done.14 = bf16[2,256,1536]{2,1,0:T(8,128)(2,1)S(1)} collective-permute-done((bf16[2,256,1536]{2,1,0:T(8,128)(2,1)S(1)}, bf16[2,256,1536]{2,1,0:T(8,128)(2,1)S(1)}, u32[]{:S(2)}, u32[]{:S(2)}) %collective-permute-start.14) | collective-permute-done | bytes 1572896 | tf_op jit(solution)/shard_map/far0/ppermute | solution.py:71
  232.4 15.2 %collective-permute-done.10 = bf16[2,256,1536]{2,1,0:T(8,128)(2,1)} collective-permute-done((bf16[2,256,1536]{2,1,0:T(8,128)(2,1)}, bf16[2,256,1536]{2,1,0:T(8,128)(2,1)}, u32[]{:S(2)}, u32[]{:S(2)}) %collective-permute-start.10) | collective-permute-done | bytes 1572896 | tf_op jit(solution)/shard_map/both1/ppermute | solution.py:71
  250.4 17.8 %collective-permute-done.11 = bf16[2,256,1536]{2,1,0:T(8,128)(2,1)S(1)} collective-permute-done((bf16[2,256,1536]{2,1,0:T(8,128)(2,1)}, bf16[2,256,1536]{2,1,0:T(8,128)(2,1)S(1)}, u32[]{:S(2)}, u32[]{:S(2)}) %collective-permute-start.11) | collective-permute-done | bytes 1572896 | tf_op jit(solution)/shard_map/near1/ppermute | solution.py:71
  273.8 10.8 %collective-permute-done.12 = bf16[2,256,1536]{2,1,0:T(8,128)(2,1)} collective-permute-done((bf16[2,256,1536]{2,1,0:T(8,128)(2,1)}, bf16[2,256,1536]{2,1,0:T(8,128)(2,1)}, u32[]{:S(2)}, u32[]{:S(2)}) %collective-permute-start.12) | collective-permute-done | bytes 1572896 | tf_op jit(solution)/shard_map/both3/ppermute | solution.py:71
  284.6 28.8 %experts.4 = (bf16[4,256,1536]{2,1,0:T(8,128)(2,1)}, bf16[4,256,1664]{2,1,0:T(8,128)(2,1)}, bf16[2,4,256,1664]{3,2,1,0:T(8,128)(2,1)}, bf16[2,2,352,1536]{3,2,1,...) custom-call(s32[10]{0:T(128)} %concatenate.70.info_ref, ...), custom_call_target="tpu_custom_call" | custom-call | flops 30000001024 | bytes 45000000 | tf_op jit(solution)/shard_map/experts/pallas_call | solution.py:372
  320.8 18.9 %collective-permute-done.18 = bf16[2,256,1536]{2,1,0:T(8,128)(2,1)S(1)} collective-permute-done((bf16[2,256,1536]{2,1,0:T(8,128)(2,1)}, bf16[2,256,1536]{2,1,0:T(8,128)(2,1)S(1)}, u32[]{:S(2)}, u32[]{:S(2)}) %collective-permute-start.18) | collective-permute-done | bytes 1572896 | tf_op jit(solution)/shard_map/near3/ppermute | solution.py:71
  343.8 28.4 %experts.5 = (bf16[4,256,1536]{2,1,0:T(8,128)(2,1)}, bf16[4,256,1664]{2,1,0:T(8,128)(2,1)}, bf16[2,4,256,1664]{3,2,1,0:T(8,128)(2,1)}, bf16[2,2,352,1536]{3,2,1,...) custom-call(s32[10]{0:T(128)} %concatenate.75.info_ref, ...), custom_call_target="tpu_custom_call" | custom-call | flops 30000001024 | bytes 45000000 | tf_op jit(solution)/shard_map/experts/pallas_call | solution.py:372
  387.1 18.1 %collective-permute-done.21 = bf16[2,256,1536]{2,1,0:T(8,128)(2,1)S(1)} collective-permute-done((bf16[2,256,1536]{2,1,0:T(8,128)(2,1)}, bf16[2,256,1536]{2,1,0:T(8,128)(2,1)S(1)}, u32[]{:S(2)}, u32[]{:S(2)}) %collective-permute-start.21) | collective-permute-done | bytes 1572896 | tf_op jit(solution)/shard_map/near2/ppermute | solution.py:71
  413.1 28.6 %experts.6 = (bf16[4,256,1536]{2,1,0:T(8,128)(2,1)}, bf16[4,256,1664]{2,1,0:T(8,128)(2,1)}, bf16[2,4,256,1664]{3,2,1,0:T(8,128)(2,1)}, bf16[2,2,352,1536]{3,2,1,...) custom-call(s32[10]{0:T(128)} %concatenate.78.info_ref, ...), custom_call_target="tpu_custom_call" | custom-call | flops 30000001024 | bytes 45000000 | tf_op jit(solution)/shard_map/experts/pallas_call | solution.py:372
  474.2 28.9 %experts.7 = (bf16[4,256,1536]{2,1,0:T(8,128)(2,1)}, bf16[4,256,1664]{2,1,0:T(8,128)(2,1)}, bf16[2,4,256,1664]{3,2,1,0:T(8,128)(2,1)}, bf16[2,2,352,1536]{3,2,1,...) custom-call(s32[10]{0:T(128)} %concatenate.77.info_ref, ...), custom_call_target="tpu_custom_call" | custom-call | flops 30000001024 | bytes 45000000 | tf_op jit(solution)/shard_map/experts/pallas_call | solution.py:372
  508.3 11.5 %wgrad_part.1 = bf16[1536,384]{1,0:T(8,128)(2,1)} custom-call(bf16[2,2,352,1536]{3,2,1,0:T(8,128)(2,1)} %get-tuple-element.179.refs_0_, bf16[2,2,352,1536]{3,2,1,0:T(8,128)(2,1)} %get-tuple-element.161.refs_1_, bf16[2,2,352,1536]{3,2,1,0:T(8,128)(2,1)} %get-tuple-element.162.refs_2_, bf16[2,2,352,1536]{3,2,1,0:T(8,128)(2,1)} %get-tuple-element.163.refs_3_, ...), custom_call_target="tpu_custom_call" | custom-call | flops 1000000 | bytes 10000 | tf_op jit(solution)/shard_map/wgrad_part/pallas_call | solution.py:423
  528.3 15.3 %wgrad_full.1 = bf16[1536,1024]{1,0:T(8,128)(2,1)} custom-call(bf16[2,2,352,1536]{3,2,1,0:T(8,128)(2,1)} %get-tuple-element.179.refs_0_, bf16[2,2,352,1536]{3,2,1,0:T(8,128)(2,1)} %get-tuple-element.161.refs_1_, bf16[2,2,352,1536]{3,2,1,0:T(8,128)(2,1)} %get-tuple-element.162.refs_2_, bf16[2,2,352,1536]{3,2,1,0:T(8,128)(2,1)} %get-tuple-element.163.refs_3_, ...), custom_call_target="tpu_custom_call" | custom-call | flops 1000000 | bytes 10000 | tf_op jit(solution)/shard_map/wgrad_full/pallas_call | solution.py:423
  569.3 11.9 %collective-permute-done.36 = bf16[256,1664]{1,0:T(8,128)(2,1)} collective-permute-done((bf16[256,1664]{1,0:T(8,128)(2,1)}, bf16[256,1664]{1,0:T(8,128)(2,1)}, u32[]{:S(2)}, u32[]{:S(2)}) %collective-permute-start.36) | collective-permute-done | bytes 852000 | tf_op jit(solution)/shard_map/d_near3/ppermute | solution.py:71
  589.0 10.3 %collective-permute-done.33 = bf16[2,256,1664]{2,1,0:T(8,128)(2,1)S(1)} collective-permute-done((bf16[2,256,1664]{2,1,0:T(8,128)(2,1)}, bf16[2,256,1664]{2,1,0:T(8,128)(2,1)S(1)}, u32[]{:S(2)}, u32[]{:S(2)}) %collective-permute-start.33) | collective-permute-done | bytes 1703968 | tf_op jit(solution)/shard_map/d_far0/ppermute | solution.py:71
  614.9 10.1 %wgrad_down.1 = bf16[1536,512]{1,0:T(8,128)(2,1)} custom-call(bf16[2,2,352,1536]{3,2,1,0:T(8,128)(2,1)} %get-tuple-element.190.refs_8_.refs_0_, bf16[2,2,352,1536]{3,2,1,0:T(8,128)(2,1)} %get-tuple-element.169.refs_9_.refs_1_, bf16[2,2,352,1536]{3,2,1,0:T(8,128)(2,1)} %get-tuple-element.170.refs_10_.refs_2_, ...), custom_call_target="tpu_custom_call" | custom-call | flops 1000000 | bytes 10000 | tf_op jit(solution)/shard_map/wgrad_down/pallas_call | solution.py:423
  630.0 11.8 %collective-permute-done.40.refs_4_ = bf16[256,1664]{1,0:T(8,128)(2,1)} collective-permute-done((bf16[256,1664]{1,0:T(8,128)(2,1)}, bf16[256,1664]{1,0:T(8,128)(2,1)}, u32[]{:S(2)}, u32[]{:S(2)}) %collective-permute-start.40) | collective-permute-done | bytes 852000 | tf_op jit(solution)/shard_map/home1/ppermute | solution.py:71
  655.0 11.9 %collective-permute-done.43 = bf16[256,1536]{1,0:T(8,128)(2,1)S(1)} collective-permute-done((bf16[256,1536]{1,0:T(8,128)(2,1)}, bf16[256,1536]{1,0:T(8,128)(2,1)S(1)}, u32[]{:S(2)}, u32[]{:S(2)}) %collective-permute-start.43) | collective-permute-done | bytes 786464 | tf_op jit(solution)/shard_map/plane_near/ppermute | solution.py:71
  695.6 11.5 %collective-permute-done.47 = bf16[2,256,1536]{2,1,0:T(8,128)(2,1)} collective-permute-done((bf16[2,256,1536]{2,1,0:T(8,128)(2,1)}, bf16[2,256,1536]{2,1,0:T(8,128)(2,1)}, u32[]{:S(2)}, u32[]{:S(2)}) %collective-permute-start.47) | collective-permute-done | bytes 1572896 | tf_op jit(solution)/shard_map/m_far1/ppermute | solution.py:71
  715.2 34.1 %attend_back.1 = (bf16[4,256,1536]{2,1,0:T(8,128)(2,1)}, bf16[1536,1024]{1,0:T(8,128)(2,1)}, f32[1,1536]{1,0:T(1,128)}) custom-call(s32[16]{0:T(128)} %concatenate.65.info_ref, bf16[4,256,1536]{2,1,0:T(8,128)(2,1)} %pad_maximum_fusion.6.da_ref, bf16[4,256,1536]{2,1,0:T(8,128)(2,1)} %pad_maximum_fusion.n1_ref, bf16[1536,1024]{1,0:T(8,128)(2,1)} %get-tuple-element.199.w_ref, ...), custom_call_target="tpu_custom_call" | custom-call | flops 1000000 | bytes 10000 | tf_op jit(solution)/shard_map/attend_back/pallas_call | solution.py:658
  795.9 15.8 %collective-permute-done.50 = bf16[2,256,1536]{2,1,0:T(8,128)(2,1)} collective-permute-done((bf16[2,256,1536]{2,1,0:T(8,128)(2,1)}, bf16[2,256,1536]{2,1,0:T(8,128)(2,1)}, u32[]{:S(2)}, u32[]{:S(2)}) %collective-permute-start.50) | collective-permute-done | bytes 1572896 | tf_op jit(solution)/shard_map/m_far0/ppermute | solution.py:71
  836.4 9.3 %unpack_experts.1 = (f32[10,192,1024]{2,1,0:T(8,128)}, f32[10,192,512]{2,1,0:T(8,128)}) custom-call(bf16[8,192,1024]{2,1,0:T(8,128)(2,1)} %all-to-all-done.4.full_ref, bf16[8,192,512]{2,1,0:T(8,128)(2,1)} %all-to-all-done.3.down_ref, bf16[8,192,384]{2,1,0:T(8,128)(2,1)} %all-to-all-done.2.part_ref), custom_call_target="tpu_custom_call" | custom-call | tf_op jit(solution)/shard_map/unpack_experts/pallas_call | solution.py:235
  854.9 11.3 %collective-permute-done.60 = f32[48,1536]{1,0:T(8,128)S(1)} collective-permute-done((f32[48,1536]{1,0:T(8,128)S(1)}, f32[48,1536]{1,0:T(8,128)S(1)}, u32[]{:S(2)}, u32[]{:S(2)}) %collective-permute-start.60) | collective-permute-done | bytes 294944 | tf_op jit(solution)/shard_map/small/ppermute | solution.py:71
  (311 shorter events, 349.9 us)
Async XLA Ops:
  14.1 31.9 %collective-permute-start.1 = (bf16[208,1024]{1,0:T(8,128)(2,1)S(1)}, bf16[208,1024]{1,0:T(8,128)(2,1)S(1)}, u32[]{:S(2)}, u32[]{:S(2)}) collective-permute-start(bf16[208,1024]{1,0:T(8,128)(2,1)S(1)} %get-tuple-element.229), channel_id=1, source_target_pairs={{0,16},{1,17},{2,18},{3,19},{4,20},{5,21},{6,22},{7,23},{8,24},{9,... | collective-permute-start | bytes 1277960 | tf_op jit(solution)/shard_map/pieces/ppermute | solution.py:71
  46.3 74.0 %all-to-all-start = ((bf16[8,192,896]{2,1,0:T(8,128)(2,1)}), bf16[8,192,896]{2,1,0:T(8,128)(2,1)}, u32[]{:S(2)}, u32[]{:S(2)}) async-start(bf16[8,192,896]{2,1,0:T(8,128)(2,1)} %pack_experts.1), calls=%async_computation | async-start | bytes 5505024 | tf_op jit(solution)/shard_map/all_to_all | solution.py:785
  96.6 35.1 %collective-permute-start.7 = (bf16[4,208,1024]{2,1,0:T(8,128)(2,1)S(1)}, bf16[4,208,1024]{2,1,0:T(8,128)(2,1)}, u32[]{:S(2)}, u32[]{:S(2)}) collective-permute-start(bf16[4,208,1024]{2,1,0:T(8,128)(2,1)S(1)} %pad_maximum_fusion.9.refs_0_), channel_id=1, source_target_pairs={{0,4},{1,5},{2,6},{3,7},{4,0},{5,1},{6,2},{7,3},{8,12},{9,13},{10,... | collective-permute-start | bytes 5111816 | tf_op jit(solution)/shard_map/pieces_theirs/ppermute | solution.py:71
  120.3 76.2 %all-to-all-start.1 = ((bf16[8,192,1024]{2,1,0:T(8,128)(2,1)}), bf16[8,192,1024]{2,1,0:T(8,128)(2,1)}, u32[]{:S(2)}, u32[]{:S(2)}) async-start(bf16[8,192,1024]{2,1,0:T(8,128)(2,1)} %slice.229), calls=%async_computation.1 | async-start | bytes 6291456 | tf_op jit(solution)/shard_map/all_to_all | solution.py:785
  179.4 53.0 %collective-permute-start.15 = (bf16[4,256,1536]{2,1,0:T(8,128)(2,1)}, bf16[4,256,1536]{2,1,0:T(8,128)(2,1)}, u32[]{:S(2)}, u32[]{:S(2)}) collective-permute-start(bf16[4,256,1536]{2,1,0:T(8,128)(2,1)} %pad_maximum_fusion.3.ya_ref), channel_id=1, source_target_pairs={{0,4},{1,5},{2,6},{3,7},{4,0},{5,1},{6,2},{7,3},{8,12},{9,13},{10,... | collective-permute-start | bytes 9437192 | tf_op jit(solution)/shard_map/y_theirs0/ppermute | solution.py:71
  211.5 36.0 %collective-permute-start.10 = (bf16[2,256,1536]{2,1,0:T(8,128)(2,1)}, bf16[2,256,1536]{2,1,0:T(8,128)(2,1)}, u32[]{:S(2)}, u32[]{:S(2)}) collective-permute-start(bf16[2,256,1536]{2,1,0:T(8,128)(2,1)} %get-tuple-element.227), channel_id=1, source_target_pairs={{0,8},{1,9},{2,10},{3,11},{4,12},{5,13},{6,14},{7,15},{8,24},{9,25... | collective-permute-start | bytes 4718600 | tf_op jit(solution)/shard_map/both1/ppermute | solution.py:71
  232.4 52.3 %collective-permute-start.16 = (bf16[4,256,1536]{2,1,0:T(8,128)(2,1)}, bf16[4,256,1536]{2,1,0:T(8,128)(2,1)}, u32[]{:S(2)}, u32[]{:S(2)}) collective-permute-start(bf16[4,256,1536]{2,1,0:T(8,128)(2,1)} %pad_maximum_fusion.2.xa_ref), channel_id=1, source_target_pairs={{0,4},{1,5},{2,6},{3,7},{4,0},{5,1},{6,2},{7,3},{8,12},{9,13},{10,... | collective-permute-start | bytes 9437192 | tf_op jit(solution)/shard_map/theirs0/ppermute | solution.py:71
  248.1 36.6 %collective-permute-start.12 = (bf16[2,256,1536]{2,1,0:T(8,128)(2,1)}, bf16[2,256,1536]{2,1,0:T(8,128)(2,1)}, u32[]{:S(2)}, u32[]{:S(2)}) collective-permute-start(bf16[2,256,1536]{2,1,0:T(8,128)(2,1)} %get-tuple-element.227), channel_id=1, source_target_pairs={{8,0},{9,1},{10,2},{11,3},{12,4},{13,5},{14,6},{15,7},{24,8},{25,9... | collective-permute-start | bytes 4718600 | tf_op jit(solution)/shard_map/both3/ppermute | solution.py:71
  271.5 43.9 %collective-permute-start.19 = (bf16[2,2,256,1536]{3,2,1,0:T(8,128)(2,1)S(1)}, bf16[2,2,256,1536]{3,2,1,0:T(8,128)(2,1)}, u32[]{:S(2)}, u32[]{:S(2)}) collective-permute-start(bf16[2,2,256,1536]{3,2,1,0:T(8,128)(2,1)S(1)} %pad_maximum_fusion.1), channel_id=1, source_target_pairs={{0,2},{1,3},{2,0},{3,1},{4,5},{5,4},{6,7},{7,6},{8,10},{9,11},{10,... | collective-permute-start | bytes 9437192 | tf_op jit(solution)/shard_map/far1/ppermute | solution.py:71
  273.8 45.3 %collective-permute-start.17 = (bf16[2,256,1536]{2,1,0:T(8,128)(2,1)}, bf16[2,256,1536]{2,1,0:T(8,128)(2,1)}, u32[]{:S(2)}, u32[]{:S(2)}) collective-permute-start(bf16[2,256,1536]{2,1,0:T(8,128)(2,1)} %collective-permute-done.10), channel_id=1, source_target_pairs={{0,8},{1,9},{2,10},{3,11},{4,12},{5,13},{6,14},{7,15},{8,24},{9,25... | collective-permute-start | bytes 4718600 | tf_op jit(solution)/shard_map/both2/ppermute | solution.py:71
  341.5 37.4 %collective-permute-start.23 = (bf16[2,2,256,1536]{3,2,1,0:T(8,128)(2,1)S(1)}, bf16[2,2,256,1536]{3,2,1,0:T(8,128)(2,1)}, u32[]{:S(2)}, u32[]{:S(2)}) collective-permute-start(bf16[2,2,256,1536]{3,2,1,0:T(8,128)(2,1)S(1)} %pad_maximum_fusion.4), channel_id=1, source_target_pairs={{0,2},{1,3},{2,0},{3,1},{4,5},{5,4},{6,7},{7,6},{8,10},{9,11},{10,... | collective-permute-start | bytes 9437192 | tf_op jit(solution)/shard_map/far3/ppermute | solution.py:71
  343.8 66.5 %collective-permute-start.22 = (bf16[2,4,256,1664]{3,2,1,0:T(8,128)(2,1)}, bf16[2,4,256,1664]{3,2,1,0:T(8,128)(2,1)}, u32[]{:S(2)}, u32[]{:S(2)}) collective-permute-start(bf16[2,4,256,1664]{3,2,1,0:T(8,128)(2,1)} %get-tuple-element.141), channel_id=1, source_target_pairs={{0,4},{1,5},{2,6},{3,7},{4,0},{5,1},{6,2},{7,3},{8,12},{9,13},{10,... | collective-permute-start | bytes 20447240 | tf_op jit(solution)/shard_map/swap0/ppermute | solution.py:71
  386.9 68.1 %collective-permute-start.26 = (bf16[2,4,256,1664]{3,2,1,0:T(8,128)(2,1)}, bf16[2,4,256,1664]{3,2,1,0:T(8,128)(2,1)}, u32[]{:S(2)}, u32[]{:S(2)}) collective-permute-start(bf16[2,4,256,1664]{3,2,1,0:T(8,128)(2,1)} %get-tuple-element.153), channel_id=1, source_target_pairs={{0,4},{1,5},{2,6},{3,7},{4,0},{5,1},{6,2},{7,3},{8,12},{9,13},{10,... | collective-permute-start | bytes 20447240 | tf_op jit(solution)/shard_map/swap1/ppermute | solution.py:71
  408.7 37.6 %collective-permute-start.25 = (bf16[2,2,256,1536]{3,2,1,0:T(8,128)(2,1)}, bf16[2,2,256,1536]{3,2,1,0:T(8,128)(2,1)}, u32[]{:S(2)}, u32[]{:S(2)}) collective-permute-start(bf16[2,2,256,1536]{3,2,1,0:T(8,128)(2,1)} %pad_maximum_fusion.5), channel_id=1, source_target_pairs={{0,2},{1,3},{2,0},{3,1},{4,5},{5,4},{6,7},{7,6},{8,10},{9,11},{10,... | collective-permute-start | bytes 9437192 | tf_op jit(solution)/shard_map/far2/ppermute | solution.py:71
  460.3 42.8 %collective-permute-start.29 = (bf16[2,256,1664]{2,1,0:T(8,128)(2,1)}, bf16[2,256,1664]{2,1,0:T(8,128)(2,1)}, u32[]{:S(2)}, u32[]{:S(2)}) collective-permute-start(bf16[2,256,1664]{2,1,0:T(8,128)(2,1)} %slice.309), channel_id=1, source_target_pairs={{0,2},{1,3},{2,0},{3,1},{4,5},{5,4},{6,7},{7,6},{8,10},{9,11},{10,... | collective-permute-start | bytes 5111816 | tf_op jit(solution)/shard_map/d_far1/ppermute | solution.py:71
  471.0 32.0 %collective-permute-start.30 = (bf16[2,256,1664]{2,1,0:T(8,128)(2,1)}, bf16[2,256,1664]{2,1,0:T(8,128)(2,1)}, u32[]{:S(2)}, u32[]{:S(2)}) collective-permute-start(bf16[2,256,1664]{2,1,0:T(8,128)(2,1)} %slice.312), channel_id=1, source_target_pairs={{0,2},{1,3},{2,0},{3,1},{4,5},{5,4},{6,7},{7,6},{8,10},{9,11},{10,... | collective-permute-start | bytes 5111816 | tf_op jit(solution)/shard_map/d_far3/ppermute | solution.py:71
  557.0 43.9 %collective-permute-start.38 = (bf16[256,1664]{1,0:T(8,128)(2,1)}, bf16[256,1664]{1,0:T(8,128)(2,1)}, u32[]{:S(2)}, u32[]{:S(2)}) collective-permute-start(bf16[256,1664]{1,0:T(8,128)(2,1)} %fusion.31), channel_id=1, source_target_pairs={{0,1},{1,0},{2,3},{3,2},{4,6},{5,7},{6,4},{7,5},{8,9},{9,8},{10,11... | collective-permute-start | bytes 2555912 | tf_op jit(solution)/shard_map/d_near1/ppermute | solution.py:71
  558.7 52.4 %all-to-all-start.2 = ((bf16[8,192,384]{2,1,0:T(8,128)(2,1)}), bf16[8,192,384]{2,1,0:T(8,128)(2,1)}, u32[]{:S(2)}, u32[]{:S(2)}) async-start(bf16[8,192,384]{2,1,0:T(8,128)(2,1)} %bitcast.216), calls=%async_computation.2 | async-start | bytes 2359296 | tf_op jit(solution)/shard_map/all_to_all | solution.py:785
  562.9 36.4 %collective-permute-start.33 = (bf16[2,256,1664]{2,1,0:T(8,128)(2,1)}, bf16[2,256,1664]{2,1,0:T(8,128)(2,1)S(1)}, u32[]{:S(2)}, u32[]{:S(2)}) collective-permute-start(bf16[2,256,1664]{2,1,0:T(8,128)(2,1)} %slice.306), channel_id=1, source_target_pairs={{0,2},{1,3},{2,0},{3,1},{4,5},{5,4},{6,7},{7,6},{8,10},{9,11},{10,... | collective-permute-start | bytes 5111816 | tf_op jit(solution)/shard_map/d_far0/ppermute | solution.py:71
  566.5 35.0 %collective-permute-start.39 = (bf16[256,1664]{1,0:T(8,128)(2,1)S(1)}, bf16[256,1664]{1,0:T(8,128)(2,1)S(1)}, u32[]{:S(2)}, u32[]{:S(2)}) collective-permute-start(bf16[256,1664]{1,0:T(8,128)(2,1)S(1)} %fusion.11), channel_id=1, source_target_pairs={{8,0},{9,1},{10,2},{11,3},{12,4},{13,5},{14,6},{15,7},{24,8},{25,9... | collective-permute-start | bytes 2555912 | tf_op jit(solution)/shard_map/home2/ppermute | solution.py:71
  584.1 63.0 %collective-permute-start.37 = (bf16[256,1664]{1,0:T(8,128)(2,1)}, bf16[256,1664]{1,0:T(8,128)(2,1)}, u32[]{:S(2)}, u32[]{:S(2)}) collective-permute-start(bf16[256,1664]{1,0:T(8,128)(2,1)} %fusion.14), channel_id=1, source_target_pairs={{0,8},{1,9},{2,10},{3,11},{4,12},{5,13},{6,14},{7,15},{8,24},{9,25... | collective-permute-start | bytes 2555912 | tf_op jit(solution)/shard_map/home3/ppermute | solution.py:71
  611.1 30.8 %collective-permute-start.40 = (bf16[256,1664]{1,0:T(8,128)(2,1)}, bf16[256,1664]{1,0:T(8,128)(2,1)}, u32[]{:S(2)}, u32[]{:S(2)}) collective-permute-start(bf16[256,1664]{1,0:T(8,128)(2,1)} %fusion.13), channel_id=1, source_target_pairs={{8,0},{9,1},{10,2},{11,3},{12,4},{13,5},{14,6},{15,7},{24,8},{25,9... | collective-permute-start | bytes 2555912 | tf_op jit(solution)/shard_map/home1/ppermute | solution.py:71
  614.5 32.6 %collective-permute-start.35 = (bf16[256,1664]{1,0:T(8,128)(2,1)}, bf16[256,1664]{1,0:T(8,128)(2,1)}, u32[]{:S(2)}, u32[]{:S(2)}) collective-permute-start(bf16[256,1664]{1,0:T(8,128)(2,1)} %fusion.33), channel_id=1, source_target_pairs={{0,1},{1,0},{2,3},{3,2},{4,6},{5,7},{6,4},{7,5},{8,9},{9,8},{10,11... | collective-permute-start | bytes 2555912 | tf_op jit(solution)/shard_map/d_near0/ppermute | solution.py:71
  641.8 42.1 %all-to-all-start.3 = ((bf16[8,192,512]{2,1,0:T(8,128)(2,1)}), bf16[8,192,512]{2,1,0:T(8,128)(2,1)}, u32[]{:S(2)}, u32[]{:S(2)}) async-start(bf16[8,192,512]{2,1,0:T(8,128)(2,1)} %bitcast.215), calls=%async_computation.3 | async-start | bytes 3145728 | tf_op jit(solution)/shard_map/all_to_all | solution.py:785
  672.3 34.8 %collective-permute-start.47 = (bf16[2,256,1536]{2,1,0:T(8,128)(2,1)}, bf16[2,256,1536]{2,1,0:T(8,128)(2,1)}, u32[]{:S(2)}, u32[]{:S(2)}) collective-permute-start(bf16[2,256,1536]{2,1,0:T(8,128)(2,1)} %slice.339), channel_id=1, source_target_pairs={{0,2},{1,3},{2,0},{3,1},{4,5},{5,4},{6,7},{7,6},{8,10},{9,11},{10,... | collective-permute-start | bytes 4718600 | tf_op jit(solution)/shard_map/m_far1/ppermute | solution.py:71
  684.0 110.3 %all-to-all-start.4 = ((bf16[8,192,1024]{2,1,0:T(8,128)(2,1)}), bf16[8,192,1024]{2,1,0:T(8,128)(2,1)}, u32[]{:S(2)}, u32[]{:S(2)}) async-start(bf16[8,192,1024]{2,1,0:T(8,128)(2,1)} %bitcast.207), calls=%async_computation.4 | async-start | bytes 6291456 | tf_op jit(solution)/shard_map/all_to_all | solution.py:785
  688.5 179.1 %reduce-scatter.2.cloned.1.call-start = ((), (), s32[]{:S(2)}) async-start(), calls=%async_computation.6 | async-start | bytes 3538944 | tf_op jit(solution)/shard_map/reduce_scatter | solution.py:948
  694.1 63.0 %collective-permute-start.46 = (bf16[2,256,1536]{2,1,0:T(8,128)(2,1)}, bf16[2,256,1536]{2,1,0:T(8,128)(2,1)}, u32[]{:S(2)}, u32[]{:S(2)}) collective-permute-start(bf16[2,256,1536]{2,1,0:T(8,128)(2,1)} %slice.337), channel_id=1, source_target_pairs={{0,2},{1,3},{2,0},{3,1},{4,5},{5,4},{6,7},{7,6},{8,10},{9,11},{10,... | collective-permute-start | bytes 4718600 | tf_op jit(solution)/shard_map/m_far3/ppermute | solution.py:71
  712.1 45.0 %collective-permute-start.45 = (bf16[256,1536]{1,0:T(8,128)(2,1)}, bf16[256,1536]{1,0:T(8,128)(2,1)}, u32[]{:S(2)}, u32[]{:S(2)}) collective-permute-start(bf16[256,1536]{1,0:T(8,128)(2,1)} %fusion.30), channel_id=1, source_target_pairs={{8,0},{9,1},{10,2},{11,3},{12,4},{13,5},{14,6},{15,7},{24,8},{25,9... | collective-permute-start | bytes 2359304 | tf_op jit(solution)/shard_map/m_home2/ppermute | solution.py:71
  714.9 42.2 %collective-permute-start.48 = (bf16[256,1536]{1,0:T(8,128)(2,1)}, bf16[256,1536]{1,0:T(8,128)(2,1)}, u32[]{:S(2)}, u32[]{:S(2)}) collective-permute-start(bf16[256,1536]{1,0:T(8,128)(2,1)} %fusion.38), channel_id=1, source_target_pairs={{0,1},{1,0},{2,3},{3,2},{4,6},{5,7},{6,4},{7,5},{8,9},{9,8},{10,11... | collective-permute-start | bytes 2359304 | tf_op jit(solution)/shard_map/m_near1/ppermute | solution.py:71
  785.5 66.3 %collective-permute-start.52 = (bf16[256,1536]{1,0:T(8,128)(2,1)}, bf16[256,1536]{1,0:T(8,128)(2,1)S(1)}, u32[]{:S(2)}, u32[]{:S(2)}) collective-permute-start(bf16[256,1536]{1,0:T(8,128)(2,1)} %fusion.25), channel_id=1, source_target_pairs={{8,0},{9,1},{10,2},{11,3},{12,4},{13,5},{14,6},{15,7},{24,8},{25,9... | collective-permute-start | bytes 2359304 | tf_op jit(solution)/shard_map/m_home1/ppermute | solution.py:71
  819.2 32.6 %collective-permute-start.54 = (bf16[256,1536]{1,0:T(8,128)(2,1)}, bf16[256,1536]{1,0:T(8,128)(2,1)}, u32[]{:S(2)}, u32[]{:S(2)}) collective-permute-start(bf16[256,1536]{1,0:T(8,128)(2,1)} %fusion.23), channel_id=1, source_target_pairs={{0,8},{1,9},{2,10},{3,11},{4,12},{5,13},{6,14},{7,15},{8,24},{9,25... | collective-permute-start | bytes 2359304 | tf_op jit(solution)/shard_map/m_home3/ppermute | solution.py:71
  (78 other events, 1139.9 us)
Sparse Core Ops, SparseCore 0:
  759.4 61.7 reduce-scatter.1

commit v3 on v2

--- a/solution.py
+++ b/solution.py
@@ -838,32 +838,33 @@
         return expert_chunk(chunk_info, rows, routes_all, router_t, weights)
 
     if fast:
-        near0 = send("near0", x, first)
         both = jnp.stack([x, y])
+        near0 = send("near0", x, first, both)
         both1 = send("both1", both, links.along)
         both3 = send("both3", both, links.against)
         pair0 = jnp.stack([x, near0])
         far0 = send("far0", pair0, second)
         mine0 = jnp.concatenate([pair0, far0])
-        theirs0 = send("theirs0", mine0, swap, y_theirs0)
         near1 = send("near1", both1, first)
+        theirs0 = send("theirs0", mine0, swap, y_theirs0, near1)
         both2 = send("both2", both1, links.along)
         pair1 = jnp.stack([both1, near1])
         far1 = send("far1", pair1, second)
-        done0 = run(0, [(mine0, None), (theirs0, None), (y_mine0, None), (y_theirs0, None)], pair1, both3)
+        done0 = run(0, [(mine0, None), (theirs0, None), (y_mine0, None), (y_theirs0, None)], pair1)
         past = done0[-1]
-        near3 = send("near3", both3, first, pair1)
+        near3 = send("near3", both3, first, past)
         mine1 = jnp.concatenate([after(pair1, past), after(far1, past)])
-        theirs1 = send("theirs1", mine1, swap, both2)
+        theirs1 = send("theirs1", mine1, swap, both3)
         swap0 = send("swap0", done0[2], swap, mine1)
         pair3 = jnp.stack([after(both3, past), after(near3, past)])
         far3 = send("far3", pair3, second)
-        near2 = send("near2", both2, first, pair3)
-        done1 = run(1, [(mine1, 0), (theirs1, 0), (mine1, 1), (theirs1, 1)], pair3, both2)
+
+        done1 = run(1, [(mine1, 0), (theirs1, 0), (mine1, 1), (theirs1, 1)], pair3)
         past = done1[-1]
+        near2 = send("near2", both2, first, past)
         mine3 = jnp.concatenate([after(pair3, past), after(far3, past)])
         pair2 = jnp.stack([after(both2, past), after(near2, past)])
-        theirs3 = send("theirs3", mine3, swap)
+        theirs3 = send("theirs3", mine3, swap, both2)
         far2 = send("far2", pair2, second)
         swap1 = send("swap1", done1[2], swap, mine3)
         d0 = add(after(done0[1], pair2), after(swap0, past)[0])
@@ -900,29 +901,27 @@
             return got
         return jnp.sum(got.reshape((-1, group) + got.shape[1:]).astype(F32), axis=0).astype(BF)
 
-    got_part = give_back(part_grad)
     if fast:
         d2 = add(after(done2[1], part_grad), swap2[0])
         d_far2 = send("d_far2", d2[2:], second)
         home3 = send("home3", total_of([d3[0], d_far3[0], d_near3]).astype(BF), links.along, part_grad)
         taken[0] = after(taken[0], d2)
+    got_part = give_back(part_grad)
     full_grad = expert_wgrad([(taken, 0, dgu, 0, 2 * F)], "wgrad_full")
     if fast:
-        d_near2 = send("d_near2", add(d2[1], d_far2[1]), first, full_grad)
-        d_far0 = send("d_far0", d0[2:], second, d_far2)
-        home2 = send("home2", total_of([d2[0], d_far2[0], d_near2]).astype(BF), links.against)
-        m2 = add(after(done[2][0], d_near2), swaps[2][1, ..., :width])
-        m_far2 = send("m_far2", m2[2:], second, d_far0)
+        n2 = add(d2[1], after(d_far2, full_grad)[1])
+        d_near2 = send("d_near2", n2, first, home3)
+        dz[0] = after(dz[0], n2)
+    down_grad = expert_wgrad([(dz, 0, hid, 0, F)], "wgrad_down")
+    if fast:
+        d_far0 = send("d_far0", d0[2:], second, d_near2)
+        home2 = send("home2", total_of([d2[0], d_far2[0], d_near2]).astype(BF), links.against, down_grad)
         h1 = total_of([d1[0], d_far1[0], d_near1, home2]).astype(BF)
         home1 = send("home1", h1, links.against, got_part)
-        d_near0 = send("d_near0", add(d0[1], d_far0[1]), first, d_near2)
-        m1 = add(after(done[1][0], h1), swaps[1][1, ..., :width])
-        m_far1 = send("m_far1", m1[2:], second, h1)
-        dz[0] = after(dz[0], m1, h1)
-    down_grad = expert_wgrad([(dz, 0, hid, 0, F)], "wgrad_down")
-    if fast:
-        m_near2 = send("m_near2", add(m2[1], m_far2[1]), first, down_grad)
-        parts = [d0[0], d_far0[0], d_near0, home3, after(home1, m_near2)]
+        d_near0 = send("d_near0", add(d0[1], after(d_far0, h1)[1]), first)
+        m2 = add(after(done[2][0], h1), swaps[2][1, ..., :width])
+        m_far2 = send("m_far2", m2[2:], second, d_far0)
+        parts = [d0[0], d_far0[0], d_near0, home3, home1]
         before = (home1,)
     else:
         before = ()
@@ -935,7 +934,9 @@
     )
     branch_group = links.gather_plane(branch_grad)
     if fast:
-        m_near1 = send("m_near1", add(m1[1], m_far1[1]), first, branch_group)
+        m1 = add(after(done[1][0], branch_grad), swaps[1][1, ..., :width])
+        m_far1 = send("m_far1", m1[2:], second, branch_grad)
+        m_near2 = send("m_near2", add(m2[1], after(m_far2, branch_grad)[1]), first)
         m_home2 = send("m_home2", total_of([m2[0], m_far2[0], m_near2]).astype(BF), links.against, branch_grad)
         m3 = add(after(done[3][0], branch_grad), swaps[3][1, ..., :width])
         m_far3 = send("m_far3", m3[2:], second, branch_group)
@@ -946,17 +947,18 @@
         heads, after(info, *before), branch_group, normed_group, attention_weights, cosine, sine, qkv, attended, lse, seqs
     )
     attention_mine = lax.psum_scatter(attention_grad, "dp", scatter_dimension=0, tiled=True).astype(F32)
-    n_parts = links.scatter_plane(dn1, *([m_home2, m_far3, m_near1] if fast else []))
+    n_parts = links.scatter_plane(dn1, *([m_far3, m_far1] if fast else []))
     first_grad = total_of(n_parts)
     small = jnp.concatenate([router_part, first_gain / norm_gains[0:1], second_gain])
     small = jnp.pad(small, ((0, 6), (0, 0)))
     if fast:
-        m0 = add(after(done[0][0], branch_grad), swaps[0][1, ..., :width])
-        m_far0 = send("m_far0", m0[2:], second, n_parts[1])
+        m_near1 = send("m_near1", add(m1[1], m_far1[1]), first, n_parts[1])
+        m0 = add(after(done[0][0], n_parts[1]), swaps[0][1, ..., :width])
+        m_far0 = send("m_far0", m0[2:], second)
         m_near3 = send("m_near3", add(m3[1], m_far3[1]), first, n_parts[1], got_full)
-        m_near0 = send("m_near0", add(m0[1], m_far0[1]), first)
+        m_near0 = send("m_near0", add(m0[1], m_far0[1]), first, attention_mine)
         m_home3 = send("m_home3", total_of([m3[0], m_far3[0], m_near3]).astype(BF), links.along)
-        m_home1 = send("m_home1", total_of([m1[0], m_far1[0], m_near1, m_home2]).astype(BF), links.against, dn1)
+        m_home1 = send("m_home1", total_of([m1[0], m_far1[0], m_near1, m_home2]).astype(BF), links.against)
         out = [m0[0], m_far0[0], m_near0, m_home1, m_home3]
         before = (m_near0, m_near3)
     else:

time: 884 us -> 866 us (0.980)
  starting transfers between devices: 107 us -> 95.2 us
  other arithmetic: 110 us -> 101 us
    all_to_all x5, waiting for transfers between devices: 29.2 us -> 55.9 us  [shards(): to_all = lambda a: lax.all_to_all(a, 'dp', 0, 0)]
    ppermute x61, waiting for transfers between devices: 327 us -> 307 us  [send(): return lax.ppermute(value, ('dp', 'tensor'), perm)]
    ppermute x61, starting transfers between devices: 78.3 us -> 66.6 us  [send(): return lax.ppermute(value, ('dp', 'tensor'), perm)]
  transfers between devices with their start and end apart: 67 -> 67, of which waited for: 38 -> 37; matrix products, arithmetic and copies ran while one was open for 17% -> 17% of each run, Pallas kernels for 26% -> 26%
where the time goes in v3:
time: 866 us; the launch traced here: 861 us
  waiting for transfers between devices  363 us (42%)
  Pallas kernels  231 us (27%)
  other arithmetic  101 us (12%)
  starting transfers between devices  95.2 us (11%)
  local copies, waits for them, and re-layouts  55.9 us (6%)
  between operations  15.3 us (2%)
    ppermute x61, waiting for transfers between devices, send(): return lax.ppermute(value, ('dp', 'tensor'), perm)  307 us
    pallas_call x4, Pallas kernels, expert_chunk(): pl.pallas_call(expert_kernel, grid_spec=pltpu.PrefetchScalarGridSpec(num_...  115 us
    ppermute x61, starting transfers between devices, send(): return lax.ppermute(value, ('dp', 'tensor'), perm)  66.6 us
    all_to_all x5, waiting for transfers between devices, shards(): to_all = lambda a: lax.all_to_all(a, 'dp', 0, 0)  55.9 us
    convert_element_type x18, other arithmetic, add(): return (a.astype(F32) + b.astype(F32)).astype(a.dtype)  44.7 us
    pallas_call x3, Pallas kernels, expert_wgrad(): pl.pallas_call(functools.partial(wgrad_kernel, chunks, len(pairs)), grid=...  36.7 us
    pallas_call x1, Pallas kernels, attend_backward(): pl.pallas_call(functools.partial(attend_back_kernel, heads, blocks, seqs)...  34.3 us
    all_to_all x5, starting transfers between devices, shards(): to_all = lambda a: lax.all_to_all(a, 'dp', 0, 0)  28.5 us
  transfers between devices with their start and end apart: 67, of which 37 were waited for; matrix products, arithmetic and copies ran while one was open for 17% of the time, Pallas kernels for 26%

profile of v3, /device:TPU:0, one launch (start us, length us, event | category | flops | bytes accessed | tf_op | source)
XLA Modules:
  0.0 860.7 jit_solution(5109607603727175210)
XLA Ops:
  22.9 9.4 %collective-permute-done = bf16[208,1024]{1,0:T(8,128)(2,1)S(1)} collective-permute-done((bf16[208,1024]{1,0:T(8,128)(2,1)S(1)}, bf16[208,1024]{1,0:T(8,128)(2,1)S(1)}, u32[]{:S(2)}, u32[]{:S(2)}) %collective-permute-start) | collective-permute-done | bytes 426016 | tf_op jit(solution)/shard_map/pieces/ppermute | solution.py:71
  32.3 13.7 %collective-permute-done.1 = bf16[208,1024]{1,0:T(8,128)(2,1)S(1)} collective-permute-done((bf16[208,1024]{1,0:T(8,128)(2,1)S(1)}, bf16[208,1024]{1,0:T(8,128)(2,1)S(1)}, u32[]{:S(2)}, u32[]{:S(2)}) %collective-permute-start.1) | collective-permute-done | bytes 426016 | tf_op jit(solution)/shard_map/pieces/ppermute | solution.py:71
  46.3 10.8 %all-to-all-start = ((bf16[8,192,896]{2,1,0:T(8,128)(2,1)}), bf16[8,192,896]{2,1,0:T(8,128)(2,1)}, u32[]{:S(2)}, u32[]{:S(2)}) async-start(bf16[8,192,896]{2,1,0:T(8,128)(2,1)} %pack_experts.1), calls=%async_computation | async-start | bytes 5505024 | tf_op jit(solution)/shard_map/all_to_all | solution.py:785
  60.1 10.2 %collective-permute-done.3 = bf16[256,1536]{1,0:T(8,128)(2,1)S(1)} collective-permute-done((bf16[256,1536]{1,0:T(8,128)(2,1)S(1)}, bf16[256,1536]{1,0:T(8,128)(2,1)S(1)}, u32[]{:S(2)}, u32[]{:S(2)}) %collective-permute-start.3) | collective-permute-done | bytes 786464 | tf_op jit(solution)/shard_map/near/ppermute | solution.py:71
  72.0 18.9 %collective-permute-done.4 = bf16[2,256,1536]{2,1,0:T(8,128)(2,1)S(1)} collective-permute-done((bf16[2,256,1536]{2,1,0:T(8,128)(2,1)S(1)}, bf16[2,256,1536]{2,1,0:T(8,128)(2,1)S(1)}, u32[]{:S(2)}, u32[]{:S(2)}) %collective-permute-start.4) | collective-permute-done | bytes 1572896 | tf_op jit(solution)/shard_map/far/ppermute | solution.py:71
  107.0 13.3 %all-to-all-done = bf16[8,192,896]{2,1,0:T(8,128)(2,1)} async-done(((bf16[8,192,896]{2,1,0:T(8,128)(2,1)}), bf16[8,192,896]{2,1,0:T(8,128)(2,1)}, u32[]{:S(2)}, u32[]{:S(2)}) %all-to-all-start) | async-done | bytes 2752544 | tf_op jit(solution)/shard_map/all_to_all | solution.py:785
  131.6 20.3 %attend.1 = (bf16[4,256,1536]{2,1,0:T(8,128)(2,1)}, bf16[1024,640]{1,0:T(8,128)(2,1)}, bf16[1024,384]{1,0:T(8,128)(2,1)}, f32[1024,128]{1,0:T(8,128)}, bf16[1536,1024]{1,0:T(8,128)(2,1)}) custom-call(s32[16]{0:T(128)} %concatenate.65.info_ref, bf16[4,256,1536]{2,1,0:T(8,128)(2,1)} %pad_maximum_fusion.n1_ref, f32[1024,128]{1,0:T(8,128)} %get-tuple-element.241.cos_ref, ...), custom_call_target="tpu_custom_call" | custom-call | flops 1000000 | bytes 10000 | tf_op jit(solution)/shard_map/attend/pallas_call | solution.py:529
  155.2 18.9 %collective-permute-done.8 = bf16[2,256,1536]{2,1,0:T(8,128)(2,1)S(1)} collective-permute-done((bf16[2,256,1536]{2,1,0:T(8,128)(2,1)S(1)}, bf16[2,256,1536]{2,1,0:T(8,128)(2,1)S(1)}, u32[]{:S(2)}, u32[]{:S(2)}) %collective-permute-start.8) | collective-permute-done | bytes 1572896 | tf_op jit(solution)/shard_map/h_far/ppermute | solution.py:71
  179.4 7.0 collective-permute-done.9
  188.3 8.2 all-to-all-done.1
  198.3 10.5 %collective-permute-done.12 = bf16[256,1536]{1,0:T(8,128)(2,1)S(1)} collective-permute-done((bf16[256,1536]{1,0:T(8,128)(2,1)S(1)}, bf16[256,1536]{1,0:T(8,128)(2,1)S(1)}, u32[]{:S(2)}, u32[]{:S(2)}) %collective-permute-start.12) | collective-permute-done | bytes 786464 | tf_op jit(solution)/shard_map/near0/ppermute | solution.py:71
  210.6 23.0 %collective-permute-done.10 = bf16[2,256,1536]{2,1,0:T(8,128)(2,1)S(1)} collective-permute-done((bf16[2,256,1536]{2,1,0:T(8,128)(2,1)S(1)}, bf16[2,256,1536]{2,1,0:T(8,128)(2,1)S(1)}, u32[]{:S(2)}, u32[]{:S(2)}) %collective-permute-start.10) | collective-permute-done | bytes 1572896 | tf_op jit(solution)/shard_map/both1/ppermute | solution.py:71
  237.1 16.9 %collective-permute-done.11 = bf16[2,256,1536]{2,1,0:T(8,128)(2,1)S(1)} collective-permute-done((bf16[2,256,1536]{2,1,0:T(8,128)(2,1)S(1)}, bf16[2,256,1536]{2,1,0:T(8,128)(2,1)S(1)}, u32[]{:S(2)}, u32[]{:S(2)}) %collective-permute-start.11) | collective-permute-done | bytes 1572896 | tf_op jit(solution)/shard_map/near1/ppermute | solution.py:71
  260.0 28.8 %experts.4 = (bf16[4,256,1536]{2,1,0:T(8,128)(2,1)}, bf16[4,256,1664]{2,1,0:T(8,128)(2,1)}, bf16[2,4,256,1664]{3,2,1,0:T(8,128)(2,1)}, bf16[2,2,352,1536]{3,2,1,...) custom-call(s32[10]{0:T(128)} %concatenate.70.info_ref, ...), custom_call_target="tpu_custom_call" | custom-call | flops 30000001024 | bytes 45000000 | tf_op jit(solution)/shard_map/experts/pallas_call | solution.py:372
  298.8 19.1 %collective-permute-done.18 = bf16[2,256,1536]{2,1,0:T(8,128)(2,1)S(1)} collective-permute-done((bf16[2,256,1536]{2,1,0:T(8,128)(2,1)}, bf16[2,256,1536]{2,1,0:T(8,128)(2,1)S(1)}, u32[]{:S(2)}, u32[]{:S(2)}) %collective-permute-start.18) | collective-permute-done | bytes 1572896 | tf_op jit(solution)/shard_map/near3/ppermute | solution.py:71
  321.8 28.5 %experts.5 = (bf16[4,256,1536]{2,1,0:T(8,128)(2,1)}, bf16[4,256,1664]{2,1,0:T(8,128)(2,1)}, bf16[2,4,256,1664]{3,2,1,0:T(8,128)(2,1)}, bf16[2,2,352,1536]{3,2,1,...) custom-call(s32[10]{0:T(128)} %concatenate.76.info_ref, ...), custom_call_target="tpu_custom_call" | custom-call | flops 30000001024 | bytes 45000000 | tf_op jit(solution)/shard_map/experts/pallas_call | solution.py:372
  365.1 18.3 %collective-permute-done.21 = bf16[2,256,1536]{2,1,0:T(8,128)(2,1)S(1)} collective-permute-done((bf16[2,256,1536]{2,1,0:T(8,128)(2,1)}, bf16[2,256,1536]{2,1,0:T(8,128)(2,1)S(1)}, u32[]{:S(2)}, u32[]{:S(2)}) %collective-permute-start.21) | collective-permute-done | bytes 1572896 | tf_op jit(solution)/shard_map/near2/ppermute | solution.py:71
  391.2 28.6 %experts.6 = (bf16[4,256,1536]{2,1,0:T(8,128)(2,1)}, bf16[4,256,1664]{2,1,0:T(8,128)(2,1)}, bf16[2,4,256,1664]{3,2,1,0:T(8,128)(2,1)}, bf16[2,2,352,1536]{3,2,1,...) custom-call(s32[10]{0:T(128)} %concatenate.75.info_ref, ...), custom_call_target="tpu_custom_call" | custom-call | flops 30000001024 | bytes 45000000 | tf_op jit(solution)/shard_map/experts/pallas_call | solution.py:372
  452.2 28.8 %experts.7 = (bf16[4,256,1536]{2,1,0:T(8,128)(2,1)}, bf16[4,256,1664]{2,1,0:T(8,128)(2,1)}, bf16[2,4,256,1664]{3,2,1,0:T(8,128)(2,1)}, bf16[2,2,352,1536]{3,2,1,...) custom-call(s32[10]{0:T(128)} %concatenate.79.info_ref, ...), custom_call_target="tpu_custom_call" | custom-call | flops 30000001024 | bytes 45000000 | tf_op jit(solution)/shard_map/experts/pallas_call | solution.py:372
  487.8 11.5 %wgrad_part.1 = bf16[1536,384]{1,0:T(8,128)(2,1)} custom-call(bf16[2,2,352,1536]{3,2,1,0:T(8,128)(2,1)} %get-tuple-element.179.refs_0_, bf16[2,2,352,1536]{3,2,1,0:T(8,128)(2,1)} %get-tuple-element.162.refs_1_, bf16[2,2,352,1536]{3,2,1,0:T(8,128)(2,1)} %get-tuple-element.163.refs_2_, bf16[2,2,352,1536]{3,2,1,0:T(8,128)(2,1)} %get-tuple-element.164.refs_3_, ...), custom_call_target="tpu_custom_call" | custom-call | flops 1000000 | bytes 10000 | tf_op jit(solution)/shard_map/wgrad_part/pallas_call | solution.py:423
  509.1 15.1 %wgrad_full.1 = bf16[1536,1024]{1,0:T(8,128)(2,1)} custom-call(bf16[2,2,352,1536]{3,2,1,0:T(8,128)(2,1)} %get-tuple-element.179.refs_0_, bf16[2,2,352,1536]{3,2,1,0:T(8,128)(2,1)} %get-tuple-element.162.refs_1_, bf16[2,2,352,1536]{3,2,1,0:T(8,128)(2,1)} %get-tuple-element.163.refs_2_, bf16[2,2,352,1536]{3,2,1,0:T(8,128)(2,1)} %get-tuple-element.164.refs_3_, ...), custom_call_target="tpu_custom_call" | custom-call | flops 1000000 | bytes 10000 | tf_op jit(solution)/shard_map/wgrad_full/pallas_call | solution.py:423
  538.6 10.1 %wgrad_down.1 = bf16[1536,512]{1,0:T(8,128)(2,1)} custom-call(bf16[2,2,352,1536]{3,2,1,0:T(8,128)(2,1)} %get-tuple-element.185.refs_8_.refs_0_, bf16[2,2,352,1536]{3,2,1,0:T(8,128)(2,1)} %get-tuple-element.170.refs_9_.refs_1_, bf16[2,2,352,1536]{3,2,1,0:T(8,128)(2,1)} %get-tuple-element.171.refs_10_.refs_2_, ...), custom_call_target="tpu_custom_call" | custom-call | flops 1000000 | bytes 10000 | tf_op jit(solution)/shard_map/wgrad_down/pallas_call | solution.py:423
  557.2 17.0 %collective-permute-done.38 = bf16[256,1664]{1,0:T(8,128)(2,1)} collective-permute-done((bf16[256,1664]{1,0:T(8,128)(2,1)}, bf16[256,1664]{1,0:T(8,128)(2,1)}, u32[]{:S(2)}, u32[]{:S(2)}) %collective-permute-start.38) | collective-permute-done | bytes 852000 | tf_op jit(solution)/shard_map/home2/ppermute | solution.py:71
  589.5 14.7 %collective-permute-done.40.refs_4_ = bf16[256,1664]{1,0:T(8,128)(2,1)S(1)} collective-permute-done((bf16[256,1664]{1,0:T(8,128)(2,1)}, bf16[256,1664]{1,0:T(8,128)(2,1)S(1)}, u32[]{:S(2)}, u32[]{:S(2)}) %collective-permute-start.40) | collective-permute-done | bytes 852000 | tf_op jit(solution)/shard_map/home1/ppermute | solution.py:71
  606.0 7.5 residual_gradient.1
  648.8 14.5 %collective-permute-done.49 = bf16[2,256,1536]{2,1,0:T(8,128)(2,1)} collective-permute-done((bf16[2,256,1536]{2,1,0:T(8,128)(2,1)S(1)}, bf16[2,256,1536]{2,1,0:T(8,128)(2,1)}, u32[]{:S(2)}, u32[]{:S(2)}) %collective-permute-start.49) | collective-permute-done | bytes 1572896 | tf_op jit(solution)/shard_map/m_far2/ppermute | solution.py:71
  671.8 34.3 %attend_back.1 = (bf16[4,256,1536]{2,1,0:T(8,128)(2,1)}, bf16[1536,1024]{1,0:T(8,128)(2,1)}, f32[1,1536]{1,0:T(1,128)}) custom-call(s32[16]{0:T(128)} %concatenate.65.info_ref, bf16[4,256,1536]{2,1,0:T(8,128)(2,1)} %pad_maximum_fusion.6.da_ref, bf16[4,256,1536]{2,1,0:T(8,128)(2,1)} %pad_maximum_fusion.n1_ref, bf16[1536,1024]{1,0:T(8,128)(2,1)} %get-tuple-element.193.w_ref, ...), custom_call_target="tpu_custom_call" | custom-call | flops 1000000 | bytes 10000 | tf_op jit(solution)/shard_map/attend_back/pallas_call | solution.py:658
  723.7 12.2 %collective-permute-done.58 = f32[48,1536]{1,0:T(8,128)S(1)} collective-permute-done((f32[48,1536]{1,0:T(8,128)S(1)}, f32[48,1536]{1,0:T(8,128)S(1)}, u32[]{:S(2)}, u32[]{:S(2)}) %collective-permute-start.58) | collective-permute-done | bytes 294944 | tf_op jit(solution)/shard_map/small/ppermute | solution.py:71
  747.7 7.5 collective-permute-done.51
  766.9 28.4 %all-to-all-done.4.full_ref = bf16[8,192,1024]{2,1,0:T(8,128)(2,1)} async-done(((bf16[8,192,1024]{2,1,0:T(8,128)(2,1)}), bf16[8,192,1024]{2,1,0:T(8,128)(2,1)}, u32[]{:S(2)}, u32[]{:S(2)}) %all-to-all-start.4) | async-done | bytes 3145760 | tf_op jit(solution)/shard_map/all_to_all | solution.py:785
  826.6 8.6 collective-permute-done.59
  840.1 9.2 %unpack_experts.1 = (f32[10,192,1024]{2,1,0:T(8,128)}, f32[10,192,512]{2,1,0:T(8,128)}) custom-call(bf16[8,192,1024]{2,1,0:T(8,128)(2,1)} %all-to-all-done.4.full_ref, bf16[8,192,512]{2,1,0:T(8,128)(2,1)} %all-to-all-done.3.down_ref, bf16[8,192,384]{2,1,0:T(8,128)(2,1)} %all-to-all-done.2.part_ref), custom_call_target="tpu_custom_call" | custom-call | tf_op jit(solution)/shard_map/unpack_experts/pallas_call | solution.py:235
  (326 shorter events, 321.5 us)
Async XLA Ops:
  14.1 31.9 %collective-permute-start.1 = (bf16[208,1024]{1,0:T(8,128)(2,1)S(1)}, bf16[208,1024]{1,0:T(8,128)(2,1)S(1)}, u32[]{:S(2)}, u32[]{:S(2)}) collective-permute-start(bf16[208,1024]{1,0:T(8,128)(2,1)S(1)} %get-tuple-element.227), channel_id=1, source_target_pairs={{0,16},{1,17},{2,18},{3,19},{4,20},{5,21},{6,22},{7,23},{8,24},{9,... | collective-permute-start | bytes 1277960 | tf_op jit(solution)/shard_map/pieces/ppermute | solution.py:71
  16.7 29.3 %collective-permute-start.2 = (bf16[208,1024]{1,0:T(8,128)(2,1)S(1)}, bf16[208,1024]{1,0:T(8,128)(2,1)S(1)}, u32[]{:S(2)}, u32[]{:S(2)}) collective-permute-start(bf16[208,1024]{1,0:T(8,128)(2,1)S(1)} %get-tuple-element.227), channel_id=1, source_target_pairs={{0,24},{1,25},{2,26},{3,27},{4,28},{5,29},{6,30},{7,31},{8,16},{9,... | collective-permute-start | bytes 1277960 | tf_op jit(solution)/shard_map/pieces/ppermute | solution.py:71
  46.3 74.0 %all-to-all-start = ((bf16[8,192,896]{2,1,0:T(8,128)(2,1)}), bf16[8,192,896]{2,1,0:T(8,128)(2,1)}, u32[]{:S(2)}, u32[]{:S(2)}) async-start(bf16[8,192,896]{2,1,0:T(8,128)(2,1)} %pack_experts.1), calls=%async_computation | async-start | bytes 5505024 | tf_op jit(solution)/shard_map/all_to_all | solution.py:785
  96.6 35.1 %collective-permute-start.7 = (bf16[4,208,1024]{2,1,0:T(8,128)(2,1)S(1)}, bf16[4,208,1024]{2,1,0:T(8,128)(2,1)}, u32[]{:S(2)}, u32[]{:S(2)}) collective-permute-start(bf16[4,208,1024]{2,1,0:T(8,128)(2,1)S(1)} %pad_maximum_fusion.9.refs_0_), channel_id=1, source_target_pairs={{0,4},{1,5},{2,6},{3,7},{4,0},{5,1},{6,2},{7,3},{8,12},{9,13},{10,... | collective-permute-start | bytes 5111816 | tf_op jit(solution)/shard_map/pieces_theirs/ppermute | solution.py:71
  120.3 76.2 %all-to-all-start.1 = ((bf16[8,192,1024]{2,1,0:T(8,128)(2,1)}), bf16[8,192,1024]{2,1,0:T(8,128)(2,1)}, u32[]{:S(2)}, u32[]{:S(2)}) async-start(bf16[8,192,1024]{2,1,0:T(8,128)(2,1)} %slice.229), calls=%async_computation.1 | async-start | bytes 6291456 | tf_op jit(solution)/shard_map/all_to_all | solution.py:785
  179.4 57.7 %collective-permute-start.14 = (bf16[4,256,1536]{2,1,0:T(8,128)(2,1)}, bf16[4,256,1536]{2,1,0:T(8,128)(2,1)}, u32[]{:S(2)}, u32[]{:S(2)}) collective-permute-start(bf16[4,256,1536]{2,1,0:T(8,128)(2,1)} %pad_maximum_fusion.3.ya_ref), channel_id=1, source_target_pairs={{0,4},{1,5},{2,6},{3,7},{4,0},{5,1},{6,2},{7,3},{8,12},{9,13},{10,... | collective-permute-start | bytes 9437192 | tf_op jit(solution)/shard_map/y_theirs0/ppermute | solution.py:71
  196.7 36.9 %collective-permute-start.10 = (bf16[2,256,1536]{2,1,0:T(8,128)(2,1)S(1)}, bf16[2,256,1536]{2,1,0:T(8,128)(2,1)S(1)}, u32[]{:S(2)}, u32[]{:S(2)}) collective-permute-start(bf16[2,256,1536]{2,1,0:T(8,128)(2,1)S(1)} %pad_maximum_fusion.8), channel_id=1, source_target_pairs={{0,8},{1,9},{2,10},{3,11},{4,12},{5,13},{6,14},{7,15},{8,24},{9,25... | collective-permute-start | bytes 4718600 | tf_op jit(solution)/shard_map/both1/ppermute | solution.py:71
  254.3 37.4 %collective-permute-start.19 = (bf16[2,2,256,1536]{3,2,1,0:T(8,128)(2,1)S(1)}, bf16[2,2,256,1536]{3,2,1,0:T(8,128)(2,1)}, u32[]{:S(2)}, u32[]{:S(2)}) collective-permute-start(bf16[2,2,256,1536]{3,2,1,0:T(8,128)(2,1)S(1)} %pad_maximum_fusion.1), channel_id=1, source_target_pairs={{0,2},{1,3},{2,0},{3,1},{4,5},{5,4},{6,7},{7,6},{8,10},{9,11},{10,... | collective-permute-start | bytes 9437192 | tf_op jit(solution)/shard_map/far1/ppermute | solution.py:71
  259.0 38.4 %collective-permute-start.17 = (bf16[2,256,1536]{2,1,0:T(8,128)(2,1)}, bf16[2,256,1536]{2,1,0:T(8,128)(2,1)}, u32[]{:S(2)}, u32[]{:S(2)}) collective-permute-start(bf16[2,256,1536]{2,1,0:T(8,128)(2,1)} %copy-done.32), channel_id=1, source_target_pairs={{8,0},{9,1},{10,2},{11,3},{12,4},{13,5},{14,6},{15,7},{24,8},{25,9... | collective-permute-start | bytes 4718600 | tf_op jit(solution)/shard_map/both3/ppermute | solution.py:71
  319.7 37.4 %collective-permute-start.23 = (bf16[2,2,256,1536]{3,2,1,0:T(8,128)(2,1)S(1)}, bf16[2,2,256,1536]{3,2,1,0:T(8,128)(2,1)}, u32[]{:S(2)}, u32[]{:S(2)}) collective-permute-start(bf16[2,2,256,1536]{3,2,1,0:T(8,128)(2,1)S(1)} %pad_maximum_fusion.4), channel_id=1, source_target_pairs={{0,2},{1,3},{2,0},{3,1},{4,5},{5,4},{6,7},{7,6},{8,10},{9,11},{10,... | collective-permute-start | bytes 9437192 | tf_op jit(solution)/shard_map/far3/ppermute | solution.py:71
  321.8 40.9 %collective-permute-start.16 = (bf16[2,256,1536]{2,1,0:T(8,128)(2,1)}, bf16[2,256,1536]{2,1,0:T(8,128)(2,1)}, u32[]{:S(2)}, u32[]{:S(2)}) collective-permute-start(bf16[2,256,1536]{2,1,0:T(8,128)(2,1)} %copy-done.34), channel_id=1, source_target_pairs={{0,8},{1,9},{2,10},{3,11},{4,12},{5,13},{6,14},{7,15},{8,24},{9,25... | collective-permute-start | bytes 4718600 | tf_op jit(solution)/shard_map/both2/ppermute | solution.py:71
  321.8 43.2 %collective-permute-start.22 = (bf16[2,4,256,1664]{3,2,1,0:T(8,128)(2,1)}, bf16[2,4,256,1664]{3,2,1,0:T(8,128)(2,1)}, u32[]{:S(2)}, u32[]{:S(2)}) collective-permute-start(bf16[2,4,256,1664]{3,2,1,0:T(8,128)(2,1)} %get-tuple-element.140), channel_id=1, source_target_pairs={{0,4},{1,5},{2,6},{3,7},{4,0},{5,1},{6,2},{7,3},{8,12},{9,13},{10,... | collective-permute-start | bytes 20447240 | tf_op jit(solution)/shard_map/swap0/ppermute | solution.py:71
  362.7 28.5 %collective-permute-start.24 = (bf16[4,2,256,1536]{3,2,1,0:T(8,128)(2,1)}, bf16[4,2,256,1536]{3,2,1,0:T(8,128)(2,1)}, u32[]{:S(2)}, u32[]{:S(2)}) collective-permute-start(bf16[4,2,256,1536]{3,2,1,0:T(8,128)(2,1)} %constant_dynamic-update-slice_fusion.2.xa_ref.ya_ref), channel_id=1, source_target_pairs={{0,4},{1,5},{2,6},{3,7},{4,0},{5,1},{6,2},{7,3},{8,12},{9,13},{10,... | collective-permute-start | bytes 18874376 | tf_op jit(solution)/shard_map/theirs3/ppermute | solution.py:71
  364.8 68.3 %collective-permute-start.26 = (bf16[2,4,256,1664]{3,2,1,0:T(8,128)(2,1)}, bf16[2,4,256,1664]{3,2,1,0:T(8,128)(2,1)}, u32[]{:S(2)}, u32[]{:S(2)}) collective-permute-start(bf16[2,4,256,1664]{3,2,1,0:T(8,128)(2,1)} %get-tuple-element.154), channel_id=1, source_target_pairs={{0,4},{1,5},{2,6},{3,7},{4,0},{5,1},{6,2},{7,3},{8,12},{9,13},{10,... | collective-permute-start | bytes 20447240 | tf_op jit(solution)/shard_map/swap1/ppermute | solution.py:71
  386.9 37.6 %collective-permute-start.25 = (bf16[2,2,256,1536]{3,2,1,0:T(8,128)(2,1)}, bf16[2,2,256,1536]{3,2,1,0:T(8,128)(2,1)}, u32[]{:S(2)}, u32[]{:S(2)}) collective-permute-start(bf16[2,2,256,1536]{3,2,1,0:T(8,128)(2,1)} %pad_maximum_fusion.5), channel_id=1, source_target_pairs={{0,2},{1,3},{2,0},{3,1},{4,5},{5,4},{6,7},{7,6},{8,10},{9,11},{10,... | collective-permute-start | bytes 9437192 | tf_op jit(solution)/shard_map/far2/ppermute | solution.py:71
  438.3 42.7 %collective-permute-start.29 = (bf16[2,256,1664]{2,1,0:T(8,128)(2,1)}, bf16[2,256,1664]{2,1,0:T(8,128)(2,1)}, u32[]{:S(2)}, u32[]{:S(2)}) collective-permute-start(bf16[2,256,1664]{2,1,0:T(8,128)(2,1)} %slice.309), channel_id=1, source_target_pairs={{0,2},{1,3},{2,0},{3,1},{4,5},{5,4},{6,7},{7,6},{8,10},{9,11},{10,... | collective-permute-start | bytes 5111816 | tf_op jit(solution)/shard_map/d_far1/ppermute | solution.py:71
  449.2 31.8 %collective-permute-start.30 = (bf16[2,256,1664]{2,1,0:T(8,128)(2,1)}, bf16[2,256,1664]{2,1,0:T(8,128)(2,1)}, u32[]{:S(2)}, u32[]{:S(2)}) collective-permute-start(bf16[2,256,1664]{2,1,0:T(8,128)(2,1)} %slice.312), channel_id=1, source_target_pairs={{0,2},{1,3},{2,0},{3,1},{4,5},{5,4},{6,7},{7,6},{8,10},{9,11},{10,... | collective-permute-start | bytes 5111816 | tf_op jit(solution)/shard_map/d_far3/ppermute | solution.py:71
  531.6 51.9 %all-to-all-start.2 = ((bf16[8,192,384]{2,1,0:T(8,128)(2,1)}), bf16[8,192,384]{2,1,0:T(8,128)(2,1)}, u32[]{:S(2)}, u32[]{:S(2)}) async-start(bf16[8,192,384]{2,1,0:T(8,128)(2,1)} %bitcast.216), calls=%async_computation.2 | async-start | bytes 2359296 | tf_op jit(solution)/shard_map/all_to_all | solution.py:785
  548.7 34.8 %collective-permute-start.36 = (bf16[2,256,1664]{2,1,0:T(8,128)(2,1)}, bf16[2,256,1664]{2,1,0:T(8,128)(2,1)}, u32[]{:S(2)}, u32[]{:S(2)}) collective-permute-start(bf16[2,256,1664]{2,1,0:T(8,128)(2,1)} %slice.306), channel_id=1, source_target_pairs={{0,2},{1,3},{2,0},{3,1},{4,5},{5,4},{6,7},{7,6},{8,10},{9,11},{10,... | collective-permute-start | bytes 5111816 | tf_op jit(solution)/shard_map/d_far0/ppermute | solution.py:71
  614.9 48.3 %all-to-all-start.3 = ((bf16[8,192,512]{2,1,0:T(8,128)(2,1)}), bf16[8,192,512]{2,1,0:T(8,128)(2,1)}, u32[]{:S(2)}, u32[]{:S(2)}) async-start(bf16[8,192,512]{2,1,0:T(8,128)(2,1)} %bitcast.87), calls=%async_computation.3 | async-start | bytes 3145728 | tf_op jit(solution)/shard_map/all_to_all | solution.py:785
  629.3 34.0 %collective-permute-start.49 = (bf16[2,256,1536]{2,1,0:T(8,128)(2,1)S(1)}, bf16[2,256,1536]{2,1,0:T(8,128)(2,1)}, u32[]{:S(2)}, u32[]{:S(2)}) collective-permute-start(bf16[2,256,1536]{2,1,0:T(8,128)(2,1)S(1)} %slice.341), channel_id=1, source_target_pairs={{0,2},{1,3},{2,0},{3,1},{4,5},{5,4},{6,7},{7,6},{8,10},{9,11},{10,... | collective-permute-start | bytes 4718600 | tf_op jit(solution)/shard_map/m_far2/ppermute | solution.py:71
  636.2 72.9 %collective-permute-start.44 = (bf16[2,256,1536]{2,1,0:T(8,128)(2,1)}, bf16[2,256,1536]{2,1,0:T(8,128)(2,1)}, u32[]{:S(2)}, u32[]{:S(2)}) collective-permute-start(bf16[2,256,1536]{2,1,0:T(8,128)(2,1)} %slice.327), channel_id=1, source_target_pairs={{0,2},{1,3},{2,0},{3,1},{4,5},{5,4},{6,7},{7,6},{8,10},{9,11},{10,... | collective-permute-start | bytes 4718600 | tf_op jit(solution)/shard_map/m_far1/ppermute | solution.py:71
  648.2 60.9 %collective-permute-start.43 = (bf16[2,256,1536]{2,1,0:T(8,128)(2,1)}, bf16[2,256,1536]{2,1,0:T(8,128)(2,1)}, u32[]{:S(2)}, u32[]{:S(2)}) collective-permute-start(bf16[2,256,1536]{2,1,0:T(8,128)(2,1)} %slice.325), channel_id=1, source_target_pairs={{0,2},{1,3},{2,0},{3,1},{4,5},{5,4},{6,7},{7,6},{8,10},{9,11},{10,... | collective-permute-start | bytes 4718600 | tf_op jit(solution)/shard_map/m_far3/ppermute | solution.py:71
  663.3 132.0 %all-to-all-start.4 = ((bf16[8,192,1024]{2,1,0:T(8,128)(2,1)}), bf16[8,192,1024]{2,1,0:T(8,128)(2,1)}, u32[]{:S(2)}, u32[]{:S(2)}) async-start(bf16[8,192,1024]{2,1,0:T(8,128)(2,1)} %bitcast.210), calls=%async_computation.5 | async-start | bytes 6291456 | tf_op jit(solution)/shard_map/all_to_all | solution.py:785
  667.8 142.1 %reduce-scatter.2.cloned.1.call-start = ((), (), s32[]{:S(2)}) async-start(), calls=%async_computation.6 | async-start | bytes 3538944 | tf_op jit(solution)/shard_map/reduce_scatter | solution.py:949
  670.3 42.1 %collective-permute-start.50 = (bf16[256,1536]{1,0:T(8,128)(2,1)}, bf16[256,1536]{1,0:T(8,128)(2,1)}, u32[]{:S(2)}, u32[]{:S(2)}) collective-permute-start(bf16[256,1536]{1,0:T(8,128)(2,1)} %fusion.39), channel_id=1, source_target_pairs={{0,1},{1,0},{2,3},{3,2},{4,6},{5,7},{6,4},{7,5},{8,9},{9,8},{10,11... | collective-permute-start | bytes 2359304 | tf_op jit(solution)/shard_map/m_near2/ppermute | solution.py:71
  709.1 26.8 %collective-permute-start.45 = (bf16[2,256,1536]{2,1,0:T(8,128)(2,1)S(1)}, bf16[2,256,1536]{2,1,0:T(8,128)(2,1)S(1)}, u32[]{:S(2)}, u32[]{:S(2)}) collective-permute-start(bf16[2,256,1536]{2,1,0:T(8,128)(2,1)S(1)} %slice.261), channel_id=1, source_target_pairs={{0,2},{1,3},{2,0},{3,1},{4,5},{5,4},{6,7},{7,6},{8,10},{9,11},{10,... | collective-permute-start | bytes 4718600 | tf_op jit(solution)/shard_map/parts_far/ppermute | solution.py:71
  714.3 40.9 %collective-permute-start.51 = (bf16[256,1536]{1,0:T(8,128)(2,1)S(1)}, bf16[256,1536]{1,0:T(8,128)(2,1)S(1)}, u32[]{:S(2)}, u32[]{:S(2)}) collective-permute-start(bf16[256,1536]{1,0:T(8,128)(2,1)S(1)} %fusion.24), channel_id=1, source_target_pairs={{8,0},{9,1},{10,2},{11,3},{12,4},{13,5},{14,6},{15,7},{24,8},{25,9... | collective-permute-start | bytes 2359304 | tf_op jit(solution)/shard_map/m_home2/ppermute | solution.py:71
  740.7 58.6 %collective-permute-start.46 = (bf16[2,256,1536]{2,1,0:T(8,128)(2,1)}, bf16[2,256,1536]{2,1,0:T(8,128)(2,1)}, u32[]{:S(2)}, u32[]{:S(2)}) collective-permute-start(bf16[2,256,1536]{2,1,0:T(8,128)(2,1)} %slice.331), channel_id=1, source_target_pairs={{0,2},{1,3},{2,0},{3,1},{4,5},{5,4},{6,7},{7,6},{8,10},{9,11},{10,... | collective-permute-start | bytes 4718600 | tf_op jit(solution)/shard_map/m_far0/ppermute | solution.py:71
  744.9 52.4 %collective-permute-start.55 = (bf16[256,1536]{1,0:T(8,128)(2,1)}, bf16[256,1536]{1,0:T(8,128)(2,1)}, u32[]{:S(2)}, u32[]{:S(2)}) collective-permute-start(bf16[256,1536]{1,0:T(8,128)(2,1)} %fusion.41), channel_id=1, source_target_pairs={{0,1},{1,0},{2,3},{3,2},{4,6},{5,7},{6,4},{7,5},{8,9},{9,8},{10,11... | collective-permute-start | bytes 2359304 | tf_op jit(solution)/shard_map/parts_near/ppermute | solution.py:71
  764.1 72.4 %collective-permute-start.52 = (bf16[256,1536]{1,0:T(8,128)(2,1)}, bf16[256,1536]{1,0:T(8,128)(2,1)}, u32[]{:S(2)}, u32[]{:S(2)}) collective-permute-start(bf16[256,1536]{1,0:T(8,128)(2,1)} %fusion.26), channel_id=1, source_target_pairs={{8,0},{9,1},{10,2},{11,3},{12,4},{13,5},{14,6},{15,7},{24,8},{25,9... | collective-permute-start | bytes 2359304 | tf_op jit(solution)/shard_map/m_home1/ppermute | solution.py:71
  809.8 26.7 %collective-permute-start.54 = (bf16[256,1536]{1,0:T(8,128)(2,1)}, bf16[256,1536]{1,0:T(8,128)(2,1)}, u32[]{:S(2)}, u32[]{:S(2)}) collective-permute-start(bf16[256,1536]{1,0:T(8,128)(2,1)} %fusion.23), channel_id=1, source_target_pairs={{0,8},{1,9},{2,10},{3,11},{4,12},{5,13},{6,14},{7,15},{8,24},{9,25... | collective-permute-start | bytes 2359304 | tf_op jit(solution)/shard_map/m_home3/ppermute | solution.py:71
  (85 other events, 1446.3 us)
Sparse Core Ops, SparseCore 0:
  707.7 93.5 reduce-scatter.1

commit v4 on v3

--- a/solution.py
+++ b/solution.py
@@ -964,7 +964,7 @@
     else:
         out = links.scatter_group([(d[0], d[2][1, ..., :width]) for d in done])
     expert_in_grad, expert_out_grad = unpack_experts(after(got_full, *before), got_down, got_part, experts, group)
-    small = links.sum_all(small, *before)
+    small = links.sum_all(small, *([n_parts[2], m_home1] if fast else []))
     layer_output = (residual + total_of(out)).astype(BF)
 
     unit = rms_unit(inputs)

time: 866 us -> 861 us (level)
    ppermute x61, waiting for transfers between devices: 307 us -> 326 us  [send(): return lax.ppermute(value, ('dp', 'tensor'), perm)]
    all_to_all x5, waiting for transfers between devices: 55.9 us -> 36.8 us  [shards(): to_all = lambda a: lax.all_to_all(a, 'dp', 0, 0)]
where the time goes in v4:
time: 861 us; the launch traced here: 856 us
  waiting for transfers between devices  363 us (42%)
  Pallas kernels  231 us (27%)
  other arithmetic  96.7 us (11%)
  starting transfers between devices  90.4 us (10%)
  local copies, waits for them, and re-layouts  59.5 us (7%)
  between operations  15.3 us (2%)
    ppermute x61, waiting for transfers between devices, send(): return lax.ppermute(value, ('dp', 'tensor'), perm)  326 us
    pallas_call x4, Pallas kernels, expert_chunk(): pl.pallas_call(expert_kernel, grid_spec=pltpu.PrefetchScalarGridSpec(num_...  115 us
    ppermute x61, starting transfers between devices, send(): return lax.ppermute(value, ('dp', 'tensor'), perm)  61.8 us
    convert_element_type x18, other arithmetic, add(): return (a.astype(F32) + b.astype(F32)).astype(a.dtype)  42.3 us
    all_to_all x5, waiting for transfers between devices, shards(): to_all = lambda a: lax.all_to_all(a, 'dp', 0, 0)  36.8 us
    pallas_call x3, Pallas kernels, expert_wgrad(): pl.pallas_call(functools.partial(wgrad_kernel, chunks, len(pairs)), grid=...  36.7 us
    pallas_call x1, Pallas kernels, attend_backward(): pl.pallas_call(functools.partial(attend_back_kernel, heads, blocks, seqs)...  34.3 us
    all_to_all x5, starting transfers between devices, shards(): to_all = lambda a: lax.all_to_all(a, 'dp', 0, 0)  28.5 us
  transfers between devices with their start and end apart: 67, of which 37 were waited for; matrix products, arithmetic and copies ran while one was open for 17% of the time, Pallas kernels for 26%

profile of v4, /device:TPU:0, one launch (start us, length us, event | category | flops | bytes accessed | tf_op | source)
XLA Modules:
  0.0 855.8 jit_solution(10175430238814616298)
XLA Ops:
  22.9 9.4 %collective-permute-done = bf16[208,1024]{1,0:T(8,128)(2,1)S(1)} collective-permute-done((bf16[208,1024]{1,0:T(8,128)(2,1)S(1)}, bf16[208,1024]{1,0:T(8,128)(2,1)S(1)}, u32[]{:S(2)}, u32[]{:S(2)}) %collective-permute-start) | collective-permute-done | bytes 426016 | tf_op jit(solution)/shard_map/pieces/ppermute | solution.py:71
  32.3 13.7 %collective-permute-done.1 = bf16[208,1024]{1,0:T(8,128)(2,1)S(1)} collective-permute-done((bf16[208,1024]{1,0:T(8,128)(2,1)S(1)}, bf16[208,1024]{1,0:T(8,128)(2,1)S(1)}, u32[]{:S(2)}, u32[]{:S(2)}) %collective-permute-start.1) | collective-permute-done | bytes 426016 | tf_op jit(solution)/shard_map/pieces/ppermute | solution.py:71
  46.3 10.8 %all-to-all-start = ((bf16[8,192,896]{2,1,0:T(8,128)(2,1)}), bf16[8,192,896]{2,1,0:T(8,128)(2,1)}, u32[]{:S(2)}, u32[]{:S(2)}) async-start(bf16[8,192,896]{2,1,0:T(8,128)(2,1)} %pack_experts.1), calls=%async_computation | async-start | bytes 5505024 | tf_op jit(solution)/shard_map/all_to_all | solution.py:785
  60.1 10.2 %collective-permute-done.3 = bf16[256,1536]{1,0:T(8,128)(2,1)S(1)} collective-permute-done((bf16[256,1536]{1,0:T(8,128)(2,1)S(1)}, bf16[256,1536]{1,0:T(8,128)(2,1)S(1)}, u32[]{:S(2)}, u32[]{:S(2)}) %collective-permute-start.3) | collective-permute-done | bytes 786464 | tf_op jit(solution)/shard_map/near/ppermute | solution.py:71
  72.0 18.9 %collective-permute-done.4 = bf16[2,256,1536]{2,1,0:T(8,128)(2,1)S(1)} collective-permute-done((bf16[2,256,1536]{2,1,0:T(8,128)(2,1)S(1)}, bf16[2,256,1536]{2,1,0:T(8,128)(2,1)S(1)}, u32[]{:S(2)}, u32[]{:S(2)}) %collective-permute-start.4) | collective-permute-done | bytes 1572896 | tf_op jit(solution)/shard_map/far/ppermute | solution.py:71
  107.0 13.3 %all-to-all-done = bf16[8,192,896]{2,1,0:T(8,128)(2,1)} async-done(((bf16[8,192,896]{2,1,0:T(8,128)(2,1)}), bf16[8,192,896]{2,1,0:T(8,128)(2,1)}, u32[]{:S(2)}, u32[]{:S(2)}) %all-to-all-start) | async-done | bytes 2752544 | tf_op jit(solution)/shard_map/all_to_all | solution.py:785
  131.6 20.3 %attend.1 = (bf16[4,256,1536]{2,1,0:T(8,128)(2,1)}, bf16[1024,640]{1,0:T(8,128)(2,1)}, bf16[1024,384]{1,0:T(8,128)(2,1)}, f32[1024,128]{1,0:T(8,128)}, bf16[1536,1024]{1,0:T(8,128)(2,1)}) custom-call(s32[16]{0:T(128)} %concatenate.65.info_ref, bf16[4,256,1536]{2,1,0:T(8,128)(2,1)} %pad_maximum_fusion.n1_ref, f32[1024,128]{1,0:T(8,128)} %get-tuple-element.241.cos_ref, ...), custom_call_target="tpu_custom_call" | custom-call | flops 1000000 | bytes 10000 | tf_op jit(solution)/shard_map/attend/pallas_call | solution.py:529
  155.2 18.9 %collective-permute-done.8 = bf16[2,256,1536]{2,1,0:T(8,128)(2,1)S(1)} collective-permute-done((bf16[2,256,1536]{2,1,0:T(8,128)(2,1)S(1)}, bf16[2,256,1536]{2,1,0:T(8,128)(2,1)S(1)}, u32[]{:S(2)}, u32[]{:S(2)}) %collective-permute-start.8) | collective-permute-done | bytes 1572896 | tf_op jit(solution)/shard_map/h_far/ppermute | solution.py:71
  188.3 8.2 all-to-all-done.1
  198.3 10.5 %collective-permute-done.12 = bf16[256,1536]{1,0:T(8,128)(2,1)S(1)} collective-permute-done((bf16[256,1536]{1,0:T(8,128)(2,1)S(1)}, bf16[256,1536]{1,0:T(8,128)(2,1)S(1)}, u32[]{:S(2)}, u32[]{:S(2)}) %collective-permute-start.12) | collective-permute-done | bytes 786464 | tf_op jit(solution)/shard_map/near0/ppermute | solution.py:71
  210.6 23.0 %collective-permute-done.10 = bf16[2,256,1536]{2,1,0:T(8,128)(2,1)S(1)} collective-permute-done((bf16[2,256,1536]{2,1,0:T(8,128)(2,1)S(1)}, bf16[2,256,1536]{2,1,0:T(8,128)(2,1)S(1)}, u32[]{:S(2)}, u32[]{:S(2)}) %collective-permute-start.10) | collective-permute-done | bytes 1572896 | tf_op jit(solution)/shard_map/both1/ppermute | solution.py:71
  237.1 16.9 %collective-permute-done.11 = bf16[2,256,1536]{2,1,0:T(8,128)(2,1)S(1)} collective-permute-done((bf16[2,256,1536]{2,1,0:T(8,128)(2,1)S(1)}, bf16[2,256,1536]{2,1,0:T(8,128)(2,1)S(1)}, u32[]{:S(2)}, u32[]{:S(2)}) %collective-permute-start.11) | collective-permute-done | bytes 1572896 | tf_op jit(solution)/shard_map/near1/ppermute | solution.py:71
  260.0 28.8 %experts.4 = (bf16[4,256,1536]{2,1,0:T(8,128)(2,1)}, bf16[4,256,1664]{2,1,0:T(8,128)(2,1)}, bf16[2,4,256,1664]{3,2,1,0:T(8,128)(2,1)}, bf16[2,2,352,1536]{3,2,1,...) custom-call(s32[10]{0:T(128)} %concatenate.70.info_ref, ...), custom_call_target="tpu_custom_call" | custom-call | flops 30000001024 | bytes 45000000 | tf_op jit(solution)/shard_map/experts/pallas_call | solution.py:372
  298.8 19.1 %collective-permute-done.18 = bf16[2,256,1536]{2,1,0:T(8,128)(2,1)S(1)} collective-permute-done((bf16[2,256,1536]{2,1,0:T(8,128)(2,1)}, bf16[2,256,1536]{2,1,0:T(8,128)(2,1)S(1)}, u32[]{:S(2)}, u32[]{:S(2)}) %collective-permute-start.18) | collective-permute-done | bytes 1572896 | tf_op jit(solution)/shard_map/near3/ppermute | solution.py:71
  321.9 28.5 %experts.5 = (bf16[4,256,1536]{2,1,0:T(8,128)(2,1)}, bf16[4,256,1664]{2,1,0:T(8,128)(2,1)}, bf16[2,4,256,1664]{3,2,1,0:T(8,128)(2,1)}, bf16[2,2,352,1536]{3,2,1,...) custom-call(s32[10]{0:T(128)} %concatenate.76.info_ref, ...), custom_call_target="tpu_custom_call" | custom-call | flops 30000001024 | bytes 45000000 | tf_op jit(solution)/shard_map/experts/pallas_call | solution.py:372
  365.2 18.2 %collective-permute-done.21 = bf16[2,256,1536]{2,1,0:T(8,128)(2,1)S(1)} collective-permute-done((bf16[2,256,1536]{2,1,0:T(8,128)(2,1)}, bf16[2,256,1536]{2,1,0:T(8,128)(2,1)S(1)}, u32[]{:S(2)}, u32[]{:S(2)}) %collective-permute-start.21) | collective-permute-done | bytes 1572896 | tf_op jit(solution)/shard_map/near2/ppermute | solution.py:71
  391.2 28.6 %experts.6 = (bf16[4,256,1536]{2,1,0:T(8,128)(2,1)}, bf16[4,256,1664]{2,1,0:T(8,128)(2,1)}, bf16[2,4,256,1664]{3,2,1,0:T(8,128)(2,1)}, bf16[2,2,352,1536]{3,2,1,...) custom-call(s32[10]{0:T(128)} %concatenate.75.info_ref, ...), custom_call_target="tpu_custom_call" | custom-call | flops 30000001024 | bytes 45000000 | tf_op jit(solution)/shard_map/experts/pallas_call | solution.py:372
  452.2 28.8 %experts.7 = (bf16[4,256,1536]{2,1,0:T(8,128)(2,1)}, bf16[4,256,1664]{2,1,0:T(8,128)(2,1)}, bf16[2,4,256,1664]{3,2,1,0:T(8,128)(2,1)}, bf16[2,2,352,1536]{3,2,1,...) custom-call(s32[10]{0:T(128)} %concatenate.79.info_ref, ...), custom_call_target="tpu_custom_call" | custom-call | flops 30000001024 | bytes 45000000 | tf_op jit(solution)/shard_map/experts/pallas_call | solution.py:372
  487.8 11.5 %wgrad_part.1 = bf16[1536,384]{1,0:T(8,128)(2,1)} custom-call(bf16[2,2,352,1536]{3,2,1,0:T(8,128)(2,1)} %get-tuple-element.179.refs_0_, bf16[2,2,352,1536]{3,2,1,0:T(8,128)(2,1)} %get-tuple-element.162.refs_1_, bf16[2,2,352,1536]{3,2,1,0:T(8,128)(2,1)} %get-tuple-element.163.refs_2_, bf16[2,2,352,1536]{3,2,1,0:T(8,128)(2,1)} %get-tuple-element.164.refs_3_, ...), custom_call_target="tpu_custom_call" | custom-call | flops 1000000 | bytes 10000 | tf_op jit(solution)/shard_map/wgrad_part/pallas_call | solution.py:423
  509.1 15.1 %wgrad_full.1 = bf16[1536,1024]{1,0:T(8,128)(2,1)} custom-call(bf16[2,2,352,1536]{3,2,1,0:T(8,128)(2,1)} %get-tuple-element.179.refs_0_, bf16[2,2,352,1536]{3,2,1,0:T(8,128)(2,1)} %get-tuple-element.162.refs_1_, bf16[2,2,352,1536]{3,2,1,0:T(8,128)(2,1)} %get-tuple-element.163.refs_2_, bf16[2,2,352,1536]{3,2,1,0:T(8,128)(2,1)} %get-tuple-element.164.refs_3_, ...), custom_call_target="tpu_custom_call" | custom-call | flops 1000000 | bytes 10000 | tf_op jit(solution)/shard_map/wgrad_full/pallas_call | solution.py:423
  538.6 10.1 %wgrad_down.1 = bf16[1536,512]{1,0:T(8,128)(2,1)} custom-call(bf16[2,2,352,1536]{3,2,1,0:T(8,128)(2,1)} %get-tuple-element.185.refs_8_.refs_0_, bf16[2,2,352,1536]{3,2,1,0:T(8,128)(2,1)} %get-tuple-element.170.refs_9_.refs_1_, bf16[2,2,352,1536]{3,2,1,0:T(8,128)(2,1)} %get-tuple-element.171.refs_10_.refs_2_, ...), custom_call_target="tpu_custom_call" | custom-call | flops 1000000 | bytes 10000 | tf_op jit(solution)/shard_map/wgrad_down/pallas_call | solution.py:423
  557.2 17.0 %collective-permute-done.38 = bf16[256,1664]{1,0:T(8,128)(2,1)} collective-permute-done((bf16[256,1664]{1,0:T(8,128)(2,1)}, bf16[256,1664]{1,0:T(8,128)(2,1)}, u32[]{:S(2)}, u32[]{:S(2)}) %collective-permute-start.38) | collective-permute-done | bytes 852000 | tf_op jit(solution)/shard_map/home2/ppermute | solution.py:71
  589.5 14.7 %collective-permute-done.40.refs_4_ = bf16[256,1664]{1,0:T(8,128)(2,1)S(1)} collective-permute-done((bf16[256,1664]{1,0:T(8,128)(2,1)}, bf16[256,1664]{1,0:T(8,128)(2,1)S(1)}, u32[]{:S(2)}, u32[]{:S(2)}) %collective-permute-start.40) | collective-permute-done | bytes 852000 | tf_op jit(solution)/shard_map/home1/ppermute | solution.py:71
  606.0 7.5 residual_gradient.1
  648.8 14.4 %collective-permute-done.49 = bf16[2,256,1536]{2,1,0:T(8,128)(2,1)S(1)} collective-permute-done((bf16[2,256,1536]{2,1,0:T(8,128)(2,1)S(1)}, bf16[2,256,1536]{2,1,0:T(8,128)(2,1)S(1)}, u32[]{:S(2)}, u32[]{:S(2)}) %collective-permute-start.49) | collective-permute-done | bytes 1572896 | tf_op jit(solution)/shard_map/m_far2/ppermute | solution.py:71
  670.7 34.3 %attend_back.1 = (bf16[4,256,1536]{2,1,0:T(8,128)(2,1)}, bf16[1536,1024]{1,0:T(8,128)(2,1)}, f32[1,1536]{1,0:T(1,128)}) custom-call(s32[16]{0:T(128)} %concatenate.65.info_ref, bf16[4,256,1536]{2,1,0:T(8,128)(2,1)} %pad_maximum_fusion.6.da_ref, bf16[4,256,1536]{2,1,0:T(8,128)(2,1)} %pad_maximum_fusion.n1_ref, bf16[1536,1024]{1,0:T(8,128)(2,1)} %get-tuple-element.193.w_ref, ...), custom_call_target="tpu_custom_call" | custom-call | flops 1000000 | bytes 10000 | tf_op jit(solution)/shard_map/attend_back/pallas_call | solution.py:658
  724.0 12.4 %collective-permute-done.58 = f32[48,1536]{1,0:T(8,128)S(1)} collective-permute-done((f32[48,1536]{1,0:T(8,128)S(1)}, f32[48,1536]{1,0:T(8,128)S(1)}, u32[]{:S(2)}, u32[]{:S(2)}) %collective-permute-start.58) | collective-permute-done | bytes 294944 | tf_op jit(solution)/shard_map/small/ppermute | solution.py:71
  746.4 11.7 %collective-permute-done.51 = bf16[256,1536]{1,0:T(8,128)(2,1)S(1)} collective-permute-done((bf16[256,1536]{1,0:T(8,128)(2,1)S(1)}, bf16[256,1536]{1,0:T(8,128)(2,1)S(1)}, u32[]{:S(2)}, u32[]{:S(2)}) %collective-permute-start.51) | collective-permute-done | bytes 786464 | tf_op jit(solution)/shard_map/m_home2/ppermute | solution.py:71
  772.9 14.9 %collective-permute-done.52 = bf16[256,1536]{1,0:T(8,128)(2,1)S(1)} collective-permute-done((bf16[256,1536]{1,0:T(8,128)(2,1)S(1)}, bf16[256,1536]{1,0:T(8,128)(2,1)S(1)}, u32[]{:S(2)}, u32[]{:S(2)}) %collective-permute-start.52) | collective-permute-done | bytes 786464 | tf_op jit(solution)/shard_map/m_home1/ppermute | solution.py:71
  787.8 9.3 %all-to-all-done.4.full_ref = bf16[8,192,1024]{2,1,0:T(8,128)(2,1)} async-done(((bf16[8,192,1024]{2,1,0:T(8,128)(2,1)}), bf16[8,192,1024]{2,1,0:T(8,128)(2,1)}, u32[]{:S(2)}, u32[]{:S(2)}) %all-to-all-start.4) | async-done | bytes 3145760 | tf_op jit(solution)/shard_map/all_to_all | solution.py:785
  809.5 11.7 %collective-permute-done.60 = f32[48,1536]{1,0:T(8,128)S(1)} collective-permute-done((f32[48,1536]{1,0:T(8,128)S(1)}, f32[48,1536]{1,0:T(8,128)S(1)}, u32[]{:S(2)}, u32[]{:S(2)}) %collective-permute-start.60) | collective-permute-done | bytes 294944 | tf_op jit(solution)/shard_map/small/ppermute | solution.py:71
  836.2 9.2 %unpack_experts.1 = (f32[10,192,1024]{2,1,0:T(8,128)}, f32[10,192,512]{2,1,0:T(8,128)}) custom-call(bf16[8,192,1024]{2,1,0:T(8,128)(2,1)} %all-to-all-done.4.full_ref, bf16[8,192,512]{2,1,0:T(8,128)(2,1)} %all-to-all-done.3.down_ref, bf16[8,192,384]{2,1,0:T(8,128)(2,1)} %all-to-all-done.2.part_ref), custom_call_target="tpu_custom_call" | custom-call | tf_op jit(solution)/shard_map/unpack_experts/pallas_call | solution.py:235
  (324 shorter events, 320.3 us)
Async XLA Ops:
  14.1 31.9 %collective-permute-start.1 = (bf16[208,1024]{1,0:T(8,128)(2,1)S(1)}, bf16[208,1024]{1,0:T(8,128)(2,1)S(1)}, u32[]{:S(2)}, u32[]{:S(2)}) collective-permute-start(bf16[208,1024]{1,0:T(8,128)(2,1)S(1)} %get-tuple-element.227), channel_id=1, source_target_pairs={{0,16},{1,17},{2,18},{3,19},{4,20},{5,21},{6,22},{7,23},{8,24},{9,... | collective-permute-start | bytes 1277960 | tf_op jit(solution)/shard_map/pieces/ppermute | solution.py:71
  16.7 29.3 %collective-permute-start.2 = (bf16[208,1024]{1,0:T(8,128)(2,1)S(1)}, bf16[208,1024]{1,0:T(8,128)(2,1)S(1)}, u32[]{:S(2)}, u32[]{:S(2)}) collective-permute-start(bf16[208,1024]{1,0:T(8,128)(2,1)S(1)} %get-tuple-element.227), channel_id=1, source_target_pairs={{0,24},{1,25},{2,26},{3,27},{4,28},{5,29},{6,30},{7,31},{8,16},{9,... | collective-permute-start | bytes 1277960 | tf_op jit(solution)/shard_map/pieces/ppermute | solution.py:71
  46.3 74.0 %all-to-all-start = ((bf16[8,192,896]{2,1,0:T(8,128)(2,1)}), bf16[8,192,896]{2,1,0:T(8,128)(2,1)}, u32[]{:S(2)}, u32[]{:S(2)}) async-start(bf16[8,192,896]{2,1,0:T(8,128)(2,1)} %pack_experts.1), calls=%async_computation | async-start | bytes 5505024 | tf_op jit(solution)/shard_map/all_to_all | solution.py:785
  96.6 35.1 %collective-permute-start.7 = (bf16[4,208,1024]{2,1,0:T(8,128)(2,1)S(1)}, bf16[4,208,1024]{2,1,0:T(8,128)(2,1)}, u32[]{:S(2)}, u32[]{:S(2)}) collective-permute-start(bf16[4,208,1024]{2,1,0:T(8,128)(2,1)S(1)} %pad_maximum_fusion.9.refs_0_), channel_id=1, source_target_pairs={{0,4},{1,5},{2,6},{3,7},{4,0},{5,1},{6,2},{7,3},{8,12},{9,13},{10,... | collective-permute-start | bytes 5111816 | tf_op jit(solution)/shard_map/pieces_theirs/ppermute | solution.py:71
  105.5 26.1 %collective-permute-start.6 = (bf16[2,256,1536]{2,1,0:T(8,128)(2,1)}, bf16[2,256,1536]{2,1,0:T(8,128)(2,1)}, u32[]{:S(2)}, u32[]{:S(2)}) collective-permute-start(bf16[2,256,1536]{2,1,0:T(8,128)(2,1)} %pad_maximum_fusion.11), channel_id=1, source_target_pairs={{0,2},{1,3},{2,0},{3,1},{4,5},{5,4},{6,7},{7,6},{8,10},{9,11},{10,... | collective-permute-start | bytes 4718600 | tf_op jit(solution)/shard_map/y_far0/ppermute | solution.py:71
  120.3 76.2 %all-to-all-start.1 = ((bf16[8,192,1024]{2,1,0:T(8,128)(2,1)}), bf16[8,192,1024]{2,1,0:T(8,128)(2,1)}, u32[]{:S(2)}, u32[]{:S(2)}) async-start(bf16[8,192,1024]{2,1,0:T(8,128)(2,1)} %slice.229), calls=%async_computation.1 | async-start | bytes 6291456 | tf_op jit(solution)/shard_map/all_to_all | solution.py:785
  179.4 57.7 %collective-permute-start.14 = (bf16[4,256,1536]{2,1,0:T(8,128)(2,1)}, bf16[4,256,1536]{2,1,0:T(8,128)(2,1)}, u32[]{:S(2)}, u32[]{:S(2)}) collective-permute-start(bf16[4,256,1536]{2,1,0:T(8,128)(2,1)} %pad_maximum_fusion.3.ya_ref), channel_id=1, source_target_pairs={{0,4},{1,5},{2,6},{3,7},{4,0},{5,1},{6,2},{7,3},{8,12},{9,13},{10,... | collective-permute-start | bytes 9437192 | tf_op jit(solution)/shard_map/y_theirs0/ppermute | solution.py:71
  196.7 36.9 %collective-permute-start.10 = (bf16[2,256,1536]{2,1,0:T(8,128)(2,1)S(1)}, bf16[2,256,1536]{2,1,0:T(8,128)(2,1)S(1)}, u32[]{:S(2)}, u32[]{:S(2)}) collective-permute-start(bf16[2,256,1536]{2,1,0:T(8,128)(2,1)S(1)} %pad_maximum_fusion.8), channel_id=1, source_target_pairs={{0,8},{1,9},{2,10},{3,11},{4,12},{5,13},{6,14},{7,15},{8,24},{9,25... | collective-permute-start | bytes 4718600 | tf_op jit(solution)/shard_map/both1/ppermute | solution.py:71
  209.0 26.1 %collective-permute-start.13 = (bf16[2,256,1536]{2,1,0:T(8,128)(2,1)S(1)}, bf16[2,256,1536]{2,1,0:T(8,128)(2,1)S(1)}, u32[]{:S(2)}, u32[]{:S(2)}) collective-permute-start(bf16[2,256,1536]{2,1,0:T(8,128)(2,1)S(1)} %pad_maximum_fusion.7), channel_id=1, source_target_pairs={{0,2},{1,3},{2,0},{3,1},{4,5},{5,4},{6,7},{7,6},{8,10},{9,11},{10,... | collective-permute-start | bytes 4718600 | tf_op jit(solution)/shard_map/far0/ppermute | solution.py:71
  254.3 37.4 %collective-permute-start.19 = (bf16[2,2,256,1536]{3,2,1,0:T(8,128)(2,1)S(1)}, bf16[2,2,256,1536]{3,2,1,0:T(8,128)(2,1)}, u32[]{:S(2)}, u32[]{:S(2)}) collective-permute-start(bf16[2,2,256,1536]{3,2,1,0:T(8,128)(2,1)S(1)} %pad_maximum_fusion.1), channel_id=1, source_target_pairs={{0,2},{1,3},{2,0},{3,1},{4,5},{5,4},{6,7},{7,6},{8,10},{9,11},{10,... | collective-permute-start | bytes 9437192 | tf_op jit(solution)/shard_map/far1/ppermute | solution.py:71
  259.0 38.3 %collective-permute-start.17 = (bf16[2,256,1536]{2,1,0:T(8,128)(2,1)}, bf16[2,256,1536]{2,1,0:T(8,128)(2,1)}, u32[]{:S(2)}, u32[]{:S(2)}) collective-permute-start(bf16[2,256,1536]{2,1,0:T(8,128)(2,1)} %copy-done.30), channel_id=1, source_target_pairs={{8,0},{9,1},{10,2},{11,3},{12,4},{13,5},{14,6},{15,7},{24,8},{25,9... | collective-permute-start | bytes 4718600 | tf_op jit(solution)/shard_map/both3/ppermute | solution.py:71
  319.7 37.4 %collective-permute-start.23 = (bf16[2,2,256,1536]{3,2,1,0:T(8,128)(2,1)S(1)}, bf16[2,2,256,1536]{3,2,1,0:T(8,128)(2,1)}, u32[]{:S(2)}, u32[]{:S(2)}) collective-permute-start(bf16[2,2,256,1536]{3,2,1,0:T(8,128)(2,1)S(1)} %pad_maximum_fusion.4), channel_id=1, source_target_pairs={{0,2},{1,3},{2,0},{3,1},{4,5},{5,4},{6,7},{7,6},{8,10},{9,11},{10,... | collective-permute-start | bytes 9437192 | tf_op jit(solution)/shard_map/far3/ppermute | solution.py:71
  321.9 40.8 %collective-permute-start.16 = (bf16[2,256,1536]{2,1,0:T(8,128)(2,1)}, bf16[2,256,1536]{2,1,0:T(8,128)(2,1)}, u32[]{:S(2)}, u32[]{:S(2)}) collective-permute-start(bf16[2,256,1536]{2,1,0:T(8,128)(2,1)} %copy-done.32), channel_id=1, source_target_pairs={{0,8},{1,9},{2,10},{3,11},{4,12},{5,13},{6,14},{7,15},{8,24},{9,25... | collective-permute-start | bytes 4718600 | tf_op jit(solution)/shard_map/both2/ppermute | solution.py:71
  321.9 43.2 %collective-permute-start.22 = (bf16[2,4,256,1664]{3,2,1,0:T(8,128)(2,1)}, bf16[2,4,256,1664]{3,2,1,0:T(8,128)(2,1)}, u32[]{:S(2)}, u32[]{:S(2)}) collective-permute-start(bf16[2,4,256,1664]{3,2,1,0:T(8,128)(2,1)} %get-tuple-element.140), channel_id=1, source_target_pairs={{0,4},{1,5},{2,6},{3,7},{4,0},{5,1},{6,2},{7,3},{8,12},{9,13},{10,... | collective-permute-start | bytes 20447240 | tf_op jit(solution)/shard_map/swap0/ppermute | solution.py:71
  362.7 28.5 %collective-permute-start.24 = (bf16[4,2,256,1536]{3,2,1,0:T(8,128)(2,1)}, bf16[4,2,256,1536]{3,2,1,0:T(8,128)(2,1)}, u32[]{:S(2)}, u32[]{:S(2)}) collective-permute-start(bf16[4,2,256,1536]{3,2,1,0:T(8,128)(2,1)} %constant_dynamic-update-slice_fusion.2.xa_ref.ya_ref), channel_id=1, source_target_pairs={{0,4},{1,5},{2,6},{3,7},{4,0},{5,1},{6,2},{7,3},{8,12},{9,13},{10,... | collective-permute-start | bytes 18874376 | tf_op jit(solution)/shard_map/theirs3/ppermute | solution.py:71
  364.9 68.3 %collective-permute-start.26 = (bf16[2,4,256,1664]{3,2,1,0:T(8,128)(2,1)}, bf16[2,4,256,1664]{3,2,1,0:T(8,128)(2,1)}, u32[]{:S(2)}, u32[]{:S(2)}) collective-permute-start(bf16[2,4,256,1664]{3,2,1,0:T(8,128)(2,1)} %get-tuple-element.154), channel_id=1, source_target_pairs={{0,4},{1,5},{2,6},{3,7},{4,0},{5,1},{6,2},{7,3},{8,12},{9,13},{10,... | collective-permute-start | bytes 20447240 | tf_op jit(solution)/shard_map/swap1/ppermute | solution.py:71
  386.9 37.6 %collective-permute-start.25 = (bf16[2,2,256,1536]{3,2,1,0:T(8,128)(2,1)}, bf16[2,2,256,1536]{3,2,1,0:T(8,128)(2,1)}, u32[]{:S(2)}, u32[]{:S(2)}) collective-permute-start(bf16[2,2,256,1536]{3,2,1,0:T(8,128)(2,1)} %pad_maximum_fusion.5), channel_id=1, source_target_pairs={{0,2},{1,3},{2,0},{3,1},{4,5},{5,4},{6,7},{7,6},{8,10},{9,11},{10,... | collective-permute-start | bytes 9437192 | tf_op jit(solution)/shard_map/far2/ppermute | solution.py:71
  438.4 42.6 %collective-permute-start.29 = (bf16[2,256,1664]{2,1,0:T(8,128)(2,1)}, bf16[2,256,1664]{2,1,0:T(8,128)(2,1)}, u32[]{:S(2)}, u32[]{:S(2)}) collective-permute-start(bf16[2,256,1664]{2,1,0:T(8,128)(2,1)} %slice.309), channel_id=1, source_target_pairs={{0,2},{1,3},{2,0},{3,1},{4,5},{5,4},{6,7},{7,6},{8,10},{9,11},{10,... | collective-permute-start | bytes 5111816 | tf_op jit(solution)/shard_map/d_far1/ppermute | solution.py:71
  449.3 31.7 %collective-permute-start.30 = (bf16[2,256,1664]{2,1,0:T(8,128)(2,1)}, bf16[2,256,1664]{2,1,0:T(8,128)(2,1)}, u32[]{:S(2)}, u32[]{:S(2)}) collective-permute-start(bf16[2,256,1664]{2,1,0:T(8,128)(2,1)} %slice.312), channel_id=1, source_target_pairs={{0,2},{1,3},{2,0},{3,1},{4,5},{5,4},{6,7},{7,6},{8,10},{9,11},{10,... | collective-permute-start | bytes 5111816 | tf_op jit(solution)/shard_map/d_far3/ppermute | solution.py:71
  531.6 51.9 %all-to-all-start.2 = ((bf16[8,192,384]{2,1,0:T(8,128)(2,1)}), bf16[8,192,384]{2,1,0:T(8,128)(2,1)}, u32[]{:S(2)}, u32[]{:S(2)}) async-start(bf16[8,192,384]{2,1,0:T(8,128)(2,1)} %bitcast.216), calls=%async_computation.2 | async-start | bytes 2359296 | tf_op jit(solution)/shard_map/all_to_all | solution.py:785
  548.7 34.8 %collective-permute-start.36 = (bf16[2,256,1664]{2,1,0:T(8,128)(2,1)}, bf16[2,256,1664]{2,1,0:T(8,128)(2,1)}, u32[]{:S(2)}, u32[]{:S(2)}) collective-permute-start(bf16[2,256,1664]{2,1,0:T(8,128)(2,1)} %slice.306), channel_id=1, source_target_pairs={{0,2},{1,3},{2,0},{3,1},{4,5},{5,4},{6,7},{7,6},{8,10},{9,11},{10,... | collective-permute-start | bytes 5111816 | tf_op jit(solution)/shard_map/d_far0/ppermute | solution.py:71
  615.0 51.1 %all-to-all-start.3 = ((bf16[8,192,512]{2,1,0:T(8,128)(2,1)}), bf16[8,192,512]{2,1,0:T(8,128)(2,1)}, u32[]{:S(2)}, u32[]{:S(2)}) async-start(bf16[8,192,512]{2,1,0:T(8,128)(2,1)} %bitcast.87), calls=%async_computation.3 | async-start | bytes 3145728 | tf_op jit(solution)/shard_map/all_to_all | solution.py:785
  629.3 33.9 %collective-permute-start.49 = (bf16[2,256,1536]{2,1,0:T(8,128)(2,1)S(1)}, bf16[2,256,1536]{2,1,0:T(8,128)(2,1)S(1)}, u32[]{:S(2)}, u32[]{:S(2)}) collective-permute-start(bf16[2,256,1536]{2,1,0:T(8,128)(2,1)S(1)} %slice.341), channel_id=1, source_target_pairs={{0,2},{1,3},{2,0},{3,1},{4,5},{5,4},{6,7},{7,6},{8,10},{9,11},{10,... | collective-permute-start | bytes 4718600 | tf_op jit(solution)/shard_map/m_far2/ppermute | solution.py:71
  636.3 73.2 %collective-permute-start.44 = (bf16[2,256,1536]{2,1,0:T(8,128)(2,1)}, bf16[2,256,1536]{2,1,0:T(8,128)(2,1)}, u32[]{:S(2)}, u32[]{:S(2)}) collective-permute-start(bf16[2,256,1536]{2,1,0:T(8,128)(2,1)} %slice.327), channel_id=1, source_target_pairs={{0,2},{1,3},{2,0},{3,1},{4,5},{5,4},{6,7},{7,6},{8,10},{9,11},{10,... | collective-permute-start | bytes 4718600 | tf_op jit(solution)/shard_map/m_far1/ppermute | solution.py:71
  648.3 61.2 %collective-permute-start.43 = (bf16[2,256,1536]{2,1,0:T(8,128)(2,1)}, bf16[2,256,1536]{2,1,0:T(8,128)(2,1)}, u32[]{:S(2)}, u32[]{:S(2)}) collective-permute-start(bf16[2,256,1536]{2,1,0:T(8,128)(2,1)} %slice.325), channel_id=1, source_target_pairs={{0,2},{1,3},{2,0},{3,1},{4,5},{5,4},{6,7},{7,6},{8,10},{9,11},{10,... | collective-permute-start | bytes 4718600 | tf_op jit(solution)/shard_map/m_far3/ppermute | solution.py:71
  664.7 47.0 %collective-permute-start.50 = (bf16[256,1536]{1,0:T(8,128)(2,1)}, bf16[256,1536]{1,0:T(8,128)(2,1)}, u32[]{:S(2)}, u32[]{:S(2)}) collective-permute-start(bf16[256,1536]{1,0:T(8,128)(2,1)} %fusion.39), channel_id=1, source_target_pairs={{0,1},{1,0},{2,3},{3,2},{4,6},{5,7},{6,4},{7,5},{8,9},{9,8},{10,11... | collective-permute-start | bytes 2359304 | tf_op jit(solution)/shard_map/m_near2/ppermute | solution.py:71
  666.1 131.0 %all-to-all-start.4 = ((bf16[8,192,1024]{2,1,0:T(8,128)(2,1)}), bf16[8,192,1024]{2,1,0:T(8,128)(2,1)}, u32[]{:S(2)}, u32[]{:S(2)}) async-start(bf16[8,192,1024]{2,1,0:T(8,128)(2,1)} %bitcast.210), calls=%async_computation.5 | async-start | bytes 6291456 | tf_op jit(solution)/shard_map/all_to_all | solution.py:785
  670.6 153.2 %reduce-scatter.2.cloned.1.call-start = ((), (), s32[]{:S(2)}) async-start(), calls=%async_computation.6 | async-start | bytes 3538944 | tf_op jit(solution)/shard_map/reduce_scatter | solution.py:949
  709.5 27.0 %collective-permute-start.45 = (bf16[2,256,1536]{2,1,0:T(8,128)(2,1)}, bf16[2,256,1536]{2,1,0:T(8,128)(2,1)}, u32[]{:S(2)}, u32[]{:S(2)}) collective-permute-start(bf16[2,256,1536]{2,1,0:T(8,128)(2,1)} %slice.261), channel_id=1, source_target_pairs={{0,2},{1,3},{2,0},{3,1},{4,5},{5,4},{6,7},{7,6},{8,10},{9,11},{10,... | collective-permute-start | bytes 4718600 | tf_op jit(solution)/shard_map/parts_far/ppermute | solution.py:71
  713.6 44.5 %collective-permute-start.51 = (bf16[256,1536]{1,0:T(8,128)(2,1)S(1)}, bf16[256,1536]{1,0:T(8,128)(2,1)S(1)}, u32[]{:S(2)}, u32[]{:S(2)}) collective-permute-start(bf16[256,1536]{1,0:T(8,128)(2,1)S(1)} %fusion.24), channel_id=1, source_target_pairs={{8,0},{9,1},{10,2},{11,3},{12,4},{13,5},{14,6},{15,7},{24,8},{25,9... | collective-permute-start | bytes 2359304 | tf_op jit(solution)/shard_map/m_home2/ppermute | solution.py:71
  741.2 65.9 %collective-permute-start.46 = (bf16[2,256,1536]{2,1,0:T(8,128)(2,1)}, bf16[2,256,1536]{2,1,0:T(8,128)(2,1)}, u32[]{:S(2)}, u32[]{:S(2)}) collective-permute-start(bf16[2,256,1536]{2,1,0:T(8,128)(2,1)} %slice.331), channel_id=1, source_target_pairs={{0,2},{1,3},{2,0},{3,1},{4,5},{5,4},{6,7},{7,6},{8,10},{9,11},{10,... | collective-permute-start | bytes 4718600 | tf_op jit(solution)/shard_map/m_far0/ppermute | solution.py:71
  759.6 28.2 %collective-permute-start.52 = (bf16[256,1536]{1,0:T(8,128)(2,1)S(1)}, bf16[256,1536]{1,0:T(8,128)(2,1)S(1)}, u32[]{:S(2)}, u32[]{:S(2)}) collective-permute-start(bf16[256,1536]{1,0:T(8,128)(2,1)S(1)} %fusion.26), channel_id=1, source_target_pairs={{8,0},{9,1},{10,2},{11,3},{12,4},{13,5},{14,6},{15,7},{24,8},{25,9... | collective-permute-start | bytes 2359304 | tf_op jit(solution)/shard_map/m_home1/ppermute | solution.py:71
  (84 other events, 1202.8 us)
Sparse Core Ops, SparseCore 0:
  710.2 98.3 reduce-scatter.1
